TPU v7x, 32 devices: a whole 2x2x4 slice. The times are simulated.
32 devices in a mesh: grp: 2 (over y), row: 4 (over z), col: 2 (over x), lay: 2 (over core).
Axes of the slice: x: 2, y: 2, z: 4, core: 2. Of those that a mesh axis runs over, the one named last changes fastest.
Arguments:
- earlier_heat_level: float32 [16, 96, 1536], P('grp', 'row', ('col', 'lay')), parts along dimension 0, may hold values from 0 to 2
- substance_per_heat_node: int32 [16, 96, 1536], P('grp', 'row', ('col', 'lay')), parts along dimension 0, may hold values from 0 to 15
- die_heating_source: float32 [192, 1536], P(('grp', 'row'), ('col', 'lay')), parts along dimension 0, may hold values from 0.2 to 5
- substance_per_solid_element: int32 [12, 32, 512], P('grp', ('row', 'lay'), 'col'), parts along dimension 0, may hold values from 0 to 15
- earlier_solid_offset: float32 [3, 12, 32, 512], P(None, 'grp', ('row', 'lay'), 'col'), parts along dimension 1, may hold values from -2.5 to 2.5
- heat_transfer_per_substance: float32 [16], replicated, may hold values from 0.5 to 8
- growth_rate_per_substance: float32 [16], replicated, may hold values from 0.2 to 2
- elastic_modulus_per_substance: float32 [16], replicated, may hold values from 0.5 to 5
Outputs:
- temperature: float32 [16, 96, 1536], P('grp', 'row', ('col', 'lay')), parts along dimension 0
- displacement: float32 [3, 12, 32, 512], P(None, 'grp', ('row', 'lay'), 'col'), parts along dimension 1
- slowdown_factor: float32 [192, 1536], P(('grp', 'row'), ('col', 'lay')), parts along dimension 0
There are 2 independent parts, one for each index of `grp`. A program takes and returns all parts, laid end to end along the dimension named above; an argument that names none is the same for every part. Nothing has to cross between parts.
All inputs are finite; a program needn't handle non-finite values.
Results may differ from a plain program's by a relative error of at most 0.00002.
Values sent between devices are 32-bit elements; how exact they have to be, the bound alone decides.
No kernel may reach another device: no remote copies, remote signals or barrier semaphores. Data moves between devices by JAX's collectives and lax.ppermute only.
A program may use at most 64 MiB of HBM per device.

v0:
```python
import jax
import jax.numpy as jnp
import numpy as np
from jax import lax
from jax.sharding import PartitionSpec as P

HEAT_GRID_DEPTH = 8
ML = 6
THERMAL_SWEEPS = 2
MECH_SWEEPS = 2


STIFF_DIAG = 12.0
LOWER_BOUND = 0.25
UPPER_BOUND = 1.75


def padded_2(cells, sides, width):
    for axis, dim in sides:
        count = lax.axis_size(axis)
        ends = count - 1
        head = lax.slice_in_dim(cells, 0, width, axis=dim)
        tail = lax.slice_in_dim(cells, cells.shape[dim] - width, cells.shape[dim], axis=dim)
        cells = jnp.concatenate(
            [
                lax.ppermute(tail, axis, [(i, (i + 1) % count) for i in range(ends)]),
                cells,
                lax.ppermute(head, axis, [((i + 1) % count, i) for i in range(ends)]),
            ],
            axis=dim,
        )
    return cells


def lookup(material, table):
    result = jnp.zeros(material.shape, jnp.float32)
    for m in range(table.shape[0]):
        result = jnp.where(material == m, table[m], result)
    return result


def smoothing_update(widened_heat_level, widened_heat_transfer, forcing_term, cooling_boundary):
    rows = widened_heat_level.shape[1] - 2
    cols = widened_heat_level.shape[2] - 2
    k_mid = widened_heat_transfer[:, 1 : 1 + rows, 1 : 1 + cols]
    numerator = forcing_term
    denominator = cooling_boundary + jnp.zeros_like(k_mid)
    for row_off, col_off in ((2, 1), (0, 1), (1, 2), (1, 0)):
        conduct = jnp.sqrt(
            k_mid * widened_heat_transfer[:, row_off : row_off + rows, col_off : col_off + cols]
        )
        numerator = (
            numerator
            + conduct * widened_heat_level[:, row_off : row_off + rows, col_off : col_off + cols]
        )
        denominator = denominator + conduct
    t_mid = widened_heat_level[:, 1 : 1 + rows, 1 : 1 + cols]
    k_pad = jnp.pad(k_mid, ((1, 1), (0, 0), (0, 0)))
    t_pad = jnp.pad(t_mid, ((1, 1), (0, 0), (0, 0)))
    depth = k_mid.shape[0]
    for layer_off in (2, 0):
        conduct = jnp.sqrt(k_mid * k_pad[layer_off : layer_off + depth])
        numerator = numerator + conduct * t_pad[layer_off : layer_off + depth]
        denominator = denominator + conduct
    return numerator / denominator


def trimmed(padded, margin):
    return padded[:, margin : padded.shape[1] - margin, margin : padded.shape[2] - margin]


def shifted(padded, axis_id, offset):
    selector = [slice(None)] * (padded.ndim - 3)
    for grid_dim in range(3):
        extent = padded.shape[padded.ndim - 3 + grid_dim] - 2
        start_at = 1 + offset if grid_dim == axis_id else 1
        selector.append(slice(start_at, start_at + extent))
    return padded[tuple(selector)]


def block_coef(d, i, j):
    if i == j:
        return 1.0 if i == d else 0.5
    if (i == d) != (j == d):
        return 0.25
    return 0.0


def load_force(s_pad):
    return jnp.stack([0.5 * (shifted(s_pad, d, 1) - shifted(s_pad, d, -1)) for d in range(3)])


def apply_stiff(v_pad, e_pad):
    e_mid = shifted(e_pad, 0, 0)
    outputs = [STIFF_DIAG * e_mid * shifted(v_pad[i], 0, 0) for i in range(3)]
    for d in range(3):
        for offset in (1, -1):
            couple = jnp.sqrt(e_mid * shifted(e_pad, d, offset))
            near = [shifted(v_pad[j], d, offset) for j in range(3)]
            for i in range(3):
                mixed = jnp.zeros_like(e_mid)
                for j in range(3):
                    weight = block_coef(d, i, j)
                    if weight != 0.0:
                        mixed = mixed + weight * near[j]
                outputs[i] = outputs[i] - couple * mixed
    return jnp.stack(outputs)


def divergence(u_pad):
    total = jnp.zeros_like(shifted(u_pad[0], 0, 0))
    for d in range(3):
        total = total + (shifted(u_pad[d], d, 1) - shifted(u_pad[d], d, -1))
    return 0.5 * total


def chebyshev(start, resid, diagonal, apply_fn, sweeps):
    theta = 0.5 * (UPPER_BOUND + LOWER_BOUND)
    delta = 0.5 * (UPPER_BOUND - LOWER_BOUND)
    sigma = theta / delta
    rho_now = 1.0 / sigma
    direction = resid / diagonal / theta
    shifted_copy = start
    for sweep in range(sweeps):
        shifted_copy = shifted_copy + direction
        if sweep < sweeps - 1:
            resid = resid - apply_fn(direction)
            rho_next = 1.0 / (2.0 * sigma - rho_now)
            direction = rho_next * rho_now * direction + 2.0 * rho_next / delta * (resid / diagonal)
            rho_now = rho_next
    return shifted_copy


def spread_mech(field):
    widened_field = padded_2(field, ((("row", "lay"), 2), ("col", 3)), 1)
    return jnp.pad(widened_field, ((0, 0), (1, 1), (0, 0), (0, 0)))


def per_device(
    earlier_heat_level,
    substance_per_heat_node,
    die_heating_source,
    substance_per_solid_element,
    earlier_solid_offset,
    heat_transfer_per_substance,
    growth_rate_per_substance,
    elastic_modulus_per_substance,
):
    lay_count = lax.axis_size("lay")
    layer = jnp.arange(HEAT_GRID_DEPTH).reshape(HEAT_GRID_DEPTH, 1, 1)
    cooling_boundary = jnp.where(layer == HEAT_GRID_DEPTH - 1, 2.0, 0.2).astype(jnp.float32)
    local_heat_transfer = lookup(substance_per_heat_node, heat_transfer_per_substance)
    linear_growth_rate = lookup(substance_per_heat_node, growth_rate_per_substance)
    width = THERMAL_SWEEPS
    bundle = jnp.concatenate(
        [earlier_heat_level, local_heat_transfer, die_heating_source[None]], axis=0
    )
    widened_field = padded_2(bundle, (("row", 1), (("col", "lay"), 2)), width)
    present_heat_level = widened_field[:HEAT_GRID_DEPTH]
    k_full = widened_field[HEAT_GRID_DEPTH : 2 * HEAT_GRID_DEPTH]
    power_full = widened_field[2 * HEAT_GRID_DEPTH :]
    for sweep in range(THERMAL_SWEEPS):
        k_now = trimmed(k_full, sweep)
        source_now = jnp.where(layer == 0, trimmed(power_full, sweep + 1), 0.0)
        present_heat_level = smoothing_update(
            present_heat_level, k_now, source_now, cooling_boundary
        )
    block_height = present_heat_level.shape[1]
    block_width = present_heat_level.shape[2]
    coarse_rows = block_height // 3
    coarse_cols = block_width // 3
    half_rows = coarse_rows // lay_count
    heating_strain = (linear_growth_rate * present_heat_level).reshape(
        HEAT_GRID_DEPTH, coarse_rows, 3, coarse_cols, 3
    ).sum(axis=(2, 4)) / 9.0
    layer_map = np.arange(ML) * HEAT_GRID_DEPTH // ML
    outgoing = heating_strain[layer_map].reshape(ML, lay_count, half_rows, coarse_cols)
    arrived = lax.all_to_all(outgoing, "lay", split_axis=1, concat_axis=3, tiled=True)
    arrived = arrived.reshape(arrived.shape[0], half_rows, lay_count * coarse_cols)
    modulus = lookup(substance_per_solid_element, elastic_modulus_per_substance)
    coeffs = padded_2(jnp.stack([modulus, modulus * arrived]), ((("row", "lay"), 2), ("col", 3)), 1)
    coeffs = jnp.pad(coeffs, ((0, 0), (1, 1), (0, 0), (0, 0)))
    e_pad = coeffs[0]
    force = load_force(coeffs[1])
    diagonal = STIFF_DIAG * modulus

    def apply_fn(field):
        return apply_stiff(spread_mech(field), e_pad)

    resid = force - apply_fn(earlier_solid_offset)
    shifted_copy = chebyshev(earlier_solid_offset, resid, diagonal, apply_fn, MECH_SWEEPS)
    stress = modulus * (divergence(spread_mech(shifted_copy)) - 3.0 * arrived)
    weights = ((ML - jnp.arange(ML)).astype(jnp.float32) / (ML * (ML + 1) / 2.0)).reshape(ML, 1, 1)
    block_die = jnp.sum(weights * stress, axis=0)
    pieces = lax.all_to_all(
        block_die.reshape(half_rows, lay_count, coarse_cols),
        "lay",
        split_axis=1,
        concat_axis=0,
        tiled=True,
    )
    die_stress = pieces.reshape(coarse_rows, coarse_cols)
    diffusion_update = jnp.repeat(jnp.repeat(die_stress, 3, axis=0), 3, axis=1)
    slowdown_factor = 1.0 + 0.2 * present_heat_level[0] + 0.5 * diffusion_update
    return (present_heat_level, shifted_copy, slowdown_factor)


def solution(mesh):
    placed = (
        P("grp", "row", ("col", "lay")),
        P("grp", "row", ("col", "lay")),
        P(("grp", "row"), ("col", "lay")),
        P("grp", ("row", "lay"), "col"),
        P(None, "grp", ("row", "lay"), "col"),
        P(),
        P(),
        P(),
    )
    return jax.shard_map(
        per_device,
        mesh=mesh,
        in_specs=placed,
        out_specs=(
            P("grp", "row", ("col", "lay")),
            P(None, "grp", ("row", "lay"), "col"),
            P(("grp", "row"), ("col", "lay")),
        ),
        check_vma=False,
    )
```

profile of v0, /device:TPU:11, one launch (start us, length us, event | category | flops | bytes accessed | tf_op | source)
XLA Modules:
  0.0 141.7 jit_solution(13314261191191365088)
XLA Ops:
  0.7 1.9 %fusion.120 = (f32[1]{0:T(128)}, f32[1]{0:T(128)}, f32[1]{0:T(128)}, f32[1]{0:T(128)}, f32[1]{0:T(128)}, /*index=5*/f32[1]{0:T(128)}, f32[1]{0:T(128)}, f32[1]{0...) fusion(f32[16]{0:T(128)} %param.15), kind=kLoop, calls=%fused_computation.255 | loop fusion | bytes 128 | tf_op jit(solution)/shard_map/slice | solution.py:38
  2.7 11.8 %select_select_fusion = (f32[8,24,384]{2,1,0:T(8,128)S(1)}, pred[8,24,384]{2,1,0:T(8,128)(4,1)S(1)}, pred[8,24,384]{2,1,0:T(8,128)(4,1)S(1)}, pred[8,24,384]{2,1...) fusion(f32[]{:T(128)} %bitcast.15, f32[]{:T(128)} %bitcast.14, ...), kind=kLoop, calls=%fused_computation.85 | loop fusion | flops 2359296 | bytes 1769536 | tf_op jit(solution)/shard_map/jit(_where)/select_n | solution.py:38
  14.6 2.1 %collective-permute-start = (f32[17,2,384]{2,1,0:T(2,128)S(1)}, f32[17,2,384]{2,1,0:T(2,128)S(1)}, u32[]{:S(2)}, u32[]{:S(2)}) collective-permute-start(f32[17,2,384]{2,1,0:T(2,128)S(1)} %get-tuple-element.47), channel_id=1, source_target_pairs={{4,0},{8,4},{12,8},{5,1},{9,5},{13,9},{6,2},{10,6},{14,10},{7,3},{... | collective-permute-start | bytes 156680 | tf_op jit(solution)/shard_map/ppermute | solution.py:28
  16.6 3.2 %collective-permute-start.1 = (f32[17,2,384]{2,1,0:T(2,128)S(1)}, f32[17,2,384]{2,1,0:T(2,128)S(1)}, u32[]{:S(2)}, u32[]{:S(2)}) collective-permute-start(f32[17,2,384]{2,1,0:T(2,128)S(1)} %get-tuple-element.46), channel_id=1, source_target_pairs={{0,4},{4,8},{8,12},{1,5},{5,9},{9,13},{2,6},{6,10},{10,14},{3,7},{... | collective-permute-start | bytes 156680 | tf_op jit(solution)/shard_map/ppermute | solution.py:26
  19.9 3.1 %collective-permute-start.9 = (f32[3,6,1,256]{3,2,1,0:T(1,128)S(1)}, f32[3,6,1,256]{3,2,1,0:T(1,128)S(1)}, u32[]{:S(2)}, u32[]{:S(2)}) collective-permute-start(f32[3,6,1,256]{3,2,1,0:T(1,128)S(1)} %get-tuple-element.75), channel_id=1, source_target_pairs={{1,0},{4,1},{5,4},{8,5},{9,8},{12,9},{13,12},{3,2},{6,3},{7,6},{10... | collective-permute-start | bytes 55304 | tf_op jit(solution)/shard_map/ppermute | solution.py:28
  23.1 3.1 %collective-permute-start.8 = (f32[3,6,1,256]{3,2,1,0:T(1,128)S(1)}, f32[3,6,1,256]{3,2,1,0:T(1,128)S(1)}, u32[]{:S(2)}, u32[]{:S(2)}) collective-permute-start(f32[3,6,1,256]{3,2,1,0:T(1,128)S(1)} %get-tuple-element.74), channel_id=1, source_target_pairs={{0,1},{1,4},{4,5},{5,8},{8,9},{9,12},{12,13},{2,3},{3,6},{6,7},{7,... | collective-permute-start | bytes 55304 | tf_op jit(solution)/shard_map/ppermute | solution.py:26
  27.8 2.2 %collective-permute-start.11 = (f32[3,6,6,1]{3,2,1,0:T(8,128)S(1)}, f32[3,6,6,1]{3,2,1,0:T(8,128)S(1)}, u32[]{:S(2)}, u32[]{:S(2)}) collective-permute-start(f32[3,6,6,1]{3,2,1,0:T(8,128)S(1)} %get-tuple-element.64), channel_id=1, source_target_pairs={{2,0},{3,1},{6,4},{7,5},{10,8},{11,9},{14,12},{15,13},{18,16},{19,... | collective-permute-start | bytes 1304 | tf_op jit(solution)/shard_map/ppermute | solution.py:28
  30.0 1.3 collective-permute-start.10
  31.5 2.7 %collective-permute-start.3 = (f32[17,28,2]{2,1,0:T(8,128)S(1)}, f32[17,28,2]{2,1,0:T(8,128)S(1)}, u32[]{:S(2)}, u32[]{:S(2)}) collective-permute-start(f32[17,28,2]{2,1,0:T(8,128)S(1)} %get-tuple-element.45), channel_id=1, source_target_pairs={{1,0},{2,1},{3,2},{5,4},{6,5},{7,6},{9,8},{10,9},{11,10},{13,12},{... | collective-permute-start | bytes 11432 | tf_op jit(solution)/shard_map/ppermute | solution.py:28
  34.2 1.3 collective-permute-start.2
  35.8 3.1 %collective-permute-done.2 = f32[17,28,2]{2,1,0:T(8,128)S(1)} collective-permute-done((f32[17,28,2]{2,1,0:T(8,128)S(1)}, f32[17,28,2]{2,1,0:T(8,128)S(1)}, u32[]{:S(2)}, u32[]{:S(2)}) %collective-permute-start.2) | collective-permute-done | bytes 3840 | tf_op jit(solution)/shard_map/ppermute | solution.py:26
  40.6 1.5 %fusion.7 = f32[8,26,386]{2,1,0:T(8,128)S(1)} fusion(f32[8,26,386]{2,1,0:T(8,128)S(1)} %get-tuple-element.41, f32[17,28,386]{2,1,0:T(8,128)S(1)} %get-tuple-element.43, f32[17,28,386]{2,1,0:T(8,128)S(1)} %get-tuple-element.42, f32[17,28,388]{2,1,0:T(8,128)S(1)} %pad_maximum_fusion, f32[8,26,386]{2,1,0:T(8,128)S(1)} %get-tuple-element.40, ...), kind=kLoop, calls=%fused_computation.15 | loop fusion | flops 2087488 | bytes 3572856 | tf_op jit(solution)/shard_map/div | solution.py:65
  42.3 11.6 %select_multiply_fusion = (f32[8,24,384]{2,1,0:T(8,128)S(1)}, f32[8,24,384]{2,1,0:T(8,128)S(1)}) fusion(pred[8,24,384]{2,1,0:T(8,128)(4,1)S(1)} %get-tuple-element.39, pred[8,24,384]{2,1,0:T(8,128)(4,1)S(1)} %get-tuple-element.38, pred[8,24,384]{2,1,0:T(8,128)(4,1)S(1)} %get-tuple-element.37, pred[8,24,384]{2,1,0:T(8,128)(4,1)S(1)} %get-tuple-element.36, ...), kind=kLoop, calls=%fused_computation.84 | loop fusion | flops 4349952 | bytes 4019752 | tf_op jit(solution)/shard_map/mul | solution.py:173
  54.0 3.3 %copy.115 = f32[8,24,384]{0,2,1:T(8,128)} copy(f32[8,24,384]{2,1,0:T(8,128)S(1)} %get-tuple-element.21) | data formatting | bytes 589824 | tf_op jit(solution)/shard_map/mul | solution.py:173
  57.3 8.1 %reshape.55 = f32[8,8,3,128,3]{0,4,3,2,1:T(4,128)} reshape(f32[8,24,384]{0,2,1:T(8,128)} %copy.115) | data formatting | bytes 589824 | tf_op jit(solution)/shard_map/reshape | solution.py:173
  65.4 5.1 %reduce_sum.18 = f32[8,8,128]{0,2,1:T(8,128)S(1)} reduce(f32[8,8,3,128,3]{0,4,3,2,1:T(4,128)} %reshape.55, f32[]{:T(128)} %constant.31.clone.1), dimensions={2,4}, to_apply=%region_0.1 | reduce | flops 65536 | bytes 327684 | tf_op jit(solution)/shard_map/reduce_sum | solution.py:175
  71.3 8.3 %all_to_all.27 = f32[6,2,4,128]{3,2,0,1:T(4,128)S(1)} all-to-all(f32[6,2,4,128]{3,2,0,1:T(4,128)S(1)} %copy.117), channel_id=1, replica_groups=mesh['grp'=2,'row'=4,'col'=2,'lay'=2] {'lay'}, dimensions={1} | all-to-all | bytes 49152 | tf_op jit(solution)/shard_map/all_to_all | solution.py:178
  79.6 9.9 %multiply_bitcast_fusion = (f32[1,6,4,256]{3,2,1,0:T(4,128)S(1)}, f32[6,4,256]{2,1,0:T(4,128)S(1)}) fusion(f32[6,4,256]{2,1,0:T(4,128)S(1)} %reshape.57, f32[]{:T(128)} %bitcast.33, s32[6,4,256]{2,1,0:T(4,128)S(1)} %copy-done.7, f32[]{:T(128)} %bitcast.32, f32[]{:T(128)} %bitcast.31, f32[]{:T(128)} %bitcast.30, f32[]{:T(128)} %bitcast.29, f32[]{:T(128)} %bitcast.28, ...), kind=kLoop, calls=%fused_computation.220 | loop fusion | flops 202752 | bytes 98368 | tf_op jit(solution)/shard_map/stack | solution.py:181
  89.6 2.3 %collective-permute-start.5 = (f32[2,6,1,256]{3,2,1,0:T(1,128)S(1)}, f32[2,6,1,256]{3,2,1,0:T(1,128)S(1)}, u32[]{:S(2)}, u32[]{:S(2)}) collective-permute-start(f32[2,6,1,256]{3,2,1,0:T(1,128)S(1)} %get-tuple-element.77), channel_id=1, source_target_pairs={{1,0},{4,1},{5,4},{8,5},{9,8},{12,9},{13,12},{3,2},{6,3},{7,6},{10... | collective-permute-start | bytes 36872 | tf_op jit(solution)/shard_map/ppermute | solution.py:28
  91.9 3.3 %collective-permute-start.4 = (f32[2,6,1,256]{3,2,1,0:T(1,128)S(1)}, f32[2,6,1,256]{3,2,1,0:T(1,128)S(1)}, u32[]{:S(2)}, u32[]{:S(2)}) collective-permute-start(f32[2,6,1,256]{3,2,1,0:T(1,128)S(1)} %get-tuple-element.76), channel_id=1, source_target_pairs={{0,1},{1,4},{4,5},{5,8},{8,9},{9,12},{12,13},{2,3},{3,6},{6,7},{7,... | collective-permute-start | bytes 36872 | tf_op jit(solution)/shard_map/ppermute | solution.py:26
  97.4 1.5 %collective-permute-start.6 = (f32[2,6,6,1]{3,2,1,0:T(8,128)S(1)}, f32[2,6,6,1]{3,2,1,0:T(8,128)S(1)}, u32[]{:S(2)}, u32[]{:S(2)}) collective-permute-start(f32[2,6,6,1]{3,2,1,0:T(8,128)S(1)} %get-tuple-element.68), channel_id=1, source_target_pairs={{0,2},{1,3},{4,6},{5,7},{8,10},{9,11},{12,14},{13,15},{16,18},{17,... | collective-permute-start | bytes 872 | tf_op jit(solution)/shard_map/ppermute | solution.py:26
  98.9 3.3 %collective-permute-done.6 = f32[2,6,6,1]{3,2,1,0:T(8,128)S(1)} collective-permute-done((f32[2,6,6,1]{3,2,1,0:T(8,128)S(1)}, f32[2,6,6,1]{3,2,1,0:T(8,128)S(1)}, u32[]{:S(2)}, u32[]{:S(2)}) %collective-permute-start.6) | collective-permute-done | bytes 320 | tf_op jit(solution)/shard_map/ppermute | solution.py:26
  103.5 4.2 %collective-permute-start.13 = (f32[3,6,1,256]{3,2,1,0:T(1,128)S(1)}, f32[3,6,1,256]{3,2,1,0:T(1,128)S(1)}, u32[]{:S(2)}, u32[]{:S(2)}) collective-permute-start(f32[3,6,1,256]{3,2,1,0:T(1,128)S(1)} %get-tuple-element.73), channel_id=1, source_target_pairs={{1,0},{4,1},{5,4},{8,5},{9,8},{12,9},{13,12},{3,2},{6,3},{7,6},{10... | collective-permute-start | bytes 55304 | tf_op jit(solution)/shard_map/ppermute | solution.py:28
  107.7 3.1 %collective-permute-start.12 = (f32[3,6,1,256]{3,2,1,0:T(1,128)S(1)}, f32[3,6,1,256]{3,2,1,0:T(1,128)S(1)}, u32[]{:S(2)}, u32[]{:S(2)}) collective-permute-start(f32[3,6,1,256]{3,2,1,0:T(1,128)S(1)} %get-tuple-element.72), channel_id=1, source_target_pairs={{0,1},{1,4},{4,5},{5,8},{8,9},{9,12},{12,13},{2,3},{3,6},{6,7},{7,... | collective-permute-start | bytes 55304 | tf_op jit(solution)/shard_map/ppermute | solution.py:26
  111.8 1.3 collective-permute-start.15
  113.1 1.3 collective-permute-start.14
  114.5 3.7 %collective-permute-done.14 = f32[3,6,6,1]{3,2,1,0:T(8,128)S(1)} collective-permute-done((f32[3,6,6,1]{3,2,1,0:T(8,128)S(1)}, f32[3,6,6,1]{3,2,1,0:T(8,128)S(1)}, u32[]{:S(2)}, u32[]{:S(2)}) %collective-permute-start.14) | collective-permute-done | bytes 464 | tf_op jit(solution)/shard_map/ppermute | solution.py:26
  119.4 4.5 %collective-permute-start.17 = (f32[3,6,1,256]{3,2,1,0:T(1,128)S(1)}, f32[3,6,1,256]{3,2,1,0:T(1,128)S(1)}, u32[]{:S(2)}, u32[]{:S(2)}) collective-permute-start(f32[3,6,1,256]{3,2,1,0:T(1,128)S(1)} %get-tuple-element.71), channel_id=1, source_target_pairs={{1,0},{4,1},{5,4},{8,5},{9,8},{12,9},{13,12},{3,2},{6,3},{7,6},{10... | collective-permute-start | bytes 55304 | tf_op jit(solution)/shard_map/ppermute | solution.py:28
  123.9 3.1 %collective-permute-start.16 = (f32[3,6,1,256]{3,2,1,0:T(1,128)S(1)}, f32[3,6,1,256]{3,2,1,0:T(1,128)S(1)}, u32[]{:S(2)}, u32[]{:S(2)}) collective-permute-start(f32[3,6,1,256]{3,2,1,0:T(1,128)S(1)} %get-tuple-element.70), channel_id=1, source_target_pairs={{0,1},{1,4},{4,5},{5,8},{8,9},{9,12},{12,13},{2,3},{3,6},{6,7},{7,... | collective-permute-start | bytes 55304 | tf_op jit(solution)/shard_map/ppermute | solution.py:26
  129.3 1.3 collective-permute-start.18
  130.7 3.7 %collective-permute-done.18 = f32[3,6,6,1]{3,2,1,0:T(8,128)S(1)} collective-permute-done((f32[3,6,6,1]{3,2,1,0:T(8,128)S(1)}, f32[3,6,6,1]{3,2,1,0:T(8,128)S(1)}, u32[]{:S(2)}, u32[]{:S(2)}) %collective-permute-start.18) | collective-permute-done | bytes 464 | tf_op jit(solution)/shard_map/ppermute | solution.py:26
  134.8 5.9 %all_to_all.28 = f32[4,2,128]{2,0,1:T(4,128)S(1)} all-to-all(f32[4,2,128]{2,0,1:T(4,128)S(1)} %bitcast.125), channel_id=1, replica_groups=mesh['grp'=2,'row'=4,'col'=2,'lay'=2] {'lay'}, dimensions={1} | all-to-all | bytes 8192 | tf_op jit(solution)/shard_map/all_to_all | solution.py:195
  (94 shorter events, 14.3 us)
Async XLA Ops:
  0.6 13.9 %copy-start.1 = (f32[24,384]{1,0:T(8,128)S(1)}, f32[24,384]{1,0:T(8,128)}, u32[]{:S(2)}) copy-start(f32[24,384]{1,0:T(8,128)} %param.12) | copy-start | bytes 110596
  0.6 13.9 %copy-start = (f32[8,24,384]{2,1,0:T(8,128)S(1)}, f32[8,24,384]{2,1,0:T(8,128)}, u32[]{:S(2)}) copy-start(f32[8,24,384]{2,1,0:T(8,128)} %param.10) | copy-start | bytes 884740
  2.6 17.3 %copy-start.2 = (f32[3,6,4,256]{3,2,1,0:T(4,128)S(1)}, f32[3,6,4,256]{3,2,1,0:T(4,128)}, u32[]{:S(2)}) copy-start(f32[3,6,4,256]{3,2,1,0:T(4,128)} %param.14) | copy-start | bytes 221188
  2.6 23.6 %copy-start.5 = (f32[16]{0:T(128)S(1)}, f32[16]{0:T(128)}, u32[]{:S(2)}) copy-start(f32[16]{0:T(128)} %param.16) | copy-start | bytes 196
  2.6 24.3 %copy-start.8 = (s32[6]{0:T(128)S(1)}, s32[6]{0:T(128)}, u32[]{:S(2)}) copy-start(s32[6]{0:T(128)} %constant.28) | copy-start | bytes 76
  2.6 24.3 %copy-start.6 = (f32[16]{0:T(128)S(1)}, f32[16]{0:T(128)}, u32[]{:S(2)}) copy-start(f32[16]{0:T(128)} %param.17) | copy-start | bytes 196
  14.6 16.7 %collective-permute-start = (f32[17,2,384]{2,1,0:T(2,128)S(1)}, f32[17,2,384]{2,1,0:T(2,128)S(1)}, u32[]{:S(2)}, u32[]{:S(2)}) collective-permute-start(f32[17,2,384]{2,1,0:T(2,128)S(1)} %get-tuple-element.47), channel_id=1, source_target_pairs={{4,0},{8,4},{12,8},{5,1},{9,5},{13,9},{6,2},{10,6},{14,10},{7,3},{... | collective-permute-start | bytes 156680 | tf_op jit(solution)/shard_map/ppermute | solution.py:28
  16.6 14.6 %collective-permute-start.1 = (f32[17,2,384]{2,1,0:T(2,128)S(1)}, f32[17,2,384]{2,1,0:T(2,128)S(1)}, u32[]{:S(2)}, u32[]{:S(2)}) collective-permute-start(f32[17,2,384]{2,1,0:T(2,128)S(1)} %get-tuple-element.46), channel_id=1, source_target_pairs={{0,4},{4,8},{8,12},{1,5},{5,9},{9,13},{2,6},{6,10},{10,14},{3,7},{... | collective-permute-start | bytes 156680 | tf_op jit(solution)/shard_map/ppermute | solution.py:26
  19.9 7.7 %collective-permute-start.9 = (f32[3,6,1,256]{3,2,1,0:T(1,128)S(1)}, f32[3,6,1,256]{3,2,1,0:T(1,128)S(1)}, u32[]{:S(2)}, u32[]{:S(2)}) collective-permute-start(f32[3,6,1,256]{3,2,1,0:T(1,128)S(1)} %get-tuple-element.75), channel_id=1, source_target_pairs={{1,0},{4,1},{5,4},{8,5},{9,8},{12,9},{13,12},{3,2},{6,3},{7,6},{10... | collective-permute-start | bytes 55304 | tf_op jit(solution)/shard_map/ppermute | solution.py:28
  23.1 4.6 %collective-permute-start.8 = (f32[3,6,1,256]{3,2,1,0:T(1,128)S(1)}, f32[3,6,1,256]{3,2,1,0:T(1,128)S(1)}, u32[]{:S(2)}, u32[]{:S(2)}) collective-permute-start(f32[3,6,1,256]{3,2,1,0:T(1,128)S(1)} %get-tuple-element.74), channel_id=1, source_target_pairs={{0,1},{1,4},{4,5},{5,8},{8,9},{9,12},{12,13},{2,3},{3,6},{6,7},{7,... | collective-permute-start | bytes 55304 | tf_op jit(solution)/shard_map/ppermute | solution.py:26
  27.8 7.7 %collective-permute-start.11 = (f32[3,6,6,1]{3,2,1,0:T(8,128)S(1)}, f32[3,6,6,1]{3,2,1,0:T(8,128)S(1)}, u32[]{:S(2)}, u32[]{:S(2)}) collective-permute-start(f32[3,6,6,1]{3,2,1,0:T(8,128)S(1)} %get-tuple-element.64), channel_id=1, source_target_pairs={{2,0},{3,1},{6,4},{7,5},{10,8},{11,9},{14,12},{15,13},{18,16},{19,... | collective-permute-start | bytes 1304 | tf_op jit(solution)/shard_map/ppermute | solution.py:28
  30.0 5.5 %collective-permute-start.10 = (f32[3,6,6,1]{3,2,1,0:T(8,128)S(1)}, f32[3,6,6,1]{3,2,1,0:T(8,128)S(1)}, u32[]{:S(2)}, u32[]{:S(2)}) collective-permute-start(f32[3,6,6,1]{3,2,1,0:T(8,128)S(1)} %get-tuple-element.63), channel_id=1, source_target_pairs={{0,2},{1,3},{4,6},{5,7},{8,10},{9,11},{12,14},{13,15},{16,18},{17,... | collective-permute-start | bytes 1304 | tf_op jit(solution)/shard_map/ppermute | solution.py:26
  31.5 4.3 %collective-permute-start.3 = (f32[17,28,2]{2,1,0:T(8,128)S(1)}, f32[17,28,2]{2,1,0:T(8,128)S(1)}, u32[]{:S(2)}, u32[]{:S(2)}) collective-permute-start(f32[17,28,2]{2,1,0:T(8,128)S(1)} %get-tuple-element.45), channel_id=1, source_target_pairs={{1,0},{2,1},{3,2},{5,4},{6,5},{7,6},{9,8},{10,9},{11,10},{13,12},{... | collective-permute-start | bytes 11432 | tf_op jit(solution)/shard_map/ppermute | solution.py:28
  34.2 4.7 %collective-permute-start.2 = (f32[17,28,2]{2,1,0:T(8,128)S(1)}, f32[17,28,2]{2,1,0:T(8,128)S(1)}, u32[]{:S(2)}, u32[]{:S(2)}) collective-permute-start(f32[17,28,2]{2,1,0:T(8,128)S(1)} %get-tuple-element.44), channel_id=1, source_target_pairs={{0,1},{1,2},{2,3},{4,5},{5,6},{6,7},{8,9},{9,10},{10,11},{12,13},{... | collective-permute-start | bytes 11432 | tf_op jit(solution)/shard_map/ppermute | solution.py:26
  54.0 87.1 %copy-start.4 = (f32[8,24,384]{2,1,0:T(8,128)}, f32[8,24,384]{2,1,0:T(8,128)S(1)}, u32[]{:S(2)}) copy-start(f32[8,24,384]{2,1,0:T(8,128)S(1)} %get-tuple-element.22) | copy-start | bytes 884740
  65.4 14.2 %copy-start.7 = (s32[6,4,256]{2,1,0:T(4,128)S(1)}, s32[6,4,256]{2,1,0:T(4,128)}, u32[]{:S(2)}) copy-start(s32[6,4,256]{2,1,0:T(4,128)} %param.13) | copy-start | bytes 73732
  89.6 5.6 %collective-permute-start.5 = (f32[2,6,1,256]{3,2,1,0:T(1,128)S(1)}, f32[2,6,1,256]{3,2,1,0:T(1,128)S(1)}, u32[]{:S(2)}, u32[]{:S(2)}) collective-permute-start(f32[2,6,1,256]{3,2,1,0:T(1,128)S(1)} %get-tuple-element.77), channel_id=1, source_target_pairs={{1,0},{4,1},{5,4},{8,5},{9,8},{12,9},{13,12},{3,2},{6,3},{7,6},{10... | collective-permute-start | bytes 36872 | tf_op jit(solution)/shard_map/ppermute | solution.py:28
  91.9 4.1 %collective-permute-start.4 = (f32[2,6,1,256]{3,2,1,0:T(1,128)S(1)}, f32[2,6,1,256]{3,2,1,0:T(1,128)S(1)}, u32[]{:S(2)}, u32[]{:S(2)}) collective-permute-start(f32[2,6,1,256]{3,2,1,0:T(1,128)S(1)} %get-tuple-element.76), channel_id=1, source_target_pairs={{0,1},{1,4},{4,5},{5,8},{8,9},{9,12},{12,13},{2,3},{3,6},{6,7},{7,... | collective-permute-start | bytes 36872 | tf_op jit(solution)/shard_map/ppermute | solution.py:26
  96.1 2.8 %collective-permute-start.7 = (f32[2,6,6,1]{3,2,1,0:T(8,128)S(1)}, f32[2,6,6,1]{3,2,1,0:T(8,128)S(1)}, u32[]{:S(2)}, u32[]{:S(2)}) collective-permute-start(f32[2,6,6,1]{3,2,1,0:T(8,128)S(1)} %get-tuple-element.69), channel_id=1, source_target_pairs={{2,0},{3,1},{6,4},{7,5},{10,8},{11,9},{14,12},{15,13},{18,16},{19,... | collective-permute-start | bytes 872 | tf_op jit(solution)/shard_map/ppermute | solution.py:28
  97.4 4.8 %collective-permute-start.6 = (f32[2,6,6,1]{3,2,1,0:T(8,128)S(1)}, f32[2,6,6,1]{3,2,1,0:T(8,128)S(1)}, u32[]{:S(2)}, u32[]{:S(2)}) collective-permute-start(f32[2,6,6,1]{3,2,1,0:T(8,128)S(1)} %get-tuple-element.68), channel_id=1, source_target_pairs={{0,2},{1,3},{4,6},{5,7},{8,10},{9,11},{12,14},{13,15},{16,18},{17,... | collective-permute-start | bytes 872 | tf_op jit(solution)/shard_map/ppermute | solution.py:26
  103.5 7.3 %collective-permute-start.13 = (f32[3,6,1,256]{3,2,1,0:T(1,128)S(1)}, f32[3,6,1,256]{3,2,1,0:T(1,128)S(1)}, u32[]{:S(2)}, u32[]{:S(2)}) collective-permute-start(f32[3,6,1,256]{3,2,1,0:T(1,128)S(1)} %get-tuple-element.73), channel_id=1, source_target_pairs={{1,0},{4,1},{5,4},{8,5},{9,8},{12,9},{13,12},{3,2},{6,3},{7,6},{10... | collective-permute-start | bytes 55304 | tf_op jit(solution)/shard_map/ppermute | solution.py:28
  107.7 4.0 %collective-permute-start.12 = (f32[3,6,1,256]{3,2,1,0:T(1,128)S(1)}, f32[3,6,1,256]{3,2,1,0:T(1,128)S(1)}, u32[]{:S(2)}, u32[]{:S(2)}) collective-permute-start(f32[3,6,1,256]{3,2,1,0:T(1,128)S(1)} %get-tuple-element.72), channel_id=1, source_target_pairs={{0,1},{1,4},{4,5},{5,8},{8,9},{9,12},{12,13},{2,3},{3,6},{6,7},{7,... | collective-permute-start | bytes 55304 | tf_op jit(solution)/shard_map/ppermute | solution.py:26
  111.8 2.7 %collective-permute-start.15 = (f32[3,6,6,1]{3,2,1,0:T(8,128)S(1)}, f32[3,6,6,1]{3,2,1,0:T(8,128)S(1)}, u32[]{:S(2)}, u32[]{:S(2)}) collective-permute-start(f32[3,6,6,1]{3,2,1,0:T(8,128)S(1)} %get-tuple-element.62), channel_id=1, source_target_pairs={{2,0},{3,1},{6,4},{7,5},{10,8},{11,9},{14,12},{15,13},{18,16},{19,... | collective-permute-start | bytes 1304 | tf_op jit(solution)/shard_map/ppermute | solution.py:28
  113.1 5.1 %collective-permute-start.14 = (f32[3,6,6,1]{3,2,1,0:T(8,128)S(1)}, f32[3,6,6,1]{3,2,1,0:T(8,128)S(1)}, u32[]{:S(2)}, u32[]{:S(2)}) collective-permute-start(f32[3,6,6,1]{3,2,1,0:T(8,128)S(1)} %get-tuple-element.61), channel_id=1, source_target_pairs={{0,2},{1,3},{4,6},{5,7},{8,10},{9,11},{12,14},{13,15},{16,18},{17,... | collective-permute-start | bytes 1304 | tf_op jit(solution)/shard_map/ppermute | solution.py:26
  119.4 21.5 %copy-start.3 = (f32[3,6,4,256]{3,2,1,0:T(4,128)}, f32[3,6,4,256]{3,2,1,0:T(4,128)S(1)}, u32[]{:S(2)}) copy-start(f32[3,6,4,256]{3,2,1,0:T(4,128)S(1)} %add_add_fusion) | copy-start | bytes 221188
  119.4 7.6 %collective-permute-start.17 = (f32[3,6,1,256]{3,2,1,0:T(1,128)S(1)}, f32[3,6,1,256]{3,2,1,0:T(1,128)S(1)}, u32[]{:S(2)}, u32[]{:S(2)}) collective-permute-start(f32[3,6,1,256]{3,2,1,0:T(1,128)S(1)} %get-tuple-element.71), channel_id=1, source_target_pairs={{1,0},{4,1},{5,4},{8,5},{9,8},{12,9},{13,12},{3,2},{6,3},{7,6},{10... | collective-permute-start | bytes 55304 | tf_op jit(solution)/shard_map/ppermute | solution.py:28
  123.9 4.0 %collective-permute-start.16 = (f32[3,6,1,256]{3,2,1,0:T(1,128)S(1)}, f32[3,6,1,256]{3,2,1,0:T(1,128)S(1)}, u32[]{:S(2)}, u32[]{:S(2)}) collective-permute-start(f32[3,6,1,256]{3,2,1,0:T(1,128)S(1)} %get-tuple-element.70), channel_id=1, source_target_pairs={{0,1},{1,4},{4,5},{5,8},{8,9},{9,12},{12,13},{2,3},{3,6},{6,7},{7,... | collective-permute-start | bytes 55304 | tf_op jit(solution)/shard_map/ppermute | solution.py:26
  128.0 2.7 %collective-permute-start.19 = (f32[3,6,6,1]{3,2,1,0:T(8,128)S(1)}, f32[3,6,6,1]{3,2,1,0:T(8,128)S(1)}, u32[]{:S(2)}, u32[]{:S(2)}) collective-permute-start(f32[3,6,6,1]{3,2,1,0:T(8,128)S(1)} %get-tuple-element.60), channel_id=1, source_target_pairs={{2,0},{3,1},{6,4},{7,5},{10,8},{11,9},{14,12},{15,13},{18,16},{19,... | collective-permute-start | bytes 1304 | tf_op jit(solution)/shard_map/ppermute | solution.py:28
  129.3 5.1 %collective-permute-start.18 = (f32[3,6,6,1]{3,2,1,0:T(8,128)S(1)}, f32[3,6,6,1]{3,2,1,0:T(8,128)S(1)}, u32[]{:S(2)}, u32[]{:S(2)}) collective-permute-start(f32[3,6,6,1]{3,2,1,0:T(8,128)S(1)} %get-tuple-element.59), channel_id=1, source_target_pairs={{0,2},{1,3},{4,6},{5,7},{8,10},{9,11},{12,14},{13,15},{16,18},{17,... | collective-permute-start | bytes 1304 | tf_op jit(solution)/shard_map/ppermute | solution.py:26
where the time goes:
time: 143 us; the launch traced here: 142 us
  starting transfers between devices  47.3 us (33%)
  other arithmetic  45.4 us (32%)
  local copies, waits for them, and re-layouts  17.1 us (12%)
  waiting for transfers between devices  16.5 us (12%)
  blocking collectives  14.2 us (10%)
    ppermute x10, starting transfers between devices, padded_2(): lax.ppermute(head, axis, [((i + 1) % count, i) for i in range(ends)])  24.8 us
    ppermute x10, starting transfers between devices, padded_2(): lax.ppermute(tail, axis, [(i, (i + 1) % count) for i in range(ends)])  22.5 us
    ppermute x10, waiting for transfers between devices, padded_2(): lax.ppermute(tail, axis, [(i, (i + 1) % count) for i in range(ends)])  16.3 us
    select_n x1, other arithmetic, lookup(): result = jnp.where(material == m, table[m], result)  11.8 us
    mul x1, other arithmetic, per_device(): linear_growth_rate * present_heat_level  11.6 us
    another operation x1, other arithmetic, per_device(): jnp.stack([modulus, modulus * arrived])  9.92 us
    all_to_all x1, blocking collectives, per_device(): lax.all_to_all(outgoing, 'lay', split_axis=1, concat_axis=3, tiled=True)  8.3 us
    reshape x1, local copies, waits for them, and re-layouts, per_device(): (linear_growth_rate * present_heat_level).reshape(HEAT_GRID_DEPTH, coarse...  8.14 us
  transfers between devices with their start and end apart: 20, of which 9 were waited for; matrix products, arithmetic and copies ran while one was open for 1% of the time, Pallas kernels for 0%

commit v1 on v0

v1 whole, which is shorter than its diff:
```python
import functools

import jax
import jax.numpy as jnp
from jax import lax
from jax.experimental import pallas as pl
from jax.experimental.pallas import tpu as pltpu
from jax.sharding import PartitionSpec as P

DEPTH = 8
ML = 6
LANES = 128
HALO = 11
MHALO = 3

STIFF_DIAG = 12.0
THETA = 1.0
DELTA = 0.75
SIGMA = THETA / DELTA
RHO0 = 1.0 / SIGMA
RHO1 = 1.0 / (2.0 * SIGMA - RHO0)

VMEM = pl.BlockSpec(memory_space=pltpu.VMEM)
SMEM = pl.BlockSpec(memory_space=pltpu.SMEM)


def call(kernel, outs, args, scratch=(), smem=0):
    return pl.pallas_call(
        kernel,
        out_shape=[jax.ShapeDtypeStruct(s, jnp.float32) for s in outs],
        in_specs=[SMEM] * smem + [VMEM] * (len(args) - smem),
        out_specs=[VMEM] * len(outs),
        scratch_shapes=[pltpu.VMEM(s, jnp.float32) for s in scratch],
        compiler_params=pltpu.CompilerParams(vmem_limit_bytes=16 * 1024 * 1024),
    )(*args)


def lane_iota(rows=8):
    return lax.broadcasted_iota(jnp.int32, (rows, LANES), 1)


def sub_iota(width):
    return lax.broadcasted_iota(jnp.int32, (8, width), 0)


def tiles(x):
    return [x[:, LANES * t : LANES * (t + 1)] for t in range(x.shape[1] // LANES)]


def gather_lanes(table, index):
    return jnp.take_along_axis(table, index, axis=1, mode="promise_in_bounds")


def lookup(table, code):
    return jnp.concatenate([gather_lanes(table, c.astype(jnp.int32)) for c in tiles(code)], axis=1)


def prev_lane(x):
    return pltpu.roll(x, 1, 1)


def next_lane(x):
    return pltpu.roll(x, x.shape[1] - 1, 1)


def prev_sub(x):
    return pltpu.roll(x, 1, 0)


def next_sub(x):
    return pltpu.roll(x, 7, 0)


def row8(ref, i):
    return ref[8 * i : 8 * i + 8, :]


def k_rows(t_ref, id_ref, src_ref, u_ref, mat_ref, a_ref, m_ref):
    rows = t_ref.shape[1]
    for t in range(t_ref.shape[2] // LANES):
        at = 17 * rows * t
        lanes = slice(LANES * t, LANES * (t + 1))
        for l in range(DEPTH):
            a_ref[pl.ds(at + l, rows, stride=16), :] = t_ref[l, :, lanes]
            a_ref[pl.ds(at + 8 + l, rows, stride=16), :] = (id_ref[l, :, lanes] + 1).astype(jnp.float32)
        a_ref[at + 16 * rows : at + 17 * rows, :] = src_ref[:, lanes]
    mrows = mat_ref.shape[1]
    m_ref[...] = jnp.zeros(m_ref.shape, jnp.float32)
    for t in range(mat_ref.shape[2] // LANES):
        at = 32 * mrows * t
        lanes = slice(LANES * t, LANES * (t + 1))
        for l in range(ML):
            for f in range(3):
                m_ref[pl.ds(at + 8 * f + l, mrows, stride=32), :] = u_ref[f, l, :, lanes]
            m_ref[pl.ds(at + 24 + l, mrows, stride=32), :] = (mat_ref[l, :, lanes] + 1).astype(jnp.float32)


def k_chip(n_edges, rows, flags, a_ref, b_ref, m_ref, n_ref, z_ref, w_ref, src_ref, mw_ref, *edge_refs):
    n_t = a_ref.shape[0] // (17 * rows)
    half = LANES * n_t
    mcols = mw_ref.shape[1]
    m_t = mcols // LANES
    mrows = m_ref.shape[0] // (32 * m_t)

    def build(left, right, rev):
        for t in range(2 * n_t):
            part = left if t < n_t else right
            base = 17 * rows * (t % n_t)
            lanes = slice(LANES * t, LANES * (t + 1))
            for g in range(rows - 1):
                i = base + 16 * (rows - 1 - g if rev else g)
                dst, at = (z_ref, 16 * g) if g < HALO else (w_ref, 16 * (g - HALO))
                dst[at : at + 16, lanes] = part[i : i + 16, :]
            for g in range(rows):
                i = base + 16 * rows + (rows - 1 - g if rev else g)
                src_ref[g : g + 1, lanes] = part[i : i + 1, :]
        for t in range(m_t):
            lanes = slice(LANES * t, LANES * (t + 1))
            for g in range(mrows + MHALO):
                if g < mrows:
                    i = mrows - 1 - g if rev else g
                    part = m_ref
                else:
                    i = 2 * mrows - 1 - g if rev else g - mrows
                    part = n_ref
                i = 32 * (mrows * t + i)
                mw_ref[32 * g : 32 * g + 32, lanes] = part[i : i + 32, :]

    @pl.when(flags[0] == 0)
    def _():
        build(a_ref, b_ref, False)

    @pl.when(flags[0] != 0)
    def _():
        build(b_ref, a_ref, True)

    for g in range(MHALO):
        z_ref[16 * HALO : 16 * HALO + 32, mcols * g : mcols * (g + 1)] = mw_ref[32 * g : 32 * g + 32, :]
    z_ref[16 * HALO + 32 : 16 * HALO + 48, :] = src_ref[0:16, :]

    lane = lane_iota()
    near = (lane < HALO) | (lane >= LANES - HALO)
    groups = [((lane - 32 * f + MHALO) & (LANES - 1)) < 2 * MHALO for f in range(4)]
    for e in range(n_edges):
        c_ref, d_ref = edge_refs[2 * e], edge_refs[2 * e + 1]
        right_edge = flags[1 + e]
        start = pl.multiple_of(right_edge * (2 * half - LANES), LANES)
        mstart = pl.multiple_of(right_edge * (mcols - LANES), LANES)
        lanes = pl.ds(start, LANES)
        mlanes = pl.ds(mstart, LANES)
        for g in range(rows - 1):
            src, at = (z_ref, 16 * g) if g < HALO else (w_ref, 16 * (g - HALO))
            t = src[at : at + 8, lanes]
            code = src[at + 8 : at + 16, lanes]
            merged = jnp.where(near, t, pltpu.roll(code, 64, 1))
            c_ref[8 * g : 8 * g + 8, :] = merged
            if g < HALO:
                d_ref[8 * g : 8 * g + 8, :] = merged
        at = 8 * (rows - 1)
        c_ref[at : at + rows, :] = src_ref[:, lanes]
        d_ref[8 * HALO : 8 * HALO + 16, :] = src_ref[0:16, lanes]
        for g in range(mrows + MHALO):
            merged = jnp.zeros((8, LANES), jnp.float32)
            for f in range(4):
                field = mw_ref[32 * g + 8 * f : 32 * g + 8 * f + 8, mlanes]
                merged = jnp.where(groups[f], pltpu.roll(field, 32 * f, 1) if f else field, merged)
            c_ref[at + rows + 8 * g : at + rows + 8 * g + 8, :] = merged
            if g < MHALO:
                d_ref[8 * HALO + 16 + 8 * g : 8 * HALO + 24 + 8 * g, :] = merged


class Sides:
    def __init__(self, flags, from_left, from_right):
        self.left = from_left
        self.right = from_right
        lane = lane_iota()
        has_left = flags[3] != 0
        has_right = flags[4] != 0
        self.masks = {
            w: ((lane < w) & has_right, (lane >= LANES - w) & has_left) for w in (HALO, MHALO)
        }

    def tile(self, at, count, width, turn=0):
        right_mask, left_mask = (m[:count] for m in self.masks[width])
        r = self.right[at : at + count, :]
        l = r if self.left is self.right else self.left[at : at + count, :]
        if turn:
            r = pltpu.roll(r, turn, 1)
            l = r if self.left is self.right else pltpu.roll(l, turn, 1)
        return jnp.where(right_mask, r, jnp.where(left_mask, l, 0.0))


def conduct_sum(ref, i, below, above):
    x = row8(ref, i)
    width = x.shape[1]
    sub = sub_iota(width)
    total = row8(ref, below) + row8(ref, above) + prev_lane(x) + next_lane(x)
    total = total + jnp.where(sub < DEPTH - 1, next_sub(x), 0.0)
    return total + jnp.where(sub > 0, prev_sub(x), 0.0)


def sink(width):
    return jnp.where(sub_iota(width) == DEPTH - 1, 2.0, 0.2).astype(jnp.float32)


def restrict_columns(x):
    width = x.shape[1]
    x = x + pltpu.roll(x, width - 1, 1) + pltpu.roll(x, width - 2, 1)
    pieces = tiles(x)
    lane = lane_iota()
    out = []
    for j in range((len(pieces) - 1) // 3):
        got = None
        for t in range(3):
            g = gather_lanes(pieces[3 * j + t], (3 * lane) & (LANES - 1))
            got = g if got is None else jnp.where((3 * lane) >= LANES * t, g, got)
        out.append(got)
    first = LANES - MHALO
    index = jnp.where(lane < MHALO, 3 * lane, jnp.where(lane >= first, LANES - 9 + 3 * (lane - first), 64))
    out.append(gather_lanes(pieces[-1], index))
    y = jnp.concatenate(out, axis=1)
    y = jnp.where(sub_iota(y.shape[1]) < 3, y, next_sub(y))
    return y * (1.0 / 9.0)


def k_inner(n_sides, rows, flags, tab, z_ref, w_ref, src_ref, *refs):
    sides = Sides(flags, refs[0], refs[n_sides - 1])
    s_ref, al_ref, q0_ref, q1_ref, di_ref, t_ref, ea_ref, strain_ref = refs[n_sides:]
    own = rows - 1
    wide = src_ref.shape[1]
    width = wide + LANES
    t_s = jnp.sqrt(tab[0:8, :])
    t_al = tab[8:16, :]
    for g in range(own):
        src, at = (z_ref, 16 * g) if g < HALO else (w_ref, 16 * (g - HALO))
        temp = jnp.concatenate([src[at : at + 8, :], sides.tile(8 * g, 8, HALO)], axis=1)
        code = jnp.concatenate([src[at + 8 : at + 16, :], sides.tile(8 * g, 8, HALO, 64)], axis=1)
        s = lookup(t_s, code)
        s_ref[8 * g : 8 * g + 8, :] = s
        al_ref[8 * g : 8 * g + 8, :] = lookup(t_al, code)
        q0_ref[8 * g : 8 * g + 8, :] = s * temp
    top = sub_iota(width) == 0
    h = sink(width)
    for g in range(1, own - 1):
        s = row8(s_ref, g)
        inv = 1.0 / (h + s * conduct_sum(s_ref, g, g - 1, g + 1))
        di_ref[8 * g : 8 * g + 8, :] = inv
        power = jnp.concatenate([src_ref[g : g + 1, :], sides.tile(8 * own + g, 1, HALO)], axis=1)
        power = jnp.where(top, jnp.broadcast_to(power, (8, width)), 0.0)
        t1 = (power + s * conduct_sum(q0_ref, g, g - 1, g + 1)) * inv
        q1_ref[8 * g : 8 * g + 8, :] = s * t1
    for g in range(2, own - 2):
        power = jnp.concatenate([src_ref[g : g + 1, :], sides.tile(8 * own + g, 1, HALO)], axis=1)
        power = jnp.where(top, jnp.broadcast_to(power, (8, width)), 0.0)
        t2 = (power + row8(s_ref, g) * conduct_sum(q1_ref, g, g - 1, g + 1)) * row8(di_ref, g)
        t_ref[8 * g : 8 * g + 8, :] = t2
        ea_ref[8 * g : 8 * g + 8, :] = row8(al_ref, g) * t2
    for m in range(1, (own - 2) // 3):
        x = row8(ea_ref, 3 * m) + row8(ea_ref, 3 * m + 1) + row8(ea_ref, 3 * m + 2)
        strain_ref[8 * m : 8 * m + 8, :] = restrict_columns(x)


def couple_sum(rows3):
    near = [[None] * 3 for _ in range(3)]
    for j in range(3):
        below, mid, above = rows3[j]
        near[0][j] = next_sub(mid) + prev_sub(mid)
        near[1][j] = above + below
        near[2][j] = next_lane(mid) + prev_lane(mid)
    out = []
    for i in range(3):
        j, k = [x for x in range(3) if x != i]
        main = near[i][i] + 0.5 * (near[j][i] + near[k][i])
        side = (near[i][j] + near[j][j]) + (near[i][k] + near[k][k])
        out.append(main + 0.25 * side)
    return out


def k_outer(n_sides, rows, flags, tab, zr_ref, mw_ref, *refs):
    sides = Sides(flags, refs[0], refs[n_sides - 1])
    corners = Sides(flags, refs[n_sides], refs[2 * n_sides - 1])
    rest = refs[2 * n_sides :]
    s_in, al_in, q0_in, q1_in, di_in, t_in, ea_in, strain_in, src_ref = rest[:9]
    x_ref, keep_ref, u_ref = rest[9:12]
    s_ref, q0_ref, q1_ref, di_ref, al_ref, ea_ref, st_ref = rest[12:19]
    ms_ref, mi_ref, mod_ref, sf_ref = rest[19:23]
    uu_refs = rest[23:26]
    p_refs = rest[26:29]
    d_refs = rest[29:32]
    own = rows - 1
    wide = zr_ref.shape[1]
    half = wide // 2
    width = wide + LANES
    t_s = jnp.sqrt(tab[0:8, :])
    t_al = tab[8:16, :]
    zsrc = 16 * HALO + 32
    for j in range(HALO):
        i = HALO - 1 - j
        temp = jnp.concatenate([zr_ref[16 * j : 16 * j + 8, :], corners.tile(8 * j, 8, HALO)], axis=1)
        code = jnp.concatenate([zr_ref[16 * j + 8 : 16 * j + 16, :], corners.tile(8 * j, 8, HALO, 64)], axis=1)
        s = lookup(t_s, code)
        s_ref[8 * i : 8 * i + 8, :] = s
        al_ref[8 * i : 8 * i + 8, :] = lookup(t_al, code)
        q0_ref[8 * i : 8 * i + 8, :] = s * temp
    for g in range(3):
        i = 8 * (HALO + g)
        s_ref[i : i + 8, :] = row8(s_in, g)
        al_ref[i : i + 8, :] = row8(al_in, g)
        q0_ref[i : i + 8, :] = row8(q0_in, g)
        if g > 0:
            q1_ref[i : i + 8, :] = row8(q1_in, g)
            di_ref[i : i + 8, :] = row8(di_in, g)
    top = sub_iota(width) == 0
    h = sink(width)

    def power_of(g):
        if g < 0:
            j = -1 - g
            p = [zr_ref[zsrc + j : zsrc + j + 1, :], corners.tile(8 * HALO + j, 1, HALO)]
        else:
            p = [src_ref[g : g + 1, :], sides.tile(8 * own + g, 1, HALO)]
        p = jnp.concatenate(p, axis=1)
        return jnp.where(top, jnp.broadcast_to(p, (8, width)), 0.0)

    for g in range(1 - HALO, 1):
        i = HALO + g
        s = row8(s_ref, i)
        inv = 1.0 / (h + s * conduct_sum(s_ref, i, i - 1, i + 1))
        di_ref[8 * i : 8 * i + 8, :] = inv
        t1 = (power_of(g) + s * conduct_sum(q0_ref, i, i - 1, i + 1)) * inv
        q1_ref[8 * i : 8 * i + 8, :] = s * t1
    ea_ref[8 * (HALO + 2) : 8 * (HALO + 3), :] = row8(ea_in, 2)

    core = flags[0]

    def other_half(x):
        return jnp.where(core == 0, x[:, half:wide], x[:, 0:half])

    def own_half(x):
        return jnp.where(core == 0, x[:, 0:half], x[:, half:wide])

    for g in range(2 - HALO, 2):
        i = HALO + g
        t2 = (power_of(g) + row8(s_ref, i) * conduct_sum(q1_ref, i, i - 1, i + 1)) * row8(di_ref, i)
        ea_ref[8 * i : 8 * i + 8, :] = row8(al_ref, i) * t2
        if g >= 0:
            keep_ref[8 * g : 8 * g + 8, :] = own_half(t2)
            x_ref[8 * g : 8 * g + 8, :] = other_half(t2)
    x_ref[16:24, :] = other_half(row8(t_in, 2))

    mrows = mw_ref.shape[0] // 32 - MHALO
    mcols = mw_ref.shape[1]
    mwidth = mcols + LANES
    n_m = mrows + 2 * MHALO
    for m in range(MHALO + 1):
        i = 3 * m + 2
        x = row8(ea_ref, i) + row8(ea_ref, i + 1) + row8(ea_ref, i + 2)
        st_ref[8 * m : 8 * m + 8, :] = restrict_columns(x)
    for m in range(1, mrows + MHALO):
        i = MHALO + m
        st_ref[8 * i : 8 * i + 8, :] = row8(strain_in, m)
    t_mod = tab[16:24, :]
    t_m = jnp.sqrt(t_mod)
    t_mi = jnp.where(t_mod > 0.0, 1.0 / jnp.where(t_mod > 0.0, t_m, 1.0), 0.0)
    at_own = 8 * own + rows
    at_corner = 8 * HALO + 16
    for i in range(n_m):
        m = i - MHALO
        fields = []
        for f in range(4):
            turn = (LANES - 32 * f) % LANES
            if m < 0:
                j = -1 - m
                body = zr_ref[16 * HALO + 8 * f : 16 * HALO + 8 * f + 8, mcols * j : mcols * (j + 1)]
                side = corners.tile(at_corner + 8 * j, 8, MHALO, turn)
            else:
                body = mw_ref[32 * m + 8 * f : 32 * m + 8 * f + 8, :]
                side = sides.tile(at_own + 8 * m, 8, MHALO, turn)
            fields.append(jnp.concatenate([body, side], axis=1))
        at = slice(8 * i, 8 * i + 8)
        code = fields[3]
        root = lookup(t_m, code)
        mod = lookup(t_mod, code)
        ms_ref[at, :] = root
        mi_ref[at, :] = lookup(t_mi, code)
        mod_ref[at, :] = mod
        sf_ref[at, :] = mod * row8(st_ref, i)
        for f in range(3):
            uu_refs[f][at, :] = root * fields[f]
    sign = jnp.where(core == 0, 0.5, -0.5).astype(jnp.float32)
    for i in range(1, n_m - 1):
        at = slice(8 * i, 8 * i + 8)
        load = row8(sf_ref, i)
        force = [
            0.5 * (next_sub(load) - prev_sub(load)),
            sign * (row8(sf_ref, i + 1) - row8(sf_ref, i - 1)),
            0.5 * (next_lane(load) - prev_lane(load)),
        ]
        near = couple_sum([[row8(r, i - 1), row8(r, i), row8(r, i + 1)] for r in uu_refs])
        inv = row8(mi_ref, i)
        for d in range(3):
            p = (force[d] * inv + near[d]) * (1.0 / STIFF_DIAG) - row8(uu_refs[d], i)
            p_refs[d][at, :] = jnp.where(inv > 0.0, p, 0.0)
    c_near = 2.0 * RHO1 / DELTA / STIFF_DIAG
    c_self = 1.0 + RHO1 * RHO0
    for i in range(2, n_m - 2):
        at = slice(8 * i, 8 * i + 8)
        near = couple_sum([[row8(r, i - 1), row8(r, i), row8(r, i + 1)] for r in p_refs])
        inv = row8(mi_ref, i)
        for d in range(3):
            moved = row8(uu_refs[d], i) + c_self * row8(p_refs[d], i) + c_near * near[d]
            d_refs[d][at, :] = moved * inv
    sub = sub_iota(mwidth)
    weight = jnp.where(sub < ML, (ML - sub).astype(jnp.float32) * (1.0 / (ML * (ML + 1) / 2.0)), 0.0)
    x_ref[24:32, :] = jnp.zeros((8, x_ref.shape[1]), jnp.float32)
    for g in range(mrows):
        i = MHALO + g
        u0, u2 = row8(d_refs[0], i), row8(d_refs[2], i)
        div = 0.5 * (next_sub(u0) - prev_sub(u0)) + 0.5 * (next_lane(u2) - prev_lane(u2))
        div = div + sign * (row8(d_refs[1], i + 1) - row8(d_refs[1], i - 1))
        stress = row8(mod_ref, i) * (div - 3.0 * row8(st_ref, i))
        die = jnp.sum(weight * stress, axis=0, keepdims=True)
        first, second = die[:, 0:LANES], die[:, LANES : 2 * LANES]
        keep_ref[16 + g : 17 + g, 0:LANES] = jnp.where(core == 0, first, second)
        x_ref[24 + g : 25 + g, 0:LANES] = jnp.where(core == 0, second, first)
        for d in range(3):
            u_ref[8 * (mrows * d + g) : 8 * (mrows * d + g) + 8, :] = row8(d_refs[d], i)[:, 0:mcols]


def k_out(rows, mrows, flags, t_in, keep_ref, xr_ref, u_in, t_out, u_out, slow_ref, buf, die, wide_die, ubuf):
    half = slow_ref.shape[1]
    mcols = u_in.shape[1]
    core = flags[0]

    def put(ref, at, x):
        count = ref.shape[0] * LANES // x.shape[1]
        for t, piece in enumerate(tiles(x)):
            ref[count * t + at : count * t + at + piece.shape[0], :] = piece

    def build(rev):
        lo = half if rev else 0
        for g in range(rows):
            i = rows - 1 - g if rev else g
            if g < 2:
                x = keep_ref[8 * g : 8 * g + 8, :]
            elif g < rows - 3:
                x = t_in[8 * g : 8 * g + 8, lo : lo + half]
            else:
                k = rows - 1 - g
                x = xr_ref[8 * k : 8 * k + 8, :]
            put(buf, 8 * i, x)
        for g in range(mrows):
            mine = 2 * mrows - 1 - g if rev else g
            theirs = g if rev else 2 * mrows - 1 - g
            die[mine : mine + 1, :] = keep_ref[16 + g : 17 + g, 0:LANES]
            die[theirs : theirs + 1, :] = xr_ref[24 + g : 25 + g, 0:LANES]
            for d in range(3):
                i = mrows - 1 - g if rev else g
                put(ubuf, 8 * (mrows * d + i), row8(u_in, mrows * d + g))

    @pl.when(core == 0)
    def _():
        build(False)

    @pl.when(core != 0)
    def _():
        build(True)

    for t in range(half // LANES):
        at = 8 * rows * t
        lanes = slice(LANES * t, LANES * (t + 1))
        for l in range(DEPTH):
            t_out[l, :, lanes] = buf[pl.ds(at + l, rows, stride=8), :]
    for t in range(mcols // LANES):
        lanes = slice(LANES * t, LANES * (t + 1))
        for d in range(3):
            for l in range(ML):
                u_out[d, l, :, lanes] = ubuf[pl.ds(8 * mrows * (3 * t + d) + l, mrows, stride=8), :]
    lane = lane_iota(2 * mrows)
    for t in range(half // LANES):
        x = gather_lanes(die[...], (lane + LANES * t) // 3)
        for b in range(3):
            wide_die[pl.ds(b, 2 * mrows, stride=3), :] = x
        lanes = slice(LANES * t, LANES * (t + 1))
        slow_ref[:, lanes] = 1.0 + 0.2 * buf[pl.ds(8 * rows * t, rows, stride=8), :] + 0.5 * wide_die[...]


def pairs(dims, sends):
    index = {}
    for r in range(dims[0]):
        for c in range(dims[1]):
            for a in range(dims[2]):
                index[(r, c, a)] = (r * dims[1] + c) * dims[2] + a
    out = []
    for source in index:
        target = sends(*source)
        if target in index:
            out.append((index[source], index[target]))
    return out


def per_device(temp, ids, power, mat, offset, heat_table, growth_table, modulus_table):
    axes = ("row", "col", "lay")
    dims = tuple(lax.axis_size(x) for x in axes)
    n_col = dims[1]
    depth, rows, half = temp.shape
    _, _, mrows, mcols = offset.shape
    a = lax.axis_index("lay")
    c = lax.axis_index("col")
    n_edges = 1 if n_col == 2 else 2
    first_edge = jnp.where(c == 0, 1, 0) if n_col == 2 else jnp.int32(1)
    flags = jnp.stack([a, first_edge, jnp.int32(0), c > 0, c < n_col - 1]).astype(jnp.int32)
    tab = jnp.stack([heat_table, growth_table, modulus_table])
    tab = jnp.pad(tab, ((0, 0), (1, LANES - 1 - tab.shape[1])))
    tab = jnp.broadcast_to(tab[:, None, :], (3, 8, LANES)).reshape(24, LANES)

    def send(x, sends):
        return lax.ppermute(x, axes, pairs(dims, sends))

    def swap(r, c, a):
        return (r, c, 1 - a)

    def along(r, c, a):
        return (r + 1, c, 0) if a == 1 else (r - 1, c, 1)

    mine, mech = call(k_rows, [(17 * rows * half // LANES, LANES), (32 * mrows * mcols // LANES, LANES)], [temp, ids, power, offset, mat])
    theirs = send(mine, swap)
    mech2 = send(mech, swap)
    wide = 2 * half
    own = rows - 1
    n_c = 8 * own + rows + 8 * (mrows + MHALO)
    n_d = 8 * HALO + 16 + 8 * MHALO
    z, w, src, mw, *edges = call(
        functools.partial(k_chip, n_edges, rows),
        [(16 * HALO + 48, wide), (16 * (own - HALO), wide), (rows, wide), (32 * (mrows + MHALO), mcols)]
        + [(n_c, LANES), (n_d, LANES)] * n_edges,
        [flags, mine, theirs, mech, mech2],
        smem=1,
    )
    zr = send(z, along)
    if n_edges == 1:
        sides = [send(edges[0], lambda r, c, a: (r, 1 - c, a))]
        corners = [send(edges[1], lambda r, c, a: along(r, 1 - c, a))]
    else:
        sides = [send(edges[0], lambda r, c, a: (r, c + 1, a)), send(edges[2], lambda r, c, a: (r, c - 1, a))]
        corners = [
            send(edges[1], lambda r, c, a: along(r, c + 1, a)),
            send(edges[3], lambda r, c, a: along(r, c - 1, a)),
        ]
    width = wide + LANES
    mwidth = mcols + LANES
    inner = call(
        functools.partial(k_inner, n_edges, rows),
        [(8 * own, width)] * 7 + [(8 * (mrows + MHALO), mwidth)],
        [flags, tab, z, w, src] + sides,
        smem=1,
    )
    t2 = inner[5]
    n_h = 8 * (HALO + 3)
    n_m = 8 * (mrows + 2 * MHALO)
    x, keep, u = call(
        functools.partial(k_outer, n_edges, rows),
        [(32, half), (24, half), (24 * mrows, mcols)],
        [flags, tab, zr, mw] + sides + corners + list(inner) + [src],
        scratch=[(n_h, width)] * 6 + [(n_m, mwidth)] * 14,
        smem=1,
    )
    xr = send(x, swap)
    t_out, u_out, slow = call(
        functools.partial(k_out, rows, mrows),
        [temp.shape, offset.shape, power.shape],
        [flags, t2, keep, xr, u],
        scratch=[
            (8 * rows * half // LANES, LANES),
            (2 * mrows, LANES),
            (rows, LANES),
            (24 * mrows * mcols // LANES, LANES),
        ],
        smem=1,
    )
    return t_out, u_out, slow


def solution(mesh):
    placed = (
        P("grp", "row", ("col", "lay")),
        P("grp", "row", ("col", "lay")),
        P(("grp", "row"), ("col", "lay")),
        P("grp", ("row", "lay"), "col"),
        P(None, "grp", ("row", "lay"), "col"),
        P(),
        P(),
        P(),
    )
    return jax.shard_map(
        per_device,
        mesh=mesh,
        in_specs=placed,
        out_specs=(
            P("grp", "row", ("col", "lay")),
            P(None, "grp", ("row", "lay"), "col"),
            P(("grp", "row"), ("col", "lay")),
        ),
        check_vma=False,
    )
```

time: 143 us -> 30.1 us (0.21)
  the two profiles are of different devices: /device:TPU:11 before, /device:TPU:0 now
where the time goes in v1:
time: 30.1 us; the launch traced here: 29.7 us
  Pallas kernels  10 us (33%)
  starting transfers between devices  8.86 us (29%)
  local copies, waits for them, and re-layouts  5.06 us (17%)
  waiting for transfers between devices  4.92 us (16%)
  between operations  0.74 us (2%)
    pallas_call x5, Pallas kernels, call(): pl.pallas_call(kernel, out_shape=[jax.ShapeDtypeStruct(s, jnp.float32) fo...  10 us
    ppermute x6, starting transfers between devices, send(): return lax.ppermute(x, axes, pairs(dims, sends))  8.86 us
    unnamed x16, local copies, waits for them, and re-layouts  4.97 us
    ppermute x6, waiting for transfers between devices, send(): return lax.ppermute(x, axes, pairs(dims, sends))  4.92 us
  transfers between devices with their start and end apart: 6, of which 3 were waited for; matrix products, arithmetic and copies ran while one was open for 1% of the time, Pallas kernels for 14%

profile of v1, /device:TPU:0, one launch (start us, length us, event | category | flops | bytes accessed | tf_op | source)
XLA Modules:
  0.0 29.7 jit_solution(14295125700637014894)
XLA Ops:
  0.6 0.0 copy-start
  0.6 1.0 %copy-done = f32[8,24,384]{2,1,0:T(8,128)S(1)} copy-done((f32[8,24,384]{2,1,0:T(8,128)S(1)}, f32[8,24,384]{2,1,0:T(8,128)}, u32[]{:S(2)}) %copy-start) | copy-done | bytes 294936
  1.6 0.0 copy-start.1
  1.6 1.0 %copy-done.1 = s32[8,24,384]{2,1,0:T(8,128)S(1)} copy-done((s32[8,24,384]{2,1,0:T(8,128)S(1)}, s32[8,24,384]{2,1,0:T(8,128)}, u32[]{:S(2)}) %copy-start.1) | copy-done | bytes 294936
  2.6 0.9 %copy-done.2 = f32[3,6,4,256]{3,2,1,0:T(4,128)S(1)} copy-done((f32[3,6,4,256]{3,2,1,0:T(4,128)S(1)}, f32[3,6,4,256]{3,2,1,0:T(4,128)}, u32[]{:S(2)}) %copy-start.2) | copy-done | bytes 73752
  3.4 0.8 %copy-done.3 = f32[24,384]{1,0:T(8,128)S(1)} copy-done((f32[24,384]{1,0:T(8,128)S(1)}, f32[24,384]{1,0:T(8,128)}, u32[]{:S(2)}) %copy-start.3) | copy-done | bytes 36888
  4.2 0.7 %copy-done.4 = s32[6,4,256]{2,1,0:T(4,128)S(1)} copy-done((s32[6,4,256]{2,1,0:T(4,128)S(1)}, s32[6,4,256]{2,1,0:T(4,128)}, u32[]{:S(2)}) %copy-start.4) | copy-done | bytes 24600
  4.9 0.3 shard_map.103
  5.2 0.5 %collective-permute-start = (f32[1224,128]{1,0:T(8,128)S(1)}, f32[1224,128]{1,0:T(8,128)S(1)}, u32[]{:S(2)}, u32[]{:S(2)}) collective-permute-start(f32[1224,128]{1,0:T(8,128)S(1)} %get-tuple-element.22.a_ref), channel_id=1, source_target_pairs={{0,1},{1,0},{2,3},{3,2},{4,5},{5,4},{6,7},{7,6},{8,9},{9,8},{10,11... | collective-permute-start | bytes 1880072 | tf_op jit(solution)/shard_map/ppermute | solution.py:518
  5.8 0.1 collective-permute-start.1
  5.8 0.1 stack.39.flags
  5.9 1.7 %collective-permute-done.1.n_ref = f32[256,128]{1,0:T(8,128)S(1)} collective-permute-done((f32[256,128]{1,0:T(8,128)S(1)}, f32[256,128]{1,0:T(8,128)S(1)}, u32[]{:S(2)}, u32[]{:S(2)}) %collective-permute-start.1) | collective-permute-done | bytes 131104 | tf_op jit(solution)/shard_map/ppermute | solution.py:518
  7.6 0.0 collective-permute-done.b_ref
  7.6 0.8 %shard_map.104 = (f32[224,768]{1,0:T(8,128)S(1)}, f32[192,768]{1,0:T(8,128)S(1)}, f32[24,768]{1,0:T(8,128)S(1)}, f32[224,256]{1,0:T(8,128)S(1)}, f32[264,128]{1,0:T(8,128)S(1)}, /*index=5*/f32[128,128]{1,0:T(8,128)S(1)}) custom-call(s32[5]{0:T(128)S(1)} %stack.39.flags, f32[1224,128]{1,0:T(8,128)S(1)} %get-tuple-element.22.a_ref, ...), custom_call_target="tpu_custom_call" | custom-call | tf_op jit(solution)/shard_map/pallas_call | solution.py:28
  8.4 0.7 %collective-permute-start.3 = (f32[224,768]{1,0:T(8,128)S(1)}, f32[224,768]{1,0:T(8,128)S(1)}, u32[]{:S(2)}, u32[]{:S(2)}) collective-permute-start(f32[224,768]{1,0:T(8,128)S(1)} %get-tuple-element.24.z_ref), channel_id=1, source_target_pairs={{1,4},{3,6},{4,1},{5,8},{6,3},{7,10},{8,5},{9,12},{10,7},{11,14},{... | collective-permute-start | bytes 2064392 | tf_op jit(solution)/shard_map/ppermute | solution.py:518
  9.1 0.0 copy-start.5
  9.1 0.0 copy-start.6
  9.2 0.0 copy-start.7
  9.2 0.6 %copy-done.5 = f32[16]{0:T(128)S(1)} copy-done((f32[16]{0:T(128)S(1)}, f32[16]{0:T(128)}, u32[]{:S(2)}) %copy-start.5) | copy-done | bytes 88
  9.8 0.0 copy-done.6
  9.8 0.0 copy-done.7
  9.8 0.1 select_maximum_fusion
  9.9 2.9 %collective-permute-start.2 = (f32[264,128]{1,0:T(8,128)S(1)}, f32[264,128]{1,0:T(8,128)S(1)}, u32[]{:S(2)}, u32[]{:S(2)}) collective-permute-start(f32[264,128]{1,0:T(8,128)S(1)} %get-tuple-element.27), channel_id=1, source_target_pairs={{0,2},{1,3},{2,0},{3,1},{4,6},{5,7},{6,4},{7,5},{8,10},{9,11},{10,... | collective-permute-start | bytes 405512 | tf_op jit(solution)/shard_map/ppermute | solution.py:518
  12.8 0.7 %collective-permute-start.4 = (f32[128,128]{1,0:T(8,128)S(1)}, f32[128,128]{1,0:T(8,128)S(1)}, u32[]{:S(2)}, u32[]{:S(2)}) collective-permute-start(f32[128,128]{1,0:T(8,128)S(1)} %get-tuple-element.30), channel_id=1, source_target_pairs={{1,6},{3,4},{4,3},{5,10},{6,1},{7,8},{8,7},{9,14},{10,5},{11,12},{... | collective-permute-start | bytes 196616 | tf_op jit(solution)/shard_map/ppermute | solution.py:518
  13.4 2.3 %collective-permute-done.2.refs_0_ = f32[264,128]{1,0:T(8,128)S(1)} collective-permute-done((f32[264,128]{1,0:T(8,128)S(1)}, f32[264,128]{1,0:T(8,128)S(1)}, u32[]{:S(2)}, u32[]{:S(2)}) %collective-permute-start.2) | collective-permute-done | bytes 135200 | tf_op jit(solution)/shard_map/ppermute | solution.py:518
  15.8 4.1 %shard_map.105 = (f32[184,896]{1,0:T(8,128)S(1)}, f32[184,896]{1,0:T(8,128)S(1)}, f32[184,896]{1,0:T(8,128)S(1)}, f32[184,896]{1,0:T(8,128)S(1)}, f32[184,896]{1...) custom-call(s32[5]{0:T(128)S(1)} %stack.39.flags, ...), custom_call_target="tpu_custom_call" | custom-call | tf_op jit(solution)/shard_map/pallas_call | solution.py:28
  19.8 0.0 collective-permute-done.4.refs_1_
  19.9 0.0 collective-permute-done.3.zr_ref
  19.9 3.5 %shard_map.106 = (f32[32,384]{1,0:T(8,128)S(1)}, f32[24,384]{1,0:T(8,128)S(1)}, f32[96,256]{1,0:T(8,128)S(1)}) custom-call(s32[5]{0:T(128)S(1)} %stack.39.flags, f32[24,128]{1,0:T(8,128)S(1)} %broadcast_bitcast_fusion.tab, f32[224,768]{1,0:T(8,128)S(1)} %collective-permute-done.3.zr_ref, f32[224,256]{1,0:T(8,128)S(1)} %get-tuple-element.29.mw_ref, ...), custom_call_target="tpu_custom_call" | custom-call | tf_op jit(solution)/shard_map/pallas_call | solution.py:28
  23.4 4.0 %collective-permute-start.5 = (f32[32,384]{1,0:T(8,128)S(1)}, f32[32,384]{1,0:T(8,128)S(1)}, u32[]{:S(2)}, u32[]{:S(2)}) collective-permute-start(f32[32,384]{1,0:T(8,128)S(1)} %get-tuple-element.39), channel_id=1, source_target_pairs={{0,1},{1,0},{2,3},{3,2},{4,5},{5,4},{6,7},{7,6},{8,9},{9,8},{10,11... | collective-permute-start | bytes 147464 | tf_op jit(solution)/shard_map/ppermute | solution.py:518
  27.4 0.9 %collective-permute-done.5.xr_ref = f32[32,384]{1,0:T(8,128)S(1)} collective-permute-done((f32[32,384]{1,0:T(8,128)S(1)}, f32[32,384]{1,0:T(8,128)S(1)}, u32[]{:S(2)}, u32[]{:S(2)}) %collective-permute-start.5) | collective-permute-done | bytes 49184 | tf_op jit(solution)/shard_map/ppermute | solution.py:518
  28.3 1.4 %shard_map.107 = (f32[8,24,384]{2,1,0:T(8,128)}, f32[3,6,4,256]{3,2,1,0:T(4,128)}, f32[24,384]{1,0:T(8,128)}) custom-call(s32[5]{0:T(128)S(1)} %stack.39.flags, f32[184,896]{1,0:T(8,128)S(1)} %get-tuple-element.28.refs_7_.t_in, f32[24,384]{1,0:T(8,128)S(1)} %get-tuple-element.38.keep_ref, f32[32,384]{1,0:T(8,128)S(1)} %collective-permute-done.5.xr_ref, ...), custom_call_target="tpu_custom_call" | custom-call | tf_op jit(solution)/shard_map/pallas_call | solution.py:28
  (4 shorter events, 0.0 us)
Async XLA Ops:
  0.6 1.0 %copy-start = (f32[8,24,384]{2,1,0:T(8,128)S(1)}, f32[8,24,384]{2,1,0:T(8,128)}, u32[]{:S(2)}) copy-start(f32[8,24,384]{2,1,0:T(8,128)} %t_ref.1) | copy-start | bytes 884740
  1.6 1.0 %copy-start.1 = (s32[8,24,384]{2,1,0:T(8,128)S(1)}, s32[8,24,384]{2,1,0:T(8,128)}, u32[]{:S(2)}) copy-start(s32[8,24,384]{2,1,0:T(8,128)} %id_ref.1) | copy-start | bytes 884740
  2.6 0.9 %copy-start.2 = (f32[3,6,4,256]{3,2,1,0:T(4,128)S(1)}, f32[3,6,4,256]{3,2,1,0:T(4,128)}, u32[]{:S(2)}) copy-start(f32[3,6,4,256]{3,2,1,0:T(4,128)} %u_ref.1) | copy-start | bytes 221188
  3.4 0.8 %copy-start.3 = (f32[24,384]{1,0:T(8,128)S(1)}, f32[24,384]{1,0:T(8,128)}, u32[]{:S(2)}) copy-start(f32[24,384]{1,0:T(8,128)} %src_ref.1) | copy-start | bytes 110596
  4.2 0.7 %copy-start.4 = (s32[6,4,256]{2,1,0:T(4,128)S(1)}, s32[6,4,256]{2,1,0:T(4,128)}, u32[]{:S(2)}) copy-start(s32[6,4,256]{2,1,0:T(4,128)} %mat_ref.1) | copy-start | bytes 73732
  5.2 2.4 %collective-permute-start = (f32[1224,128]{1,0:T(8,128)S(1)}, f32[1224,128]{1,0:T(8,128)S(1)}, u32[]{:S(2)}, u32[]{:S(2)}) collective-permute-start(f32[1224,128]{1,0:T(8,128)S(1)} %get-tuple-element.22.a_ref), channel_id=1, source_target_pairs={{0,1},{1,0},{2,3},{3,2},{4,5},{5,4},{6,7},{7,6},{8,9},{9,8},{10,11... | collective-permute-start | bytes 1880072 | tf_op jit(solution)/shard_map/ppermute | solution.py:518
  5.8 1.9 %collective-permute-start.1 = (f32[256,128]{1,0:T(8,128)S(1)}, f32[256,128]{1,0:T(8,128)S(1)}, u32[]{:S(2)}, u32[]{:S(2)}) collective-permute-start(f32[256,128]{1,0:T(8,128)S(1)} %get-tuple-element.23.m_ref), channel_id=1, source_target_pairs={{0,1},{1,0},{2,3},{3,2},{4,5},{5,4},{6,7},{7,6},{8,9},{9,8},{10,11... | collective-permute-start | bytes 393224 | tf_op jit(solution)/shard_map/ppermute | solution.py:518
  8.4 11.4 %collective-permute-start.3 = (f32[224,768]{1,0:T(8,128)S(1)}, f32[224,768]{1,0:T(8,128)S(1)}, u32[]{:S(2)}, u32[]{:S(2)}) collective-permute-start(f32[224,768]{1,0:T(8,128)S(1)} %get-tuple-element.24.z_ref), channel_id=1, source_target_pairs={{1,4},{3,6},{4,1},{5,8},{6,3},{7,10},{8,5},{9,12},{10,7},{11,14},{... | collective-permute-start | bytes 2064392 | tf_op jit(solution)/shard_map/ppermute | solution.py:518
  9.1 0.7 %copy-start.5 = (f32[16]{0:T(128)S(1)}, f32[16]{0:T(128)}, u32[]{:S(2)}) copy-start(f32[16]{0:T(128)} %param.15) | copy-start | bytes 196
  9.1 0.7 %copy-start.6 = (f32[16]{0:T(128)S(1)}, f32[16]{0:T(128)}, u32[]{:S(2)}) copy-start(f32[16]{0:T(128)} %param.14) | copy-start | bytes 196
  9.2 0.7 %copy-start.7 = (f32[16]{0:T(128)S(1)}, f32[16]{0:T(128)}, u32[]{:S(2)}) copy-start(f32[16]{0:T(128)} %param.13) | copy-start | bytes 196
  9.9 5.9 %collective-permute-start.2 = (f32[264,128]{1,0:T(8,128)S(1)}, f32[264,128]{1,0:T(8,128)S(1)}, u32[]{:S(2)}, u32[]{:S(2)}) collective-permute-start(f32[264,128]{1,0:T(8,128)S(1)} %get-tuple-element.27), channel_id=1, source_target_pairs={{0,2},{1,3},{2,0},{3,1},{4,6},{5,7},{6,4},{7,5},{8,10},{9,11},{10,... | collective-permute-start | bytes 405512 | tf_op jit(solution)/shard_map/ppermute | solution.py:518
  12.8 7.1 %collective-permute-start.4 = (f32[128,128]{1,0:T(8,128)S(1)}, f32[128,128]{1,0:T(8,128)S(1)}, u32[]{:S(2)}, u32[]{:S(2)}) collective-permute-start(f32[128,128]{1,0:T(8,128)S(1)} %get-tuple-element.30), channel_id=1, source_target_pairs={{1,6},{3,4},{4,3},{5,10},{6,1},{7,8},{8,7},{9,14},{10,5},{11,12},{... | collective-permute-start | bytes 196616 | tf_op jit(solution)/shard_map/ppermute | solution.py:518
  23.4 4.9 %collective-permute-start.5 = (f32[32,384]{1,0:T(8,128)S(1)}, f32[32,384]{1,0:T(8,128)S(1)}, u32[]{:S(2)}, u32[]{:S(2)}) collective-permute-start(f32[32,384]{1,0:T(8,128)S(1)} %get-tuple-element.39), channel_id=1, source_target_pairs={{0,1},{1,0},{2,3},{3,2},{4,5},{5,4},{6,7},{7,6},{8,9},{9,8},{10,11... | collective-permute-start | bytes 147464 | tf_op jit(solution)/shard_map/ppermute | solution.py:518

commit v2 on v1

v2 whole, which is shorter than its diff:
```python
import functools

import jax
import jax.numpy as jnp
from jax import lax
from jax.experimental import pallas as pl
from jax.experimental.pallas import tpu as pltpu
from jax.sharding import PartitionSpec as P

DEPTH = 8
ML = 6
LANES = 128
HALO = 11
MHALO = 3

STIFF_DIAG = 12.0
THETA = 1.0
DELTA = 0.75
SIGMA = THETA / DELTA
RHO0 = 1.0 / SIGMA
RHO1 = 1.0 / (2.0 * SIGMA - RHO0)

VMEM = pl.BlockSpec(memory_space=pltpu.VMEM)
FRONT = 9
AHEAD = 5
STEP = 3
SPAN = 16
MSPAN = 8
ZMECH = 4 * ML
CORE = "lay"
UNROLL_STRAIN = 3


def call(kernel, outs, args, scratch=(), specs=None):
    return pl.pallas_call(
        kernel,
        out_shape=[jax.ShapeDtypeStruct(s, jnp.float32) for s in outs],
        in_specs=specs or [VMEM] * len(args),
        out_specs=[VMEM] * len(outs),
        scratch_shapes=[pltpu.VMEM(s, jnp.float32) if isinstance(s, tuple) else s for s in scratch],
        compiler_params=pltpu.CompilerParams(vmem_limit_bytes=16 * 1024 * 1024),
    )(*args)


def lane_iota(rows=8):
    return lax.broadcasted_iota(jnp.int32, (rows, LANES), 1)


def sub_iota(width):
    return lax.broadcasted_iota(jnp.int32, (8, width), 0)


def tile_lanes(t):
    return slice(LANES * t, LANES * (t + 1))


def tiles(x):
    return [x[:, tile_lanes(t)] for t in range(x.shape[1] // LANES)]


def table_of(ref, k):
    return jnp.broadcast_to(ref[k : k + 1, :], (8, LANES))


def gather_lanes(table, index):
    return jnp.take_along_axis(table, index, axis=1, mode="promise_in_bounds")


def lookup(table, code):
    return jnp.concatenate([gather_lanes(table, c.astype(jnp.int32)) for c in tiles(code)], axis=1)


def prev_lane(x):
    return pltpu.roll(x, 1, 1)


def next_lane(x):
    return pltpu.roll(x, x.shape[1] - 1, 1)


def prev_sub(x):
    return pltpu.roll(x, 1, 0)


def next_sub(x):
    return pltpu.roll(x, 7, 0)


def at8(i):
    return pl.ds(8 * i, 8) if isinstance(i, int) else pl.ds(pl.multiple_of(8 * i, 8), 8)


def row8(ref, i):
    return ref[at8(i), :]


def turned(core, last, g):
    return core * last + (1 - 2 * core) * g


def k_rows(in_ref, id_ref, a_ref, one_ref):
    other = 1 - lax.axis_index(CORE)
    rows = in_ref.shape[2]
    n_t = in_ref.shape[3] // LANES
    for t in range(n_t):
        at = 16 * rows * t
        for l in range(DEPTH):
            a_ref[pl.ds(at + l, rows, stride=16), :] = in_ref[0, l, :, tile_lanes(t)]
            a_ref[pl.ds(at + DEPTH + l, rows, stride=16), :] = (id_ref[l, :, tile_lanes(t)] + 1).astype(jnp.float32)
    for t in range(n_t):
        to = 17 * rows * t
        for g in range(rows):
            i = 16 * (rows * t + turned(other, rows - 1, g))
            one_ref[to + 16 * g : to + 16 * g + 16, :] = a_ref[pl.ds(pl.multiple_of(i, 16), 16), :]
        for b in range(rows // 8):
            k = to + 16 * rows + 8 * b
            one_ref[k : k + 8, :] = power_rows(in_ref, other, b, t)


def k_solid(u_ref, mat_ref, mg_ref, next_ref, m_ref):
    core = lax.axis_index(CORE)
    mrows = mat_ref.shape[1]
    m_t = mat_ref.shape[2] // LANES
    m_ref[...] = jnp.zeros(m_ref.shape, jnp.float32)
    for t in range(m_t):
        at = 32 * mrows * t
        for l in range(ML):
            for f in range(3):
                m_ref[pl.ds(at + 8 * f + l, mrows, stride=32), :] = u_ref[f, l, :, tile_lanes(t)]
            m_ref[pl.ds(at + 24 + l, mrows, stride=32), :] = (mat_ref[l, :, tile_lanes(t)] + 1).astype(jnp.float32)
        for g in range(mrows):
            i = 32 * (mrows * t + turned(core, mrows - 1, g))
            mg_ref[32 * g : 32 * g + 32, tile_lanes(t)] = m_ref[pl.ds(pl.multiple_of(i, 32), 32), :]
        for g in range(MHALO):
            i = 32 * (mrows * t + turned(core, mrows - 1, mrows - 1 - g))
            next_ref[32 * g : 32 * g + 32, tile_lanes(t)] = m_ref[pl.ds(pl.multiple_of(i, 32), 32), :]


def power_rows(in_ref, turn, b, t):
    rows = in_ref.shape[2]
    x = in_ref[1, 0, at8(turned(turn, rows // 8 - 1, b)), tile_lanes(t)]
    return jnp.take_along_axis(x, turned(turn, 7, sub_iota(LANES)), axis=0, mode="promise_in_bounds")


def k_edge(n_edges, p_ref, a_ref, got_ref, mg_ref, z_ref, *edge_refs):
    core = lax.axis_index(CORE)
    n_t = z_ref.shape[1] // LANES // 2
    rows = p_ref.shape[2]
    mcols = mg_ref.shape[1]
    n = 16 * HALO

    def build(first):
        for t in range(n_t):
            lanes = tile_lanes(t if first else n_t + t)
            for g in range(HALO):
                i = 16 * (rows * t + (g if first else rows - 1 - g))
                z_ref[16 * g : 16 * g + 16, lanes] = a_ref[i : i + 16, :]
            for b in range(2):
                z_ref[n + ZMECH + 8 * b : n + ZMECH + 8 * b + 8, lanes] = power_rows(p_ref, 0 if first else 1, b, t)
            lanes = tile_lanes(n_t + t if first else t)
            at = 17 * rows * t
            z_ref[0:n, lanes] = got_ref[at : at + n, :]
            at += 16 * rows
            z_ref[n + ZMECH : n + ZMECH + 16, lanes] = got_ref[at : at + 16, :]

    @pl.when(core == 0)
    def _():
        build(True)

    @pl.when(core != 0)
    def _():
        build(False)

    for g in range(MHALO):
        for f in range(4):
            at = n + ML * f
            z_ref[at : at + ML, mcols * g : mcols * (g + 1)] = mg_ref[32 * g + 8 * f : 32 * g + 8 * f + ML, :]
    for e in range(n_edges):
        side, lanes, mlanes = edge_lanes(n_edges, e, z_ref.shape[1], mcols)
        cells = [z_ref[8 * i : 8 * i + 8, lanes] for i in range(2 * HALO)]
        cells += [z_ref[n + ZMECH + 8 * b : n + ZMECH + 8 * b + 8, lanes] for b in range(2)]
        fields = [mg_ref[8 * i : 8 * i + 8, mlanes] for i in range(4 * MHALO)]
        pack_edge(edge_refs[e], side, cells, fields)


def edge_lanes(n_edges, e, wide, mcols):
    if n_edges == 1:
        side = 1 - lax.axis_index("col")
        lanes = pl.ds(pl.multiple_of(side * (wide - LANES), LANES), LANES)
        mlanes = pl.ds(pl.multiple_of(side * (mcols - LANES), LANES), LANES)
        return side, lanes, mlanes
    side = 1 - e
    return side, tile_lanes(side * (wide // LANES - 1)), tile_lanes(side * (mcols // LANES - 1))


def pack_edge(ref, side, cells, fields):
    lane = lane_iota()
    at = 0
    for blocks, span, keep in ((cells, SPAN, HALO), (fields, MSPAN, MHALO)):
        per = LANES // span
        for i in range(0, len(blocks), per):
            acc = jnp.zeros((8, LANES), jnp.float32)
            for k, x in enumerate(blocks[i : i + per]):
                acc = jnp.where(lane // span == k, pltpu.roll(x, span * k + side * keep, 1), acc)
            ref[at : at + 8, :] = acc
            at += 8


def edge_size(cells, fields):
    return 8 * (-(-cells * SPAN // LANES) - (-fields * MSPAN // LANES))


def k_chip(n_edges, rows, p_ref, a_ref, got_ref, mg_ref, next_ref, z_ref, w_ref, src_ref, mw_ref, *edge_refs):
    core = lax.axis_index(CORE)
    wide = w_ref.shape[1]
    n_t = wide // LANES // 2
    mcols = mw_ref.shape[1]
    mrows = mg_ref.shape[0] // 32
    n = 16 * HALO
    w_ref[0:n, :] = z_ref[0:n, :]
    src_ref[0:16, :] = z_ref[n + ZMECH : n + ZMECH + 16, :]
    rest = 16 * (rows - HALO)

    def build(first):
        for t in range(n_t):
            lanes = tile_lanes(t if first else n_t + t)
            for g in range(HALO, rows):
                i = 16 * (rows * t + (g if first else rows - 1 - g))
                w_ref[16 * g : 16 * g + 16, lanes] = a_ref[i : i + 16, :]
            for b in range(2, rows // 8):
                src_ref[8 * b : 8 * b + 8, lanes] = power_rows(p_ref, 0 if first else 1, b, t)
            lanes = tile_lanes(n_t + t if first else t)
            at = 17 * rows * t
            w_ref[n : n + rest, lanes] = got_ref[at + n : at + n + rest, :]
            at += 16 * rows
            src_ref[16:rows, lanes] = got_ref[at + 16 : at + rows, :]

    @pl.when(core == 0)
    def _():
        build(True)

    @pl.when(core != 0)
    def _():
        build(False)

    mw_ref[0 : 32 * mrows, :] = mg_ref[...]
    mw_ref[32 * mrows : 32 * (mrows + MHALO), :] = next_ref[...]

    for e in range(n_edges):
        side, lanes, mlanes = edge_lanes(n_edges, e, wide, mcols)
        cells = [w_ref[8 * i : 8 * i + 8, lanes] for i in range(2 * (rows - 1))]
        cells += [src_ref[8 * b : 8 * b + 8, lanes] for b in range(rows // 8)]
        fields = [mw_ref[8 * i : 8 * i + 8, mlanes] for i in range(4 * (mrows + MHALO))]
        pack_edge(edge_refs[e], side, cells, fields)


class Sides:
    def __init__(self, n_col, count, from_left, from_right):
        self.left = from_left
        self.right = from_right
        self.count = count
        lane = lane_iota()
        col = lax.axis_index("col")
        self.masks = {
            w: ((lane < w) & (col < n_col - 1), (lane >= LANES - w) & (col > 0)) for w in (HALO, MHALO)
        }
        self.only = self.left is self.right
        self.side = col

    def take(self, v, k, span, width):
        right_mask, left_mask = self.masks[width]
        x = row8(self.right, v)
        if self.only:
            x = pltpu.roll(x, LANES - span * k - self.side * width, 1)
            return jnp.where(right_mask | left_mask, x, 0.0)
        r = pltpu.roll(x, (LANES - span * k) % LANES, 1)
        l = pltpu.roll(row8(self.left, v), LANES - span * k - width, 1)
        return jnp.where(right_mask, r, jnp.where(left_mask, l, 0.0))

    def tile(self, i):
        per = LANES // SPAN
        return self.take(i // per, i % per, SPAN, HALO)

    def field(self, i):
        per = LANES // MSPAN
        first = -(-self.count * SPAN // LANES)
        return self.take(first + i // per, i % per, MSPAN, MHALO)


def spread_power(ref, n, blocks):
    ref[...] = jnp.zeros(ref.shape, jnp.float32)
    count = ref.shape[0] // (n * 8)
    for first, x in blocks:
        for t, piece in enumerate(tiles(x)):
            ref[pl.ds(8 * (n * t + first), piece.shape[0], stride=8), :] = piece
    return count


def power_row(ref, n, i):
    count = ref.shape[0] // (n * 8)
    return jnp.concatenate([row8(ref, n * t + i) for t in range(count)], axis=1)


def conduct_sum(ref, i):
    x = row8(ref, i)
    sub = sub_iota(x.shape[1])
    total = row8(ref, i - 1) + row8(ref, i + 1) + prev_lane(x) + next_lane(x)
    total = total + jnp.where(sub < DEPTH - 1, next_sub(x), 0.0)
    return total + jnp.where(sub > 0, prev_sub(x), 0.0)


def sink(width):
    return jnp.where(sub_iota(width) == DEPTH - 1, 2.0, 0.2).astype(jnp.float32)


def restrict_columns(x):
    width = x.shape[1]
    x = x + pltpu.roll(x, width - 1, 1) + pltpu.roll(x, width - 2, 1)
    pieces = tiles(x)
    lane = lane_iota()
    out = []
    for j in range((len(pieces) - 1) // 3):
        got = None
        for t in range(3):
            g = gather_lanes(pieces[3 * j + t], (3 * lane) & (LANES - 1))
            got = g if got is None else jnp.where((3 * lane) >= LANES * t, g, got)
        out.append(got)
    first = LANES - MHALO
    index = jnp.where(lane < MHALO, 3 * lane, jnp.where(lane >= first, LANES - 9 + 3 * (lane - first), 64))
    out.append(gather_lanes(pieces[-1], index))
    y = jnp.concatenate(out, axis=1)
    y = jnp.where(sub_iota(y.shape[1]) < 3, y, next_sub(y))
    return y * (1.0 / 9.0)


def first_sweep(s_ref, q0_ref, i, power, h):
    s = row8(s_ref, i)
    inv = 1.0 / (h + s * conduct_sum(s_ref, i))
    return inv, s * ((power + s * conduct_sum(q0_ref, i)) * inv)


def second_sweep(s_ref, q1_ref, di_ref, i, power):
    return (power + row8(s_ref, i) * conduct_sum(q1_ref, i)) * row8(di_ref, i)


def k_inner(n_edges, n_col, rows, tab, w_ref, src_ref, *refs):
    sides = Sides(n_col, 2 * (rows - 1) + rows // 8, refs[0], refs[n_edges - 1])
    s_ref, al_ref, q0_ref, q1_ref, di_ref, t_ref, ea_ref, strain_ref, pw_ref = refs[n_edges:]
    own = rows - 1
    width = src_ref.shape[1] + LANES
    t_s = jnp.sqrt(table_of(tab, 0))
    t_al = table_of(tab, 1)
    side_power = jnp.concatenate([sides.tile(2 * own + k) for k in range(rows // 8)], axis=0)
    n_p = s_ref.shape[0] // 8
    spread_power(pw_ref, n_p, [(FRONT, jnp.concatenate([src_ref[...], side_power], axis=1))])
    h = sink(width)

    for i in range(0, own + 2 * STEP + 2, STEP):
        later = []
        for g in range(i, min(i + STEP, own)):
            temp = jnp.concatenate([w_ref[16 * g : 16 * g + 8, :], sides.tile(2 * g)], axis=1)
            code = jnp.concatenate([w_ref[16 * g + 8 : 16 * g + 16, :], sides.tile(2 * g + 1)], axis=1)
            s = lookup(t_s, code)
            later += [(s_ref, FRONT + g, s), (q0_ref, FRONT + g, s * temp)]
            later += [(al_ref, FRONT + g, lookup(t_al, code))]
        for g in range(max(1, i - STEP - 1), min(i - 1, own - 1)):
            r = FRONT + g
            inv, q1 = first_sweep(s_ref, q0_ref, r, power_row(pw_ref, n_p, r), h)
            later += [(di_ref, r, inv), (q1_ref, r, q1)]
        for g in range(max(2, i - 2 * STEP - 2), min(i - STEP - 2, own - 2)):
            r = FRONT + g
            t2 = second_sweep(s_ref, q1_ref, di_ref, r, power_row(pw_ref, n_p, r))
            later += [(t_ref, r, t2), (ea_ref, r, row8(al_ref, r) * t2)]
        for ref, r, x in later:
            ref[at8(r), :] = x

    def strain(m, carry):
        i = FRONT + 3 * m
        x = row8(ea_ref, i) + row8(ea_ref, i + 1) + row8(ea_ref, i + 2)
        strain_ref[at8(m), :] = restrict_columns(x)
        return carry

    lax.fori_loop(1, (own - 2) // 3, strain, 0, unroll=UNROLL_STRAIN)


def couple_sum(rows3):
    near = [[None] * 3 for _ in range(3)]
    for j in range(3):
        below, mid, above = rows3[j]
        near[0][j] = next_sub(mid) + prev_sub(mid)
        near[1][j] = above + below
        near[2][j] = next_lane(mid) + prev_lane(mid)
    out = []
    for i in range(3):
        j, k = [x for x in range(3) if x != i]
        main = near[i][i] + 0.5 * (near[j][i] + near[k][i])
        side = (near[i][j] + near[j][j]) + (near[i][k] + near[k][k])
        out.append(main + 0.25 * side)
    return out


def mech_tables(tab):
    t_mod = table_of(tab, 2)
    t_m = jnp.sqrt(t_mod)
    return t_m, jnp.where(t_mod > 0.0, 1.0 / jnp.where(t_mod > 0.0, t_m, 1.0), 0.0), t_mod


def k_mech(n_edges, n_col, rows, tab, mw_ref, *refs):
    sides = Sides(n_col, 2 * (rows - 1) + rows // 8, refs[0], refs[n_edges - 1])
    mi_ref, mod_ref = refs[n_edges : n_edges + 2]
    uu_refs = refs[n_edges + 2 : n_edges + 5]
    pre_refs = refs[n_edges + 5 : n_edges + 8]
    t_m, t_mi, t_mod = mech_tables(tab)
    count = mw_ref.shape[0] // 32
    for m in range(count):
        fields = []
        for f in range(4):
            side = sides.field(4 * m + f)
            fields.append(jnp.concatenate([mw_ref[32 * m + 8 * f : 32 * m + 8 * f + 8, :], side], axis=1))
        root = lookup(t_m, fields[3])
        mi_ref[at8(m), :] = lookup(t_mi, fields[3])
        mod_ref[at8(m), :] = lookup(t_mod, fields[3])
        for f in range(3):
            uu_refs[f][at8(m), :] = root * fields[f]
    for m in range(1, count - 1):
        near = couple_sum([[row8(r, m - 1), row8(r, m), row8(r, m + 1)] for r in uu_refs])
        for d in range(3):
            pre_refs[d][at8(m), :] = near[d] * (1.0 / STIFF_DIAG) - row8(uu_refs[d], m)


def k_outer(n_edges, n_col, rows, tab, zr_ref, *refs):
    sides = Sides(n_col, 2 * (rows - 1) + rows // 8, refs[0], refs[n_edges - 1])
    corners = Sides(n_col, 2 * HALO + 2, refs[n_edges], refs[2 * n_edges - 1])
    rest = refs[2 * n_edges :]
    s_in, al_in, q0_in, q1_in, di_in, t_in, ea_in, strain_in, src_ref = rest[:9]
    mi_in, mod_in = rest[9:11]
    uu_in, pre_in = rest[11:14], rest[14:17]
    x_ref, keep_ref, u_ref = rest[17:20]
    s_ref, q0_ref, q1_ref, di_ref, al_ref, ea_ref, t_keep, pw_ref = rest[20:28]
    st_ref, mi_ref, mod_ref, sf_ref = rest[28:32]
    uu_refs, p_refs, d_refs = rest[32:35], rest[35:38], rest[38:41]
    own = rows - 1
    wide = zr_ref.shape[1]
    half = wide // 2
    width = wide + LANES
    t_s = jnp.sqrt(table_of(tab, 0))
    t_al = table_of(tab, 1)
    zsrc = 16 * HALO + ZMECH
    for g in range(3):
        k = AHEAD - 1 - g
        for dst, src in ((s_ref, s_in), (al_ref, al_in), (q0_ref, q0_in)):
            dst[at8(k), :] = row8(src, FRONT + g)
    ea_ref[at8(AHEAD - 3), :] = row8(ea_in, FRONT + 2)
    for g in (1, 2):
        q1_ref[at8(AHEAD - 1 - g), :] = row8(q1_in, FRONT + g)
    di_ref[at8(AHEAD - 2), :] = row8(di_in, FRONT + 1)
    n_p = s_ref.shape[0] // 8
    near = jnp.concatenate([src_ref[0:8, :], sides.tile(2 * own)], axis=1)
    far = jnp.concatenate([corners.tile(2 * HALO), corners.tile(2 * HALO + 1)], axis=0)
    far = jnp.concatenate([zr_ref[zsrc : zsrc + 16, :], far], axis=1)
    spread_power(
        pw_ref,
        n_p,
        [(AHEAD - 1, near[0:1, :]), (AHEAD - 2, near[1:2, :]), (AHEAD, far[0:8, :]), (AHEAD + 8, far[8:HALO, :])],
    )
    h = sink(width)

    for i in range(0, HALO + 2 * STEP + 1, STEP):
        later = []
        for j in range(i, min(i + STEP, HALO)):
            temp = jnp.concatenate([zr_ref[16 * j : 16 * j + 8, :], corners.tile(2 * j)], axis=1)
            code = jnp.concatenate([zr_ref[16 * j + 8 : 16 * j + 16, :], corners.tile(2 * j + 1)], axis=1)
            s = lookup(t_s, code)
            later += [(s_ref, AHEAD + j, s), (q0_ref, AHEAD + j, s * temp)]
            if j < HALO - 2:
                later += [(al_ref, AHEAD + j, lookup(t_al, code))]
        for j in range(max(-1, i - STEP - 1), min(i - 1, HALO - 1)):
            r = AHEAD + j
            inv, q1 = first_sweep(s_ref, q0_ref, r, power_row(pw_ref, n_p, r), h)
            later += [(di_ref, r, inv), (q1_ref, r, q1)]
        for j in range(max(-2, i - 2 * STEP - 2), min(i - STEP - 2, HALO - 2)):
            r = AHEAD + j
            t2 = second_sweep(s_ref, q1_ref, di_ref, r, power_row(pw_ref, n_p, r))
            later += [(t_keep, r, t2), (ea_ref, r, row8(al_ref, r) * t2)]
        for ref, r, x in later:
            ref[at8(r), :] = x

    core = lax.axis_index(CORE)

    def other_half(x):
        return jnp.where(core == 0, x[:, half:wide], x[:, 0:half])

    def own_half(x):
        return jnp.where(core == 0, x[:, 0:half], x[:, half:wide])

    for g in range(2):
        t2 = row8(t_keep, AHEAD - 1 - g)
        keep_ref[8 * g : 8 * g + 8, :] = own_half(t2)
        x_ref[8 * g : 8 * g + 8, :] = other_half(t2)
    x_ref[16:24, :] = other_half(row8(t_in, FRONT + 2))

    count = mod_in.shape[0] // 8
    mrows = count - MHALO
    mwidth = mod_in.shape[1]
    mcols = mwidth - LANES
    n_m = count + MHALO
    for m in range(MHALO + 1):
        i = AHEAD - 3 + 3 * m
        x = row8(ea_ref, i) + row8(ea_ref, i + 1) + row8(ea_ref, i + 2)
        st_ref[at8(MHALO - m), :] = restrict_columns(x)
    for m in range(1, count):
        st_ref[at8(MHALO + m), :] = row8(strain_in, m)
    t_m, t_mi, t_mod = mech_tables(tab)
    for i in range(MHALO):
        j = MHALO - 1 - i
        fields = []
        for f in range(4):
            body = zr_ref[16 * HALO + ML * f : 16 * HALO + ML * f + 8, mcols * j : mcols * (j + 1)]
            body = jnp.where(sub_iota(mcols) < ML, body, 0.0)
            side = corners.field(4 * j + f)
            fields.append(jnp.concatenate([body, side], axis=1))
        root = lookup(t_m, fields[3])
        mi_ref[at8(i), :] = lookup(t_mi, fields[3])
        mod_ref[at8(i), :] = lookup(t_mod, fields[3])
        for f in range(3):
            uu_refs[f][at8(i), :] = root * fields[f]
    for ref, src in zip((mi_ref, mod_ref, *uu_refs), (mi_in, mod_in, *uu_in)):
        ref[8 * MHALO : 8 * n_m, :] = src[...]
    for i in range(n_m):
        sf_ref[at8(i), :] = row8(mod_ref, i) * row8(st_ref, i)
    sign = jnp.where(core == 0, 0.5, -0.5).astype(jnp.float32)
    for i in range(1, n_m - 1):
        load = row8(sf_ref, i)
        force = [
            0.5 * (next_sub(load) - prev_sub(load)),
            sign * (row8(sf_ref, i + 1) - row8(sf_ref, i - 1)),
            0.5 * (next_lane(load) - prev_lane(load)),
        ]
        inv = row8(mi_ref, i)
        inside = inv > 0.0
        if i <= MHALO:
            near = couple_sum([[row8(r, i - 1), row8(r, i), row8(r, i + 1)] for r in uu_refs])
            pre = [near[d] * (1.0 / STIFF_DIAG) - row8(uu_refs[d], i) for d in range(3)]
        else:
            pre = [row8(r, i - MHALO) for r in pre_in]
        inv = inv * (1.0 / STIFF_DIAG)
        for d in range(3):
            p_refs[d][at8(i), :] = jnp.where(inside, force[d] * inv + pre[d], 0.0)
    c_near = 2.0 * RHO1 / DELTA / STIFF_DIAG
    c_self = 1.0 + RHO1 * RHO0
    for i in range(2, n_m - 2):
        near = couple_sum([[row8(r, i - 1), row8(r, i), row8(r, i + 1)] for r in p_refs])
        inv = row8(mi_ref, i)
        for d in range(3):
            moved = row8(uu_refs[d], i) + c_self * row8(p_refs[d], i) + c_near * near[d]
            d_refs[d][at8(i), :] = moved * inv
    sub = sub_iota(mwidth)
    weight = jnp.where(sub < ML, (ML - sub).astype(jnp.float32) * (1.0 / (ML * (ML + 1) / 2.0)), 0.0)
    x_ref[24:32, :] = jnp.zeros((8, x_ref.shape[1]), jnp.float32)
    for g in range(mrows):
        i = MHALO + g
        u0, u2 = row8(d_refs[0], i), row8(d_refs[2], i)
        div = 0.5 * (next_sub(u0) - prev_sub(u0)) + 0.5 * (next_lane(u2) - prev_lane(u2))
        div = div + sign * (row8(d_refs[1], i + 1) - row8(d_refs[1], i - 1))
        stress = row8(mod_ref, i) * (div - 3.0 * row8(st_ref, i))
        die = jnp.sum(weight * stress, axis=0, keepdims=True)
        first, second = die[:, 0:LANES], die[:, LANES : 2 * LANES]
        keep_ref[16 + g : 17 + g, 0:LANES] = jnp.where(core == 0, first, second)
        x_ref[24 + g : 25 + g, 0:LANES] = jnp.where(core == 0, second, first)
        for d in range(3):
            u_ref[8 * (mrows * d + g) : 8 * (mrows * d + g) + 8, :] = row8(d_refs[d], i)[:, 0:mcols]


def k_out(rows, mrows, t_in, keep_ref, xr_ref, u_in, t_out, u_out, slow_ref, buf, die, wide_die, ubuf):
    half = slow_ref.shape[1]
    mcols = u_in.shape[1]
    core = lax.axis_index(CORE)

    def put(ref, at, x):
        count = ref.shape[0] * LANES // x.shape[1]
        for t, piece in enumerate(tiles(x)):
            ref[count * t + at : count * t + at + piece.shape[0], :] = piece

    def build(rev):
        lo = half if rev else 0
        for g in range(rows):
            i = rows - 1 - g if rev else g
            if g < 2:
                x = keep_ref[8 * g : 8 * g + 8, :]
            elif g < rows - 3:
                x = t_in[8 * (FRONT + g) : 8 * (FRONT + g) + 8, lo : lo + half]
            else:
                k = rows - 1 - g
                x = xr_ref[8 * k : 8 * k + 8, :]
            put(buf, 8 * i, x)
        for g in range(mrows):
            mine = 2 * mrows - 1 - g if rev else g
            theirs = g if rev else 2 * mrows - 1 - g
            die[mine : mine + 1, :] = keep_ref[16 + g : 17 + g, 0:LANES]
            die[theirs : theirs + 1, :] = xr_ref[24 + g : 25 + g, 0:LANES]
            for d in range(3):
                i = mrows - 1 - g if rev else g
                put(ubuf, 8 * (mrows * d + i), row8(u_in, mrows * d + g))

    @pl.when(core == 0)
    def _():
        build(False)

    @pl.when(core != 0)
    def _():
        build(True)

    for t in range(half // LANES):
        at = 8 * rows * t
        for l in range(DEPTH):
            t_out[l, :, tile_lanes(t)] = buf[pl.ds(at + l, rows, stride=8), :]
    for t in range(mcols // LANES):
        for d in range(3):
            for l in range(ML):
                u_out[d, l, :, tile_lanes(t)] = ubuf[pl.ds(8 * mrows * (3 * t + d) + l, mrows, stride=8), :]
    lane = lane_iota(2 * mrows)
    for t in range(half // LANES):
        x = gather_lanes(die[...], (lane + LANES * t) // 3)
        for b in range(3):
            wide_die[pl.ds(b, 2 * mrows, stride=3), :] = x
        slow = 1.0 + 0.2 * buf[pl.ds(8 * rows * t, rows, stride=8), :] + 0.5 * wide_die[...]
        slow_ref[:, tile_lanes(t)] = slow


def pairs(dims, sends):
    index = {}
    for r in range(dims[0]):
        for c in range(dims[1]):
            for a in range(dims[2]):
                index[(r, c, a)] = (r * dims[1] + c) * dims[2] + a
    out = []
    for source in index:
        target = sends(*source)
        if target in index:
            out.append((index[source], index[target]))
    return out


def per_device(temp, ids, power, mat, offset, heat_table, growth_table, modulus_table):
    axes = ("row", "col", "lay")
    dims = tuple(lax.axis_size(x) for x in axes)
    n_col = dims[1]
    _, rows, half = temp.shape
    _, _, mrows, mcols = offset.shape
    n_edges = 1 if n_col == 2 else 2
    n_t = half // LANES
    m_t = mcols // LANES

    def send(x, sends):
        return lax.ppermute(x, axes, pairs(dims, sends))

    def swap(r, c, a):
        return (r, c, 1 - a)

    def along(r, c, a):
        return (r + 1, c, 0) if a == 1 else (r - 1, c, 1)

    kind = lax.broadcasted_iota(jnp.int32, (2, *temp.shape), 0)
    packed = jnp.where(kind == 0, temp[None], power[None, None])
    tab = jnp.stack([heat_table, growth_table, modulus_table])
    tab = jnp.pad(tab, ((0, 0), (1, LANES - 1 - tab.shape[1])))
    cells, one = call(k_rows, [(16 * rows * n_t, LANES), (17 * rows * n_t, LANES)], [packed, ids])
    got = send(one, swap)
    mg, ahead = call(
        k_solid,
        [(32 * mrows, mcols), (32 * MHALO, mcols)],
        [offset, mat],
        scratch=[(32 * mrows * m_t, LANES)],
    )
    ahead = send(ahead, swap)
    wide = 2 * half
    own = rows - 1
    z, *edges = call(
        functools.partial(k_edge, n_edges),
        [(16 * HALO + ZMECH + 16, wide)] + [(edge_size(2 * HALO + 2, 4 * MHALO), LANES)] * n_edges,
        [packed, cells, got, mg],
    )
    zr = send(z, along)
    if n_edges == 1:
        corners = [send(edges[0], lambda r, c, a: along(r, 1 - c, a))]
    else:
        corners = [
            send(edges[0], lambda r, c, a: along(r, c + 1, a)),
            send(edges[1], lambda r, c, a: along(r, c - 1, a)),
        ]
    w, src, mw, *edges = call(
        functools.partial(k_chip, n_edges, rows),
        [(16 * rows, wide), (rows, wide), (32 * (mrows + MHALO), mcols)]
        + [(edge_size(2 * own + rows // 8, 4 * (mrows + MHALO)), LANES)] * n_edges,
        [packed, cells, got, mg, ahead, z],
    )
    if n_edges == 1:
        sides = [send(edges[0], lambda r, c, a: (r, 1 - c, a))]
    else:
        sides = [send(edges[0], lambda r, c, a: (r, c + 1, a)), send(edges[1], lambda r, c, a: (r, c - 1, a))]
    width = wide + LANES
    mwidth = mcols + LANES
    n_w = 8 * (rows + FRONT + 4)
    inner = call(
        functools.partial(k_inner, n_edges, n_col, rows),
        [(n_w, width)] * 7 + [(8 * (mrows + MHALO), mwidth)],
        [tab, w, src] + sides,
        scratch=[(n_w * (width // LANES), LANES)],
    )
    t2 = inner[5]
    solid = call(
        functools.partial(k_mech, n_edges, n_col, rows), [(8 * (mrows + MHALO), mwidth)] * 8, [tab, mw] + sides
    )
    n_h = 8 * (AHEAD + HALO + 5)
    n_m = 8 * (mrows + 2 * MHALO)
    x, keep, u = call(
        functools.partial(k_outer, n_edges, n_col, rows),
        [(32, half), (24, half), (24 * mrows, mcols)],
        [tab, zr] + sides + corners + list(inner) + [src] + list(solid),
        scratch=[(n_h, width)] * 7 + [(n_h * (width // LANES), LANES)] + [(n_m, mwidth)] * 13,
    )
    xr = send(x, swap)
    t_out, u_out, slow = call(
        functools.partial(k_out, rows, mrows),
        [temp.shape, offset.shape, power.shape],
        [t2, keep, xr, u],
        scratch=[
            (8 * rows * n_t, LANES),
            (2 * mrows, LANES),
            (rows, LANES),
            (24 * mrows * m_t, LANES),
        ],
    )
    return t_out, u_out, slow


def solution(mesh):
    placed = (
        P("grp", "row", ("col", "lay")),
        P("grp", "row", ("col", "lay")),
        P(("grp", "row"), ("col", "lay")),
        P("grp", ("row", "lay"), "col"),
        P(None, "grp", ("row", "lay"), "col"),
        P(),
        P(),
        P(),
    )
    return jax.shard_map(
        per_device,
        mesh=mesh,
        in_specs=placed,
        out_specs=(
            P("grp", "row", ("col", "lay")),
            P(None, "grp", ("row", "lay"), "col"),
            P(("grp", "row"), ("col", "lay")),
        ),
        check_vma=False,
    )
```

time: 30.1 us -> 24.1 us (0.80)
  local copies, waits for them, and re-layouts: 5.06 us -> 0.03 us
  Pallas kernels: 10 us -> 7.72 us
  other arithmetic: 0.08 us -> 1.22 us
    unnamed x16 -> x12, local copies, waits for them, and re-layouts: 4.97 us -> 0.03 us
    pallas_call x5 -> x8, Pallas kernels: 10 us -> 7.72 us  [call(): pl.pallas_call(kernel, out_shape=[jax.ShapeDtypeStruct(s, jnp.float32) fo...]
    select_n x0 -> x1, other arithmetic: none -> 1.14 us  [per_device(): packed = jnp.where(kind == 0, temp[None], power[None, None])]
  transfers between devices with their start and end apart: 6 -> 6, of which waited for: 3 -> 4; matrix products, arithmetic and copies ran while one was open for 1% -> 0% of each run, Pallas kernels for 14% -> 17%
where the time goes in v2:
time: 24.1 us; the launch traced here: 23.9 us
  starting transfers between devices  9.05 us (38%)
  Pallas kernels  7.72 us (32%)
  waiting for transfers between devices  5.12 us (21%)
  other arithmetic  1.22 us (5%)
  between operations  0.81 us (3%)
    ppermute x6, starting transfers between devices, send(): return lax.ppermute(x, axes, pairs(dims, sends))  9.05 us
    pallas_call x8, Pallas kernels, call(): pl.pallas_call(kernel, out_shape=[jax.ShapeDtypeStruct(s, jnp.float32) fo...  7.72 us
    ppermute x6, waiting for transfers between devices, send(): return lax.ppermute(x, axes, pairs(dims, sends))  5.12 us
    select_n x1, other arithmetic, per_device(): packed = jnp.where(kind == 0, temp[None], power[None, None])  1.14 us
  transfers between devices with their start and end apart: 6, of which 4 were waited for; matrix products, arithmetic and copies ran while one was open for 0% of the time, Pallas kernels for 17%

profile of v2, /device:TPU:0, one launch (start us, length us, event | category | flops | bytes accessed | tf_op | source)
XLA Modules:
  0.0 23.9 jit_solution(8633927422506291985)
XLA Ops:
  0.6 0.0 copy-start
  0.6 0.0 copy-start.2
  0.7 0.0 copy-start.1
  0.7 1.1 %broadcast_select_fusion.in_ref.p_ref = f32[2,8,24,384]{3,2,1,0:T(8,128)S(1)} fusion(f32[24,384]{1,0:T(8,128)} %param.10, f32[8,24,384]{2,1,0:T(8,128)} %param.8, pred[2]{0:T(512)(128)(4,1)S(1)} %iota_compare_fusion.2), kind=kLoop, calls=%fused_computation | loop fusion | flops 147456 | bytes 921602 | tf_op jit(solution)/shard_map/jit(_where)/select_n | solution.py:664
  1.8 0.0 copy-done
  1.8 0.3 %shard_map.103 = (f32[1152,128]{1,0:T(8,128)S(1)}, f32[1224,128]{1,0:T(8,128)S(1)}) custom-call(f32[2,8,24,384]{3,2,1,0:T(8,128)S(1)} %broadcast_select_fusion.in_ref.p_ref, s32[8,24,384]{2,1,0:T(8,128)S(1)} %copy-done), custom_call_target="tpu_custom_call" | custom-call | tf_op jit(solution)/shard_map/pallas_call | solution.py:35
  2.1 0.5 %collective-permute-start = (f32[1224,128]{1,0:T(8,128)S(1)}, f32[1224,128]{1,0:T(8,128)S(1)}, u32[]{:S(2)}, u32[]{:S(2)}) collective-permute-start(f32[1224,128]{1,0:T(8,128)S(1)} %get-tuple-element.33), channel_id=1, source_target_pairs={{0,1},{1,0},{2,3},{3,2},{4,5},{5,4},{6,7},{7,6},{8,9},{9,8},{10,11... | collective-permute-start | bytes 1880072 | tf_op jit(solution)/shard_map/ppermute | solution.py:655
  2.6 0.0 copy-done.2
  2.6 0.0 copy-done.1
  2.6 0.1 shard_map.104
  2.7 1.6 %collective-permute-done.got_ref = f32[1224,128]{1,0:T(8,128)S(1)} collective-permute-done((f32[1224,128]{1,0:T(8,128)S(1)}, f32[1224,128]{1,0:T(8,128)S(1)}, u32[]{:S(2)}, u32[]{:S(2)}) %collective-permute-start) | collective-permute-done | bytes 626720 | tf_op jit(solution)/shard_map/ppermute | solution.py:655
  4.3 0.1 shard_map.105
  4.4 0.7 %collective-permute-start.3 = (f32[216,768]{1,0:T(8,128)S(1)}, f32[216,768]{1,0:T(8,128)S(1)}, u32[]{:S(2)}, u32[]{:S(2)}) collective-permute-start(f32[216,768]{1,0:T(8,128)S(1)} %get-tuple-element.36.z_ref), channel_id=1, source_target_pairs={{1,4},{3,6},{4,1},{5,8},{6,3},{7,10},{8,5},{9,12},{10,7},{11,14},{... | collective-permute-start | bytes 1990664 | tf_op jit(solution)/shard_map/ppermute | solution.py:655
  5.2 0.0 copy-start.3
  5.2 0.0 copy-start.4
  5.2 0.0 copy-start.5
  5.2 4.3 %collective-permute-start.1 = (f32[96,256]{1,0:T(8,128)S(1)}, f32[96,256]{1,0:T(8,128)S(1)}, u32[]{:S(2)}, u32[]{:S(2)}) collective-permute-start(f32[96,256]{1,0:T(8,128)S(1)} %get-tuple-element.35), channel_id=1, source_target_pairs={{0,1},{1,0},{2,3},{3,2},{4,5},{5,4},{6,7},{7,6},{8,9},{9,8},{10,11... | collective-permute-start | bytes 294920 | tf_op jit(solution)/shard_map/ppermute | solution.py:655
  9.5 0.9 %collective-permute-done.1.next_ref = f32[96,256]{1,0:T(8,128)S(1)} collective-permute-done((f32[96,256]{1,0:T(8,128)S(1)}, f32[96,256]{1,0:T(8,128)S(1)}, u32[]{:S(2)}, u32[]{:S(2)}) %collective-permute-start.1) | collective-permute-done | bytes 98336 | tf_op jit(solution)/shard_map/ppermute | solution.py:655
  10.5 0.2 %shard_map.106 = (f32[384,768]{1,0:T(8,128)S(1)}, f32[24,768]{1,0:T(8,128)S(1)}, f32[224,256]{1,0:T(8,128)S(1)}, f32[72,128]{1,0:T(8,128)S(1)}) custom-call(f32[2,8,24,384]{3,2,1,0:T(8,128)S(1)} %broadcast_select_fusion.in_ref.p_ref, f32[1152,128]{1,0:T(8,128)S(1)} %get-tuple-element.32.a_ref, f32[1224,128]{1,0:T(8,128)S(1)} %collective-permute-done.got_ref, ...), custom_call_target="tpu_custom_call" | custom-call | tf_op jit(solution)/shard_map/pallas_call | solution.py:35
  10.7 1.6 %collective-permute-start.2 = (f32[72,128]{1,0:T(8,128)S(1)}, f32[72,128]{1,0:T(8,128)S(1)}, u32[]{:S(2)}, u32[]{:S(2)}) collective-permute-start(f32[72,128]{1,0:T(8,128)S(1)} %get-tuple-element.39), channel_id=1, source_target_pairs={{0,2},{1,3},{2,0},{3,1},{4,6},{5,7},{6,4},{7,5},{8,10},{9,11},{10,... | collective-permute-start | bytes 110600 | tf_op jit(solution)/shard_map/ppermute | solution.py:655
  12.3 0.7 %collective-permute-start.4 = (f32[32,128]{1,0:T(8,128)S(1)}, f32[32,128]{1,0:T(8,128)S(1)}, u32[]{:S(2)}, u32[]{:S(2)}) collective-permute-start(f32[32,128]{1,0:T(8,128)S(1)} %get-tuple-element.41), channel_id=1, source_target_pairs={{1,6},{3,4},{4,3},{5,10},{6,1},{7,8},{8,7},{9,14},{10,5},{11,12},{... | collective-permute-start | bytes 49160 | tf_op jit(solution)/shard_map/ppermute | solution.py:655
  12.9 0.0 copy-done.3
  13.0 0.1 select_maximum_fusion.tab
  13.1 1.7 %collective-permute-done.2.refs_0_ = f32[72,128]{1,0:T(8,128)S(1)} collective-permute-done((f32[72,128]{1,0:T(8,128)S(1)}, f32[72,128]{1,0:T(8,128)S(1)}, u32[]{:S(2)}, u32[]{:S(2)}) %collective-permute-start.2) | collective-permute-done | bytes 36896 | tf_op jit(solution)/shard_map/ppermute | solution.py:655
  14.8 0.5 %shard_map.108 = (f32[56,384]{1,0:T(8,128)S(1)}, f32[56,384]{1,0:T(8,128)S(1)}, f32[56,384]{1,0:T(8,128)S(1)}, f32[56,384]{1,0:T(8,128)S(1)}, f32[56,384]{1,0:T(...) custom-call(f32[3,128]{1,0:T(4,128)S(1)} %select_maximum_fusion.tab, ...), custom_call_target="tpu_custom_call" | custom-call | tf_op jit(solution)/shard_map/pallas_call | solution.py:35
  15.2 3.4 %shard_map.107 = (f32[296,896]{1,0:T(8,128)S(1)}, f32[296,896]{1,0:T(8,128)S(1)}, f32[296,896]{1,0:T(8,128)S(1)}, f32[296,896]{1,0:T(8,128)S(1)}, f32[296,896]{1...) custom-call(f32[3,128]{1,0:T(4,128)S(1)} %select_maximum_fusion.tab, ...), custom_call_target="tpu_custom_call" | custom-call | tf_op jit(solution)/shard_map/pallas_call | solution.py:35
  18.6 0.0 collective-permute-done.4.refs_1_
  18.6 0.0 collective-permute-done.3.zr_ref
  18.6 2.3 %shard_map.109 = (f32[32,384]{1,0:T(8,128)S(1)}, f32[24,384]{1,0:T(8,128)S(1)}, f32[96,256]{1,0:T(8,128)S(1)}) custom-call(f32[3,128]{1,0:T(4,128)S(1)} %select_maximum_fusion.tab, f32[216,768]{1,0:T(8,128)S(1)} %collective-permute-done.3.zr_ref, f32[72,128]{1,0:T(8,128)S(1)} %collective-permute-done.2.refs_0_, ...), custom_call_target="tpu_custom_call" | custom-call | tf_op jit(solution)/shard_map/pallas_call | solution.py:35
  21.0 1.3 %collective-permute-start.5 = (f32[32,384]{1,0:T(8,128)S(1)}, f32[32,384]{1,0:T(8,128)S(1)}, u32[]{:S(2)}, u32[]{:S(2)}) collective-permute-start(f32[32,384]{1,0:T(8,128)S(1)} %get-tuple-element.59), channel_id=1, source_target_pairs={{0,1},{1,0},{2,3},{3,2},{4,5},{5,4},{6,7},{7,6},{8,9},{9,8},{10,11... | collective-permute-start | bytes 147464 | tf_op jit(solution)/shard_map/ppermute | solution.py:655
  22.2 0.9 %collective-permute-done.5.xr_ref = f32[32,384]{1,0:T(8,128)S(1)} collective-permute-done((f32[32,384]{1,0:T(8,128)S(1)}, f32[32,384]{1,0:T(8,128)S(1)}, u32[]{:S(2)}, u32[]{:S(2)}) %collective-permute-start.5) | collective-permute-done | bytes 49184 | tf_op jit(solution)/shard_map/ppermute | solution.py:655
  23.1 0.8 %shard_map.110 = (f32[8,24,384]{2,1,0:T(8,128)}, f32[3,6,4,256]{3,2,1,0:T(4,128)}, f32[24,384]{1,0:T(8,128)}) custom-call(f32[296,896]{1,0:T(8,128)S(1)} %get-tuple-element.40.refs_7_.t_in, f32[24,384]{1,0:T(8,128)S(1)} %get-tuple-element.58.keep_ref, f32[32,384]{1,0:T(8,128)S(1)} %collective-permute-done.5.xr_ref, f32[96,256]{1,0:T(8,128)S(1)} %get-tuple-element.60.u_in), custom_call_target="tpu_custom_call" | custom-call | tf_op jit(solution)/shard_map/pallas_call | solution.py:35
  (3 shorter events, 0.0 us)
Async XLA Ops:
  0.6 1.2 %copy-start = (s32[8,24,384]{2,1,0:T(8,128)S(1)}, s32[8,24,384]{2,1,0:T(8,128)}, u32[]{:S(2)}) copy-start(s32[8,24,384]{2,1,0:T(8,128)} %id_ref.1) | copy-start | bytes 884740
  0.6 2.0 %copy-start.2 = (s32[6,4,256]{2,1,0:T(4,128)S(1)}, s32[6,4,256]{2,1,0:T(4,128)}, u32[]{:S(2)}) copy-start(s32[6,4,256]{2,1,0:T(4,128)} %mat_ref.1) | copy-start | bytes 73732
  0.7 2.0 %copy-start.1 = (f32[3,6,4,256]{3,2,1,0:T(4,128)S(1)}, f32[3,6,4,256]{3,2,1,0:T(4,128)}, u32[]{:S(2)}) copy-start(f32[3,6,4,256]{3,2,1,0:T(4,128)} %u_ref.1) | copy-start | bytes 221188
  2.1 2.2 %collective-permute-start = (f32[1224,128]{1,0:T(8,128)S(1)}, f32[1224,128]{1,0:T(8,128)S(1)}, u32[]{:S(2)}, u32[]{:S(2)}) collective-permute-start(f32[1224,128]{1,0:T(8,128)S(1)} %get-tuple-element.33), channel_id=1, source_target_pairs={{0,1},{1,0},{2,3},{3,2},{4,5},{5,4},{6,7},{7,6},{8,9},{9,8},{10,11... | collective-permute-start | bytes 1880072 | tf_op jit(solution)/shard_map/ppermute | solution.py:655
  4.4 14.2 %collective-permute-start.3 = (f32[216,768]{1,0:T(8,128)S(1)}, f32[216,768]{1,0:T(8,128)S(1)}, u32[]{:S(2)}, u32[]{:S(2)}) collective-permute-start(f32[216,768]{1,0:T(8,128)S(1)} %get-tuple-element.36.z_ref), channel_id=1, source_target_pairs={{1,4},{3,6},{4,1},{5,8},{6,3},{7,10},{8,5},{9,12},{10,7},{11,14},{... | collective-permute-start | bytes 1990664 | tf_op jit(solution)/shard_map/ppermute | solution.py:655
  5.2 7.8 %copy-start.3 = (f32[16]{0:T(128)S(1)}, f32[16]{0:T(128)}, u32[]{:S(2)}) copy-start(f32[16]{0:T(128)} %param.15) | copy-start | bytes 196
  5.2 7.8 %copy-start.4 = (f32[16]{0:T(128)S(1)}, f32[16]{0:T(128)}, u32[]{:S(2)}) copy-start(f32[16]{0:T(128)} %param.14) | copy-start | bytes 196
  5.2 7.8 %copy-start.5 = (f32[16]{0:T(128)S(1)}, f32[16]{0:T(128)}, u32[]{:S(2)}) copy-start(f32[16]{0:T(128)} %param.13) | copy-start | bytes 196
  5.2 5.3 %collective-permute-start.1 = (f32[96,256]{1,0:T(8,128)S(1)}, f32[96,256]{1,0:T(8,128)S(1)}, u32[]{:S(2)}, u32[]{:S(2)}) collective-permute-start(f32[96,256]{1,0:T(8,128)S(1)} %get-tuple-element.35), channel_id=1, source_target_pairs={{0,1},{1,0},{2,3},{3,2},{4,5},{5,4},{6,7},{7,6},{8,9},{9,8},{10,11... | collective-permute-start | bytes 294920 | tf_op jit(solution)/shard_map/ppermute | solution.py:655
  10.7 4.0 %collective-permute-start.2 = (f32[72,128]{1,0:T(8,128)S(1)}, f32[72,128]{1,0:T(8,128)S(1)}, u32[]{:S(2)}, u32[]{:S(2)}) collective-permute-start(f32[72,128]{1,0:T(8,128)S(1)} %get-tuple-element.39), channel_id=1, source_target_pairs={{0,2},{1,3},{2,0},{3,1},{4,6},{5,7},{6,4},{7,5},{8,10},{9,11},{10,... | collective-permute-start | bytes 110600 | tf_op jit(solution)/shard_map/ppermute | solution.py:655
  12.3 6.3 %collective-permute-start.4 = (f32[32,128]{1,0:T(8,128)S(1)}, f32[32,128]{1,0:T(8,128)S(1)}, u32[]{:S(2)}, u32[]{:S(2)}) collective-permute-start(f32[32,128]{1,0:T(8,128)S(1)} %get-tuple-element.41), channel_id=1, source_target_pairs={{1,6},{3,4},{4,3},{5,10},{6,1},{7,8},{8,7},{9,14},{10,5},{11,12},{... | collective-permute-start | bytes 49160 | tf_op jit(solution)/shard_map/ppermute | solution.py:655
  21.0 2.2 %collective-permute-start.5 = (f32[32,384]{1,0:T(8,128)S(1)}, f32[32,384]{1,0:T(8,128)S(1)}, u32[]{:S(2)}, u32[]{:S(2)}) collective-permute-start(f32[32,384]{1,0:T(8,128)S(1)} %get-tuple-element.59), channel_id=1, source_target_pairs={{0,1},{1,0},{2,3},{3,2},{4,5},{5,4},{6,7},{7,6},{8,9},{9,8},{10,11... | collective-permute-start | bytes 147464 | tf_op jit(solution)/shard_map/ppermute | solution.py:655

commit v3 on v2

--- a/solution.py
+++ b/solution.py
@@ -26,6 +26,10 @@
 STEP = 3
 SPAN = 16
 MSPAN = 8
+NMAT = 16
+FAR = 1
+FAR_ROW = 9 - 3 * FAR
+NEAR = FAR_ROW + 2
 ZMECH = 4 * ML
 CORE = "lay"
 UNROLL_STRAIN = 3
@@ -70,6 +74,23 @@
     return jnp.concatenate([gather_lanes(table, c.astype(jnp.int32)) for c in tiles(code)], axis=1)
 
 
+def splats(table, count):
+    return [jnp.broadcast_to(table[:, m : m + 1], (8, LANES)) for m in range(count + 1)]
+
+
+def choose(lists, code):
+    out = [[] for _ in lists]
+    for c in tiles(code):
+        c = c.astype(jnp.int32)
+        bits = [(c & (1 << k)) != 0 for k in range(5)]
+        for n, values in enumerate(lists):
+            level = values[:16]
+            for k in range(4):
+                level = [jnp.where(bits[k], b, a) for a, b in zip(level[::2], level[1::2])]
+            out[n].append(jnp.where(bits[4], values[16], level[0]))
+    return [jnp.concatenate(x, axis=1) for x in out]
+
+
 def prev_lane(x):
     return pltpu.roll(x, 1, 1)
 
@@ -99,28 +120,36 @@
 
 
 def k_rows(in_ref, id_ref, a_ref, one_ref):
-    other = 1 - lax.axis_index(CORE)
+    core = lax.axis_index(CORE)
+    other = 1 - core
     rows = in_ref.shape[2]
     n_t = in_ref.shape[3] // LANES
+    n = 16 * HALO
     for t in range(n_t):
         at = 16 * rows * t
         for l in range(DEPTH):
             a_ref[pl.ds(at + l, rows, stride=16), :] = in_ref[0, l, :, tile_lanes(t)]
             a_ref[pl.ds(at + DEPTH + l, rows, stride=16), :] = (id_ref[l, :, tile_lanes(t)] + 1).astype(jnp.float32)
     for t in range(n_t):
-        to = 17 * rows * t
-        for g in range(rows):
+        to = (n + 16) * t
+        for g in range(HALO):
             i = 16 * (rows * t + turned(other, rows - 1, g))
             one_ref[to + 16 * g : to + 16 * g + 16, :] = a_ref[pl.ds(pl.multiple_of(i, 16), 16), :]
-        for b in range(rows // 8):
-            k = to + 16 * rows + 8 * b
-            one_ref[k : k + 8, :] = power_rows(in_ref, other, b, t)
-
-
-def k_solid(u_ref, mat_ref, mg_ref, next_ref, m_ref):
+        for b in range(2):
+            one_ref[to + n + 8 * b : to + n + 8 * b + 8, :] = power_rows(in_ref, other, b, t)
+    for k, x in enumerate(far_strip(in_ref, a_ref, other, core * (n_t - 1), core)):
+        to = (n + 16) * n_t + 8 * k
+        one_ref[to : to + 8, :] = x
+
+
+def k_rest(n_edges, in_ref, a_ref, u_ref, mat_ref, two_ref, mg_ref, strip_ref, m_ref):
     core = lax.axis_index(CORE)
+    other = 1 - core
+    rows = in_ref.shape[2]
+    n_t = in_ref.shape[3] // LANES
     mrows = mat_ref.shape[1]
-    m_t = mat_ref.shape[2] // LANES
+    mcols = mat_ref.shape[2]
+    m_t = mcols // LANES
     m_ref[...] = jnp.zeros(m_ref.shape, jnp.float32)
     for t in range(m_t):
         at = 32 * mrows * t
@@ -131,37 +160,93 @@
         for g in range(mrows):
             i = 32 * (mrows * t + turned(core, mrows - 1, g))
             mg_ref[32 * g : 32 * g + 32, tile_lanes(t)] = m_ref[pl.ds(pl.multiple_of(i, 32), 32), :]
+    for e in range(n_edges):
+        side = edge_side(n_edges, e)
+        fields = []
+        for g in range(MHALO):
+            i = 32 * (mrows * side * (m_t - 1) + turned(core, mrows - 1, mrows - 1 - g))
+            fields += [m_ref[pl.ds(pl.multiple_of(i + 8 * f, 8), 8), :] for f in range(4)]
+        (strip_ref[8 * e : 8 * e + 8, :],) = packed(side, fields, MSPAN, MHALO)
+    rest = 16 * (rows - HALO)
+    for t in range(n_t):
+        to = (rest + rows - 16) * t
+        for g in range(HALO, rows):
+            i = 16 * (rows * t + turned(other, rows - 1, g))
+            k = to + 16 * (g - HALO)
+            two_ref[k : k + 16, :] = a_ref[pl.ds(pl.multiple_of(i, 16), 16), :]
+        for b in range(2, rows // 8):
+            two_ref[to + rest + 8 * (b - 2) : to + rest + 8 * (b - 1), :] = power_rows(in_ref, other, b, t)
+    for t in range(m_t):
         for g in range(MHALO):
             i = 32 * (mrows * t + turned(core, mrows - 1, mrows - 1 - g))
-            next_ref[32 * g : 32 * g + 32, tile_lanes(t)] = m_ref[pl.ds(pl.multiple_of(i, 32), 32), :]
+            k = (rest + rows - 16) * n_t + 32 * (MHALO * t + g)
+            two_ref[k : k + 32, :] = m_ref[pl.ds(pl.multiple_of(i, 32), 32), :]
 
 
 def power_rows(in_ref, turn, b, t):
     rows = in_ref.shape[2]
-    x = in_ref[1, 0, at8(turned(turn, rows // 8 - 1, b)), tile_lanes(t)]
+    lanes = tile_lanes(t) if isinstance(t, int) else pl.ds(pl.multiple_of(LANES * t, LANES), LANES)
+    x = in_ref[1, 0, at8(turned(turn, rows // 8 - 1, b)), lanes]
     return jnp.take_along_axis(x, turned(turn, 7, sub_iota(LANES)), axis=0, mode="promise_in_bounds")
 
 
-def k_edge(n_edges, p_ref, a_ref, got_ref, mg_ref, z_ref, *edge_refs):
+def far_strip(in_ref, a_ref, turn, t, side):
+    rows = in_ref.shape[2]
+    blocks = []
+    for g in range(HALO, rows - 1):
+        i = 16 * (rows * t + turned(turn, rows - 1, g))
+        blocks += [a_ref[pl.ds(pl.multiple_of(i + k, 8), 8), :] for k in (0, 8)]
+    blocks += [power_rows(in_ref, turn, b, t) for b in range(2, rows // 8)]
+    return packed(side, blocks, SPAN, HALO)
+
+
+def edge_side(n_edges, e):
+    return 1 - lax.axis_index("col") if n_edges == 1 else 1 - e
+
+
+def edge_tile(side, width):
+    if isinstance(side, int):
+        return tile_lanes(side * (width // LANES - 1))
+    return pl.ds(pl.multiple_of(side * (width - LANES), LANES), LANES)
+
+
+def packed(side, blocks, span, keep):
+    lane = lane_iota()
+    per = LANES // span
+    out = []
+    for i in range(0, len(blocks), per):
+        acc = jnp.zeros((8, LANES), jnp.float32)
+        for k, x in enumerate(blocks[i : i + per]):
+            acc = jnp.where(lane // span == k, pltpu.roll(x, span * k + side * keep, 1), acc)
+        out.append(acc)
+    return out
+
+
+def far_rows(rows):
+    return -(-(2 * (rows - 1 - HALO) + rows // 8 - 2) * SPAN // LANES)
+
+
+def k_edge(n_edges, tab, in_ref, a_ref, got_ref, mg_ref, strip_ref, z_ref, w_ref, *refs):
     core = lax.axis_index(CORE)
-    n_t = z_ref.shape[1] // LANES // 2
-    rows = p_ref.shape[2]
+    wide = z_ref.shape[1]
+    n_t = wide // LANES // 2
+    rows = in_ref.shape[2]
     mcols = mg_ref.shape[1]
+    mrows = mg_ref.shape[0] // 32
     n = 16 * HALO
+    edge_refs, (s_ref, q0_ref, q1_ref, di_ref) = refs[: 2 * n_edges], refs[2 * n_edges :]
 
     def build(first):
         for t in range(n_t):
             lanes = tile_lanes(t if first else n_t + t)
             for g in range(HALO):
                 i = 16 * (rows * t + (g if first else rows - 1 - g))
-                z_ref[16 * g : 16 * g + 16, lanes] = a_ref[i : i + 16, :]
+                w_ref[16 * g : 16 * g + 16, lanes] = a_ref[i : i + 16, :]
             for b in range(2):
-                z_ref[n + ZMECH + 8 * b : n + ZMECH + 8 * b + 8, lanes] = power_rows(p_ref, 0 if first else 1, b, t)
+                w_ref[n + 8 * b : n + 8 * b + 8, lanes] = power_rows(in_ref, 0 if first else 1, b, t)
             lanes = tile_lanes(n_t + t if first else t)
-            at = 17 * rows * t
-            z_ref[0:n, lanes] = got_ref[at : at + n, :]
-            at += 16 * rows
-            z_ref[n + ZMECH : n + ZMECH + 16, lanes] = got_ref[at : at + 16, :]
+            at = (n + 16) * t
+            w_ref[0 : n + 16, lanes] = got_ref[at : at + n + 16, :]
 
     @pl.when(core == 0)
     def _():
@@ -171,54 +256,72 @@
     def _():
         build(False)
 
+    m = 16 * NEAR
+    z_ref[0:m, :] = w_ref[0:m, :]
+    z_ref[m + ZMECH : m + ZMECH + 8, :] = w_ref[n : n + 8, :]
+    z_ref[m + ZMECH + 8 : m + ZMECH + 16, :] = jnp.zeros((8, wide), jnp.float32)
     for g in range(MHALO):
         for f in range(4):
-            at = n + ML * f
+            at = m + ML * f
             z_ref[at : at + ML, mcols * g : mcols * (g + 1)] = mg_ref[32 * g + 8 * f : 32 * g + 8 * f + ML, :]
     for e in range(n_edges):
-        side, lanes, mlanes = edge_lanes(n_edges, e, z_ref.shape[1], mcols)
-        cells = [z_ref[8 * i : 8 * i + 8, lanes] for i in range(2 * HALO)]
-        cells += [z_ref[n + ZMECH + 8 * b : n + ZMECH + 8 * b + 8, lanes] for b in range(2)]
-        fields = [mg_ref[8 * i : 8 * i + 8, mlanes] for i in range(4 * MHALO)]
-        pack_edge(edge_refs[e], side, cells, fields)
-
-
-def edge_lanes(n_edges, e, wide, mcols):
-    if n_edges == 1:
-        side = 1 - lax.axis_index("col")
-        lanes = pl.ds(pl.multiple_of(side * (wide - LANES), LANES), LANES)
-        mlanes = pl.ds(pl.multiple_of(side * (mcols - LANES), LANES), LANES)
-        return side, lanes, mlanes
-    side = 1 - e
-    return side, tile_lanes(side * (wide // LANES - 1)), tile_lanes(side * (mcols // LANES - 1))
-
-
-def pack_edge(ref, side, cells, fields):
-    lane = lane_iota()
-    at = 0
-    for blocks, span, keep in ((cells, SPAN, HALO), (fields, MSPAN, MHALO)):
-        per = LANES // span
-        for i in range(0, len(blocks), per):
-            acc = jnp.zeros((8, LANES), jnp.float32)
-            for k, x in enumerate(blocks[i : i + per]):
-                acc = jnp.where(lane // span == k, pltpu.roll(x, span * k + side * keep, 1), acc)
-            ref[at : at + 8, :] = acc
-            at += 8
-
-
-def edge_size(cells, fields):
-    return 8 * (-(-cells * SPAN // LANES) - (-fields * MSPAN // LANES))
-
-
-def k_chip(n_edges, rows, p_ref, a_ref, got_ref, mg_ref, next_ref, z_ref, w_ref, src_ref, mw_ref, *edge_refs):
+        c_ref, d_ref = edge_refs[2 * e], edge_refs[2 * e + 1]
+        side = edge_side(n_edges, e)
+        lanes, mlanes = edge_tile(side, wide), edge_tile(side, mcols)
+        blocks = [w_ref[8 * i : 8 * i + 8, lanes] for i in range(2 * HALO)]
+        blocks += [w_ref[n + 8 * b : n + 8 * b + 8, lanes] for b in range(2)]
+        fields = [mg_ref[8 * i : 8 * i + 8, mlanes] for i in range(4 * mrows)]
+        near = packed(side, blocks, SPAN, HALO) + packed(side, fields[: 4 * MHALO], MSPAN, MHALO)
+        far = []
+        for k, x in enumerate(far_strip(in_ref, a_ref, core, side * (n_t - 1), side)):
+            at = (n + 16) * n_t + 8 * k
+            far.append(jnp.where(core == side, x, got_ref[at : at + 8, :]))
+        far += packed(side, fields[4 * MHALO :], MSPAN, MHALO)
+        far.append(strip_ref[8 * e : 8 * e + 8, :])
+        at = FAR * mcols + far_tiles() * LANES * e
+        for k, x in enumerate(packed(side, blocks[2 * NEAR : 2 * HALO] + blocks[2 * HALO + 1 :], SPAN, HALO)):
+            z_ref[m + ZMECH + 8 : m + ZMECH + 16, at + LANES * k : at + LANES * (k + 1)] = x
+        for k, x in enumerate(near + far):
+            c_ref[8 * k : 8 * k + 8, :] = x
+        for k, x in enumerate(near):
+            d_ref[8 * k : 8 * k + 8, :] = x
+    t_s = jnp.sqrt(table_of(tab, 0))
+    t_al = table_of(tab, 1)
+    v_s = splats(t_s, NMAT)
+    codes = {}
+    for g in range(FAR_ROW - 2, HALO):
+        codes[g] = w_ref[16 * g + 8 : 16 * g + 16, :]
+        (x,) = choose([v_s], codes[g])
+        s_ref[at8(g), :] = x
+        q0_ref[at8(g), :] = x * w_ref[16 * g : 16 * g + 8, :]
+    h = sink(wide)
+    top = sub_iota(wide) == 0
+    powers = {
+        g: jnp.where(top, jnp.broadcast_to(w_ref[n + g : n + g + 1, :], (8, wide)), 0.0)
+        for g in range(FAR_ROW - 1, HALO - 1)
+    }
+    for g in range(FAR_ROW - 1, HALO - 1):
+        di_ref[at8(g), :], q1_ref[at8(g), :] = first_sweep(s_ref, q0_ref, g, powers[g], h, True)
+    for f in range(FAR):
+        x = None
+        for g in range(FAR_ROW + 3 * f, FAR_ROW + 3 * f + 3):
+            t2 = second_sweep(s_ref, q1_ref, di_ref, g, powers[g], True)
+            ea = lookup(t_al, codes[g]) * t2
+            x = ea if x is None else x + ea
+        z_ref[m + ZMECH + 8 : m + ZMECH + 16, mcols * f : mcols * (f + 1)] = restrict_main(x)
+
+
+def far_tiles():
+    return -(-(2 * (HALO - NEAR) + 1) * SPAN // LANES)
+
+
+def k_chip(rows, in_ref, a_ref, got_ref, mg_ref, z_ref, after_ref, w_ref, src_ref, mw_ref):
     core = lax.axis_index(CORE)
-    wide = w_ref.shape[1]
-    n_t = wide // LANES // 2
-    mcols = mw_ref.shape[1]
+    n_t = w_ref.shape[1] // LANES // 2
     mrows = mg_ref.shape[0] // 32
     n = 16 * HALO
     w_ref[0:n, :] = z_ref[0:n, :]
-    src_ref[0:16, :] = z_ref[n + ZMECH : n + ZMECH + 16, :]
+    src_ref[0:16, :] = z_ref[n : n + 16, :]
     rest = 16 * (rows - HALO)
 
     def build(first):
@@ -228,12 +331,11 @@
                 i = 16 * (rows * t + (g if first else rows - 1 - g))
                 w_ref[16 * g : 16 * g + 16, lanes] = a_ref[i : i + 16, :]
             for b in range(2, rows // 8):
-                src_ref[8 * b : 8 * b + 8, lanes] = power_rows(p_ref, 0 if first else 1, b, t)
+                src_ref[8 * b : 8 * b + 8, lanes] = power_rows(in_ref, 0 if first else 1, b, t)
             lanes = tile_lanes(n_t + t if first else t)
-            at = 17 * rows * t
-            w_ref[n : n + rest, lanes] = got_ref[at + n : at + n + rest, :]
-            at += 16 * rows
-            src_ref[16:rows, lanes] = got_ref[at + 16 : at + rows, :]
+            at = (rest + rows - 16) * t
+            w_ref[n : n + rest, lanes] = got_ref[at : at + rest, :]
+            src_ref[16:rows, lanes] = got_ref[at + rest : at + rest + rows - 16, :]
 
     @pl.when(core == 0)
     def _():
@@ -244,21 +346,17 @@
         build(False)
 
     mw_ref[0 : 32 * mrows, :] = mg_ref[...]
-    mw_ref[32 * mrows : 32 * (mrows + MHALO), :] = next_ref[...]
-
-    for e in range(n_edges):
-        side, lanes, mlanes = edge_lanes(n_edges, e, wide, mcols)
-        cells = [w_ref[8 * i : 8 * i + 8, lanes] for i in range(2 * (rows - 1))]
-        cells += [src_ref[8 * b : 8 * b + 8, lanes] for b in range(rows // 8)]
-        fields = [mw_ref[8 * i : 8 * i + 8, mlanes] for i in range(4 * (mrows + MHALO))]
-        pack_edge(edge_refs[e], side, cells, fields)
+    for t in range(mw_ref.shape[1] // LANES):
+        at = (rest + rows - 16) * n_t + 32 * MHALO * t
+        mw_ref[32 * mrows : 32 * (mrows + MHALO), tile_lanes(t)] = got_ref[at : at + 32 * MHALO, :]
 
 
 class Sides:
-    def __init__(self, n_col, count, from_left, from_right):
+    def __init__(self, n_col, rows, mrows, from_left, from_right):
         self.left = from_left
         self.right = from_right
-        self.count = count
+        self.rows = rows
+        self.mrows = mrows
         lane = lane_iota()
         col = lax.axis_index("col")
         self.masks = {
@@ -277,14 +375,28 @@
         l = pltpu.roll(row8(self.left, v), LANES - span * k - width, 1)
         return jnp.where(right_mask, r, jnp.where(left_mask, l, 0.0))
 
-    def tile(self, i):
-        per = LANES // SPAN
-        return self.take(i // per, i % per, SPAN, HALO)
-
-    def field(self, i):
-        per = LANES // MSPAN
-        first = -(-self.count * SPAN // LANES)
-        return self.take(first + i // per, i % per, MSPAN, MHALO)
+    def block(self, first, i, span, width):
+        per = LANES // span
+        return self.take(first + i // per, i % per, span, width)
+
+    def cell(self, g, kind):
+        if g < HALO:
+            return self.block(0, 2 * g + kind, SPAN, HALO)
+        return self.block(4, 2 * (g - HALO) + kind, SPAN, HALO)
+
+    def power(self, b):
+        if b < 2:
+            return self.block(0, 2 * HALO + b, SPAN, HALO)
+        return self.block(4, 2 * (self.rows - 1 - HALO) + b - 2, SPAN, HALO)
+
+    def field(self, m, f):
+        if m < MHALO:
+            return self.block(3, 4 * m + f, MSPAN, MHALO)
+        first = 4 + far_rows(self.rows)
+        if m < self.mrows:
+            return self.block(first, 4 * (m - MHALO) + f, MSPAN, MHALO)
+        first += -(-4 * (self.mrows - MHALO) * MSPAN // LANES)
+        return self.block(first, 4 * (m - self.mrows) + f, MSPAN, MHALO)
 
 
 def spread_power(ref, n, blocks):
@@ -301,10 +413,15 @@
     return jnp.concatenate([row8(ref, n * t + i) for t in range(count)], axis=1)
 
 
-def conduct_sum(ref, i):
+def conduct_sum(ref, i, closed=False):
     x = row8(ref, i)
     sub = sub_iota(x.shape[1])
-    total = row8(ref, i - 1) + row8(ref, i + 1) + prev_lane(x) + next_lane(x)
+    before, after = prev_lane(x), next_lane(x)
+    if closed:
+        lane = lax.broadcasted_iota(jnp.int32, x.shape, 1)
+        before = jnp.where(lane > 0, before, 0.0)
+        after = jnp.where(lane < x.shape[1] - 1, after, 0.0)
+    total = row8(ref, i - 1) + row8(ref, i + 1) + before + after
     total = total + jnp.where(sub < DEPTH - 1, next_sub(x), 0.0)
     return total + jnp.where(sub > 0, prev_sub(x), 0.0)
 
@@ -313,44 +430,66 @@
     return jnp.where(sub_iota(width) == DEPTH - 1, 2.0, 0.2).astype(jnp.float32)
 
 
-def restrict_columns(x):
+def column_sums(x):
     width = x.shape[1]
-    x = x + pltpu.roll(x, width - 1, 1) + pltpu.roll(x, width - 2, 1)
-    pieces = tiles(x)
+    return x + pltpu.roll(x, width - 1, 1) + pltpu.roll(x, width - 2, 1)
+
+
+def to_solid_layers(y):
+    return jnp.where(sub_iota(y.shape[1]) < 3, y, next_sub(y)) * (1.0 / 9.0)
+
+
+def gather_main(pieces):
     lane = lane_iota()
     out = []
-    for j in range((len(pieces) - 1) // 3):
+    for j in range(len(pieces) // 3):
         got = None
         for t in range(3):
             g = gather_lanes(pieces[3 * j + t], (3 * lane) & (LANES - 1))
             got = g if got is None else jnp.where((3 * lane) >= LANES * t, g, got)
         out.append(got)
+    return out
+
+
+def gather_sides(piece):
+    lane = lane_iota()
     first = LANES - MHALO
     index = jnp.where(lane < MHALO, 3 * lane, jnp.where(lane >= first, LANES - 9 + 3 * (lane - first), 64))
-    out.append(gather_lanes(pieces[-1], index))
-    y = jnp.concatenate(out, axis=1)
-    y = jnp.where(sub_iota(y.shape[1]) < 3, y, next_sub(y))
-    return y * (1.0 / 9.0)
-
-
-def first_sweep(s_ref, q0_ref, i, power, h):
+    return gather_lanes(piece, index)
+
+
+def restrict_main(x):
+    return to_solid_layers(jnp.concatenate(gather_main(tiles(column_sums(x))), axis=1))
+
+
+def restrict_sides(x):
+    return to_solid_layers(gather_sides(column_sums(x)))
+
+
+def restrict_columns(x):
+    pieces = tiles(column_sums(x))
+    return to_solid_layers(jnp.concatenate(gather_main(pieces[:-1]) + [gather_sides(pieces[-1])], axis=1))
+
+
+def first_sweep(s_ref, q0_ref, i, power, h, closed=False):
     s = row8(s_ref, i)
-    inv = 1.0 / (h + s * conduct_sum(s_ref, i))
-    return inv, s * ((power + s * conduct_sum(q0_ref, i)) * inv)
-
-
-def second_sweep(s_ref, q1_ref, di_ref, i, power):
-    return (power + row8(s_ref, i) * conduct_sum(q1_ref, i)) * row8(di_ref, i)
+    inv = 1.0 / (h + s * conduct_sum(s_ref, i, closed))
+    return inv, s * ((power + s * conduct_sum(q0_ref, i, closed)) * inv)
+
+
+def second_sweep(s_ref, q1_ref, di_ref, i, power, closed=False):
+    return (power + row8(s_ref, i) * conduct_sum(q1_ref, i, closed)) * row8(di_ref, i)
 
 
 def k_inner(n_edges, n_col, rows, tab, w_ref, src_ref, *refs):
-    sides = Sides(n_col, 2 * (rows - 1) + rows // 8, refs[0], refs[n_edges - 1])
+    sides = Sides(n_col, rows, rows // 6, refs[0], refs[n_edges - 1])
     s_ref, al_ref, q0_ref, q1_ref, di_ref, t_ref, ea_ref, strain_ref, pw_ref = refs[n_edges:]
     own = rows - 1
     width = src_ref.shape[1] + LANES
     t_s = jnp.sqrt(table_of(tab, 0))
     t_al = table_of(tab, 1)
-    side_power = jnp.concatenate([sides.tile(2 * own + k) for k in range(rows // 8)], axis=0)
+    v_s = splats(t_s, NMAT)
+    side_power = jnp.concatenate([sides.power(k) for k in range(rows // 8)], axis=0)
     n_p = s_ref.shape[0] // 8
     spread_power(pw_ref, n_p, [(FRONT, jnp.concatenate([src_ref[...], side_power], axis=1))])
     h = sink(width)
@@ -358,11 +497,10 @@
     for i in range(0, own + 2 * STEP + 2, STEP):
         later = []
         for g in range(i, min(i + STEP, own)):
-            temp = jnp.concatenate([w_ref[16 * g : 16 * g + 8, :], sides.tile(2 * g)], axis=1)
-            code = jnp.concatenate([w_ref[16 * g + 8 : 16 * g + 16, :], sides.tile(2 * g + 1)], axis=1)
-            s = lookup(t_s, code)
-            later += [(s_ref, FRONT + g, s), (q0_ref, FRONT + g, s * temp)]
-            later += [(al_ref, FRONT + g, lookup(t_al, code))]
+            temp = jnp.concatenate([w_ref[16 * g : 16 * g + 8, :], sides.cell(g, 0)], axis=1)
+            code = jnp.concatenate([w_ref[16 * g + 8 : 16 * g + 16, :], sides.cell(g, 1)], axis=1)
+            s, al = choose([v_s], code)[0], lookup(t_al, code)
+            later += [(s_ref, FRONT + g, s), (q0_ref, FRONT + g, s * temp), (al_ref, FRONT + g, al)]
         for g in range(max(1, i - STEP - 1), min(i - 1, own - 1)):
             r = FRONT + g
             inv, q1 = first_sweep(s_ref, q0_ref, r, power_row(pw_ref, n_p, r), h)
@@ -399,27 +537,26 @@
     return out
 
 
-def mech_tables(tab):
-    t_mod = table_of(tab, 2)
-    t_m = jnp.sqrt(t_mod)
-    return t_m, jnp.where(t_mod > 0.0, 1.0 / jnp.where(t_mod > 0.0, t_m, 1.0), 0.0), t_mod
+def moduli(values, code):
+    (mod,) = choose([values], code)
+    inside = mod > 0.0
+    root = jnp.sqrt(mod)
+    return mod, root, jnp.where(inside, 1.0 / jnp.where(inside, root, 1.0), 0.0)
 
 
 def k_mech(n_edges, n_col, rows, tab, mw_ref, *refs):
-    sides = Sides(n_col, 2 * (rows - 1) + rows // 8, refs[0], refs[n_edges - 1])
+    sides = Sides(n_col, rows, rows // 6, refs[0], refs[n_edges - 1])
     mi_ref, mod_ref = refs[n_edges : n_edges + 2]
     uu_refs = refs[n_edges + 2 : n_edges + 5]
     pre_refs = refs[n_edges + 5 : n_edges + 8]
-    t_m, t_mi, t_mod = mech_tables(tab)
+    values = splats(table_of(tab, 2), NMAT)
     count = mw_ref.shape[0] // 32
     for m in range(count):
         fields = []
         for f in range(4):
-            side = sides.field(4 * m + f)
+            side = sides.field(m, f)
             fields.append(jnp.concatenate([mw_ref[32 * m + 8 * f : 32 * m + 8 * f + 8, :], side], axis=1))
-        root = lookup(t_m, fields[3])
-        mi_ref[at8(m), :] = lookup(t_mi, fields[3])
-        mod_ref[at8(m), :] = lookup(t_mod, fields[3])
+        mod_ref[at8(m), :], root, mi_ref[at8(m), :] = moduli(values, fields[3])
         for f in range(3):
             uu_refs[f][at8(m), :] = root * fields[f]
     for m in range(1, count - 1):
@@ -428,9 +565,58 @@
             pre_refs[d][at8(m), :] = near[d] * (1.0 / STIFF_DIAG) - row8(uu_refs[d], m)
 
 
+def edge_patch(n_edges, e, corners, zr_ref, mcols, v_s, t_al, scratch):
+    s_ref, q0_ref, q1_ref, di_ref = scratch
+    side = edge_side(n_edges, e)
+    lanes = edge_tile(side, zr_ref.shape[1])
+    lane = lane_iota()
+    mine = ((lane >= LANES - HALO) & (side == 1)) | ((lane < HALO) & (side == 0))
+    zsrc = 16 * NEAR + ZMECH
+    per = LANES // SPAN
+
+    def strip(i):
+        at = FAR * mcols + LANES * (far_tiles() * e + i // per)
+        x = zr_ref[zsrc + 8 : zsrc + 16, at : at + LANES]
+        return pltpu.roll(x, LANES - SPAN * (i % per) - side * HALO, 1)
+
+    def cell(j, kind):
+        x = zr_ref[16 * j + 8 * kind : 16 * j + 8 * kind + 8, lanes] if j < NEAR else strip(2 * (j - NEAR) + kind)
+        return jnp.where(mine, x, corners.cell(j, kind))
+
+    first = FAR_ROW - 2
+    codes = {}
+    for j in range(first, HALO):
+        codes[j] = cell(j, 1)
+        (s,) = choose([v_s], codes[j])
+        s_ref[at8(j - first), :] = s
+        q0_ref[at8(j - first), :] = s * cell(j, 0)
+    power = [
+        jnp.where(mine, zr_ref[zsrc : zsrc + 8, lanes], corners.power(0)),
+        jnp.where(mine, strip(2 * (HALO - NEAR)), corners.power(1)),
+    ]
+    top = sub_iota(LANES) == 0
+    h = sink(LANES)
+
+    def power_of(j):
+        x = power[j // 8][j % 8 : j % 8 + 1, :]
+        return jnp.where(top, jnp.broadcast_to(x, (8, LANES)), 0.0)
+
+    for j in range(first + 1, HALO - 1):
+        at = at8(j - first)
+        di_ref[at, :], q1_ref[at, :] = first_sweep(s_ref, q0_ref, j - first, power_of(j), h)
+    out = []
+    for f in range(FAR):
+        x = None
+        for j in range(FAR_ROW + 3 * f, FAR_ROW + 3 * f + 3):
+            ea = lookup(t_al, codes[j]) * second_sweep(s_ref, q1_ref, di_ref, j - first, power_of(j))
+            x = ea if x is None else x + ea
+        out.append(restrict_sides(x))
+    return out
+
+
 def k_outer(n_edges, n_col, rows, tab, zr_ref, *refs):
-    sides = Sides(n_col, 2 * (rows - 1) + rows // 8, refs[0], refs[n_edges - 1])
-    corners = Sides(n_col, 2 * HALO + 2, refs[n_edges], refs[2 * n_edges - 1])
+    sides = Sides(n_col, rows, rows // 6, refs[0], refs[n_edges - 1])
+    corners = Sides(n_col, rows, rows // 6, refs[n_edges], refs[2 * n_edges - 1])
     rest = refs[2 * n_edges :]
     s_in, al_in, q0_in, q1_in, di_in, t_in, ea_in, strain_in, src_ref = rest[:9]
     mi_in, mod_in = rest[9:11]
@@ -445,7 +631,10 @@
     width = wide + LANES
     t_s = jnp.sqrt(table_of(tab, 0))
     t_al = table_of(tab, 1)
-    zsrc = 16 * HALO + ZMECH
+    v_s = splats(t_s, NMAT)
+    zmech = 16 * NEAR
+    zsrc = zmech + ZMECH
+    zfar = zsrc + 8
     for g in range(3):
         k = AHEAD - 1 - g
         for dst, src in ((s_ref, s_in), (al_ref, al_in), (q0_ref, q0_in)):
@@ -455,30 +644,27 @@
         q1_ref[at8(AHEAD - 1 - g), :] = row8(q1_in, FRONT + g)
     di_ref[at8(AHEAD - 2), :] = row8(di_in, FRONT + 1)
     n_p = s_ref.shape[0] // 8
-    near = jnp.concatenate([src_ref[0:8, :], sides.tile(2 * own)], axis=1)
-    far = jnp.concatenate([corners.tile(2 * HALO), corners.tile(2 * HALO + 1)], axis=0)
-    far = jnp.concatenate([zr_ref[zsrc : zsrc + 16, :], far], axis=1)
+    near = jnp.concatenate([src_ref[0:8, :], sides.power(0)], axis=1)
+    far = jnp.concatenate([zr_ref[zsrc : zsrc + 8, :], corners.power(0)], axis=1)
     spread_power(
         pw_ref,
         n_p,
-        [(AHEAD - 1, near[0:1, :]), (AHEAD - 2, near[1:2, :]), (AHEAD, far[0:8, :]), (AHEAD + 8, far[8:HALO, :])],
+        [(AHEAD - 1, near[0:1, :]), (AHEAD - 2, near[1:2, :]), (AHEAD, far)],
     )
     h = sink(width)
 
-    for i in range(0, HALO + 2 * STEP + 1, STEP):
+    for i in range(0, NEAR + 2 * STEP + 1, STEP):
         later = []
-        for j in range(i, min(i + STEP, HALO)):
-            temp = jnp.concatenate([zr_ref[16 * j : 16 * j + 8, :], corners.tile(2 * j)], axis=1)
-            code = jnp.concatenate([zr_ref[16 * j + 8 : 16 * j + 16, :], corners.tile(2 * j + 1)], axis=1)
-            s = lookup(t_s, code)
-            later += [(s_ref, AHEAD + j, s), (q0_ref, AHEAD + j, s * temp)]
-            if j < HALO - 2:
-                later += [(al_ref, AHEAD + j, lookup(t_al, code))]
-        for j in range(max(-1, i - STEP - 1), min(i - 1, HALO - 1)):
+        for j in range(i, min(i + STEP, NEAR)):
+            temp = jnp.concatenate([zr_ref[16 * j : 16 * j + 8, :], corners.cell(j, 0)], axis=1)
+            code = jnp.concatenate([zr_ref[16 * j + 8 : 16 * j + 16, :], corners.cell(j, 1)], axis=1)
+            s, al = choose([v_s], code)[0], lookup(t_al, code)
+            later += [(s_ref, AHEAD + j, s), (q0_ref, AHEAD + j, s * temp), (al_ref, AHEAD + j, al)]
+        for j in range(max(-1, i - STEP - 1), min(i - 1, NEAR - 1)):
             r = AHEAD + j
             inv, q1 = first_sweep(s_ref, q0_ref, r, power_row(pw_ref, n_p, r), h)
             later += [(di_ref, r, inv), (q1_ref, r, q1)]
-        for j in range(max(-2, i - 2 * STEP - 2), min(i - STEP - 2, HALO - 2)):
+        for j in range(max(-2, i - 2 * STEP - 2), min(i - STEP - 2, NEAR - 2)):
             r = AHEAD + j
             t2 = second_sweep(s_ref, q1_ref, di_ref, r, power_row(pw_ref, n_p, r))
             later += [(t_keep, r, t2), (ea_ref, r, row8(al_ref, r) * t2)]
@@ -504,24 +690,32 @@
     mwidth = mod_in.shape[1]
     mcols = mwidth - LANES
     n_m = count + MHALO
-    for m in range(MHALO + 1):
+    for m in range(MHALO + 1 - FAR):
         i = AHEAD - 3 + 3 * m
         x = row8(ea_ref, i) + row8(ea_ref, i + 1) + row8(ea_ref, i + 2)
         st_ref[at8(MHALO - m), :] = restrict_columns(x)
+    lane = lane_iota()
+    has_left, has_right = sides.side > 0, sides.side < n_col - 1
+    patches = [edge_patch(n_edges, e, corners, zr_ref, mcols, v_s, t_al, rest[41:45]) for e in range(n_edges)]
+    for f in range(FAR):
+        pieces = tiles(zr_ref[zfar : zfar + 8, mcols * f : mcols * (f + 1)])
+        right, left = patches[0][f], patches[-1][f]
+        pieces[0] = jnp.where((lane == 0) & has_left, left, pieces[0])
+        pieces[-1] = jnp.where((lane == LANES - 1) & has_right, right, pieces[-1])
+        beside = jnp.where((lane < MHALO) & has_right, right, jnp.where((lane >= LANES - MHALO) & has_left, left, 0.0))
+        st_ref[at8(FAR - 1 - f), :] = jnp.concatenate(pieces + [beside], axis=1)
     for m in range(1, count):
         st_ref[at8(MHALO + m), :] = row8(strain_in, m)
-    t_m, t_mi, t_mod = mech_tables(tab)
+    values = splats(table_of(tab, 2), NMAT)
     for i in range(MHALO):
         j = MHALO - 1 - i
         fields = []
         for f in range(4):
-            body = zr_ref[16 * HALO + ML * f : 16 * HALO + ML * f + 8, mcols * j : mcols * (j + 1)]
+            body = zr_ref[zmech + ML * f : zmech + ML * f + 8, mcols * j : mcols * (j + 1)]
             body = jnp.where(sub_iota(mcols) < ML, body, 0.0)
-            side = corners.field(4 * j + f)
+            side = corners.field(j, f)
             fields.append(jnp.concatenate([body, side], axis=1))
-        root = lookup(t_m, fields[3])
-        mi_ref[at8(i), :] = lookup(t_mi, fields[3])
-        mod_ref[at8(i), :] = lookup(t_mod, fields[3])
+        mod_ref[at8(i), :], root, mi_ref[at8(i), :] = moduli(values, fields[3])
         for f in range(3):
             uu_refs[f][at8(i), :] = root * fields[f]
     for ref, src in zip((mi_ref, mod_ref, *uu_refs), (mi_in, mod_in, *uu_in)):
@@ -660,44 +854,50 @@
     def along(r, c, a):
         return (r + 1, c, 0) if a == 1 else (r - 1, c, 1)
 
+    wide = 2 * half
+    own = rows - 1
     kind = lax.broadcasted_iota(jnp.int32, (2, *temp.shape), 0)
-    packed = jnp.where(kind == 0, temp[None], power[None, None])
+    both = jnp.where(kind == 0, temp[None], power[None, None])
     tab = jnp.stack([heat_table, growth_table, modulus_table])
     tab = jnp.pad(tab, ((0, 0), (1, LANES - 1 - tab.shape[1])))
-    cells, one = call(k_rows, [(16 * rows * n_t, LANES), (17 * rows * n_t, LANES)], [packed, ids])
-    got = send(one, swap)
-    mg, ahead = call(
-        k_solid,
-        [(32 * mrows, mcols), (32 * MHALO, mcols)],
-        [offset, mat],
+    n = 16 * HALO
+    n_far = 8 * far_rows(rows)
+    cells, one = call(k_rows, [(16 * rows * n_t, LANES), ((n + 16) * n_t + n_far, LANES)], [both, ids])
+    got1 = send(one, swap)
+    two, mg, strip = call(
+        functools.partial(k_rest, n_edges),
+        [
+            ((16 * (rows - HALO) + rows - 16) * n_t + 32 * MHALO * m_t, LANES),
+            (32 * mrows, mcols),
+            (8 * n_edges, LANES),
+        ],
+        [both, cells, offset, mat],
         scratch=[(32 * mrows * m_t, LANES)],
     )
-    ahead = send(ahead, swap)
-    wide = 2 * half
-    own = rows - 1
-    z, *edges = call(
+    strip = send(strip, swap)
+    got2 = send(two, swap)
+    n_c = 32 + n_far - 8 * (-4 * (mrows - MHALO) * MSPAN // LANES) + 8
+    z, first_rows, *edges = call(
         functools.partial(k_edge, n_edges),
-        [(16 * HALO + ZMECH + 16, wide)] + [(edge_size(2 * HALO + 2, 4 * MHALO), LANES)] * n_edges,
-        [packed, cells, got, mg],
+        [(16 * NEAR + ZMECH + 16, wide), (n + 16, wide)] + [(n_c, LANES), (32, LANES)] * n_edges,
+        [tab, both, cells, got1, mg, strip],
+        scratch=[(8 * HALO, wide)] * 4,
     )
     zr = send(z, along)
     if n_edges == 1:
-        corners = [send(edges[0], lambda r, c, a: along(r, 1 - c, a))]
+        sides = [send(edges[0], lambda r, c, a: (r, 1 - c, a))]
+        corners = [send(edges[1], lambda r, c, a: along(r, 1 - c, a))]
     else:
+        sides = [send(edges[0], lambda r, c, a: (r, c + 1, a)), send(edges[2], lambda r, c, a: (r, c - 1, a))]
         corners = [
-            send(edges[0], lambda r, c, a: along(r, c + 1, a)),
-            send(edges[1], lambda r, c, a: along(r, c - 1, a)),
+            send(edges[1], lambda r, c, a: along(r, c + 1, a)),
+            send(edges[3], lambda r, c, a: along(r, c - 1, a)),
         ]
-    w, src, mw, *edges = call(
-        functools.partial(k_chip, n_edges, rows),
-        [(16 * rows, wide), (rows, wide), (32 * (mrows + MHALO), mcols)]
-        + [(edge_size(2 * own + rows // 8, 4 * (mrows + MHALO)), LANES)] * n_edges,
-        [packed, cells, got, mg, ahead, z],
+    w, src, mw = call(
+        functools.partial(k_chip, rows),
+        [(16 * rows, wide), (rows, wide), (32 * (mrows + MHALO), mcols)],
+        [both, cells, got2, mg, first_rows, sides[0]],
     )
-    if n_edges == 1:
-        sides = [send(edges[0], lambda r, c, a: (r, 1 - c, a))]
-    else:
-        sides = [send(edges[0], lambda r, c, a: (r, c + 1, a)), send(edges[1], lambda r, c, a: (r, c - 1, a))]
     width = wide + LANES
     mwidth = mcols + LANES
     n_w = 8 * (rows + FRONT + 4)
@@ -717,7 +917,10 @@
         functools.partial(k_outer, n_edges, n_col, rows),
         [(32, half), (24, half), (24 * mrows, mcols)],
         [tab, zr] + sides + corners + list(inner) + [src] + list(solid),
-        scratch=[(n_h, width)] * 7 + [(n_h * (width // LANES), LANES)] + [(n_m, mwidth)] * 13,
+        scratch=[(n_h, width)] * 7
+        + [(n_h * (width // LANES), LANES)]
+        + [(n_m, mwidth)] * 13
+        + [(8 * HALO, LANES)] * 4,
     )
     xr = send(x, swap)
     t_out, u_out, slow = call(

time: 24.1 us -> 21.6 us (0.90)
  waiting for transfers between devices: 5.12 us -> 3.76 us
  Pallas kernels: 7.72 us -> 6.58 us
    ppermute x6 -> x7, waiting for transfers between devices: 5.12 us -> 3.76 us  [send(): return lax.ppermute(x, axes, pairs(dims, sends))]
    pallas_call x8, Pallas kernels: 7.72 us -> 6.58 us  [call(): pl.pallas_call(kernel, out_shape=[jax.ShapeDtypeStruct(s, jnp.float32) fo...]
    ppermute x6 -> x7, starting transfers between devices: 9.05 us -> 9.08 us  [send(): return lax.ppermute(x, axes, pairs(dims, sends))]
  transfers between devices with their start and end apart: 6 -> 7, of which waited for: 4 -> 3; matrix products, arithmetic and copies ran while one was open for 0% -> 0% of each run, Pallas kernels for 17% -> 13%
where the time goes in v3:
time: 21.6 us; the launch traced here: 21.4 us
  starting transfers between devices  9.08 us (42%)
  Pallas kernels  6.58 us (30%)
  waiting for transfers between devices  3.76 us (17%)
  other arithmetic  1.22 us (6%)
  between operations  0.78 us (4%)
    ppermute x7, starting transfers between devices, send(): return lax.ppermute(x, axes, pairs(dims, sends))  9.08 us
    pallas_call x8, Pallas kernels, call(): pl.pallas_call(kernel, out_shape=[jax.ShapeDtypeStruct(s, jnp.float32) fo...  6.58 us
    ppermute x7, waiting for transfers between devices, send(): return lax.ppermute(x, axes, pairs(dims, sends))  3.76 us
    select_n x1, other arithmetic, per_device(): both = jnp.where(kind == 0, temp[None], power[None, None])  1.14 us
  transfers between devices with their start and end apart: 7, of which 3 were waited for; matrix products, arithmetic and copies ran while one was open for 0% of the time, Pallas kernels for 13%

profile of v3, /device:TPU:0, one launch (start us, length us, event | category | flops | bytes accessed | tf_op | source)
XLA Modules:
  0.0 21.4 jit_solution(7659144434715753417)
XLA Ops:
  0.6 0.0 copy-start
  0.6 0.0 copy-start.2
  0.7 0.0 copy-start.1
  0.7 1.1 %broadcast_select_fusion.in_ref = f32[2,8,24,384]{3,2,1,0:T(8,128)S(1)} fusion(f32[24,384]{1,0:T(8,128)} %param.10, f32[8,24,384]{2,1,0:T(8,128)} %param.8, pred[2]{0:T(512)(128)(4,1)S(1)} %iota_compare_fusion.2), kind=kLoop, calls=%fused_computation | loop fusion | flops 147456 | bytes 921602 | tf_op jit(solution)/shard_map/jit(_where)/select_n | solution.py:860
  1.8 0.0 copy-done
  1.8 0.0 copy-start.3
  1.8 0.0 copy-start.4
  1.8 0.0 copy-start.5
  1.9 0.3 %shard_map.103 = (f32[1152,128]{1,0:T(8,128)S(1)}, f32[608,128]{1,0:T(8,128)S(1)}) custom-call(f32[2,8,24,384]{3,2,1,0:T(8,128)S(1)} %broadcast_select_fusion.in_ref, s32[8,24,384]{2,1,0:T(8,128)S(1)} %copy-done), custom_call_target="tpu_custom_call" | custom-call | tf_op jit(solution)/shard_map/pallas_call | solution.py:39
  2.2 0.5 %collective-permute-start.1 = (f32[608,128]{1,0:T(8,128)S(1)}, f32[608,128]{1,0:T(8,128)S(1)}, u32[]{:S(2)}, u32[]{:S(2)}) collective-permute-start(f32[608,128]{1,0:T(8,128)S(1)} %get-tuple-element.37), channel_id=1, source_target_pairs={{0,1},{1,0},{2,3},{3,2},{4,5},{5,4},{6,7},{7,6},{8,9},{9,8},{10,11... | collective-permute-start | bytes 933896 | tf_op jit(solution)/shard_map/ppermute | solution.py:849
  2.7 0.2 shard_map.104
  2.9 0.1 collective-permute-start.2
  3.0 0.0 copy-done.4
  3.0 0.1 select_maximum_fusion.tab
  3.1 1.0 %collective-permute-done.2.strip_ref = f32[8,128]{1,0:T(8,128)S(1)} collective-permute-done((f32[8,128]{1,0:T(8,128)S(1)}, f32[8,128]{1,0:T(8,128)S(1)}, u32[]{:S(2)}, u32[]{:S(2)}) %collective-permute-start.2) | collective-permute-done | bytes 4128 | tf_op jit(solution)/shard_map/ppermute | solution.py:849
  4.1 0.0 collective-permute-done.1.got_ref
  4.1 0.7 %shard_map.105 = (f32[168,768]{1,0:T(8,128)S(1)}, f32[192,768]{1,0:T(8,128)S(1)}, f32[80,128]{1,0:T(8,128)S(1)}, f32[32,128]{1,0:T(8,128)S(1)}) custom-call(f32[3,128]{1,0:T(4,128)S(1)} %select_maximum_fusion.tab, f32[2,8,24,384]{3,2,1,0:T(8,128)S(1)} %broadcast_select_fusion.in_ref, f32[1152,128]{1,0:T(8,128)S(1)} %get-tuple-element.34.a_ref, ...), custom_call_target="tpu_custom_call" | custom-call | tf_op jit(solution)/shard_map/pallas_call | solution.py:39
  4.8 0.7 %collective-permute-start.4 = (f32[168,768]{1,0:T(8,128)S(1)}, f32[168,768]{1,0:T(8,128)S(1)}, u32[]{:S(2)}, u32[]{:S(2)}) collective-permute-start(f32[168,768]{1,0:T(8,128)S(1)} %get-tuple-element.44), channel_id=1, source_target_pairs={{1,4},{3,6},{4,1},{5,8},{6,3},{7,10},{8,5},{9,12},{10,7},{11,14},{... | collective-permute-start | bytes 1548296 | tf_op jit(solution)/shard_map/ppermute | solution.py:849
  5.5 4.2 %collective-permute-start = (f32[840,128]{1,0:T(8,128)S(1)}, f32[840,128]{1,0:T(8,128)S(1)}, u32[]{:S(2)}, u32[]{:S(2)}) collective-permute-start(f32[840,128]{1,0:T(8,128)S(1)} %get-tuple-element.35), channel_id=1, source_target_pairs={{0,1},{1,0},{2,3},{3,2},{4,5},{5,4},{6,7},{7,6},{8,9},{9,8},{10,11... | collective-permute-start | bytes 1290248 | tf_op jit(solution)/shard_map/ppermute | solution.py:849
  9.7 1.5 %collective-permute-start.3 = (f32[80,128]{1,0:T(8,128)S(1)}, f32[80,128]{1,0:T(8,128)S(1)}, u32[]{:S(2)}, u32[]{:S(2)}) collective-permute-start(f32[80,128]{1,0:T(8,128)S(1)} %get-tuple-element.40), channel_id=1, source_target_pairs={{0,2},{1,3},{2,0},{3,1},{4,6},{5,7},{6,4},{7,5},{8,10},{9,11},{10,... | collective-permute-start | bytes 122888 | tf_op jit(solution)/shard_map/ppermute | solution.py:849
  11.2 0.7 %collective-permute-start.5 = (f32[32,128]{1,0:T(8,128)S(1)}, f32[32,128]{1,0:T(8,128)S(1)}, u32[]{:S(2)}, u32[]{:S(2)}) collective-permute-start(f32[32,128]{1,0:T(8,128)S(1)} %get-tuple-element.45), channel_id=1, source_target_pairs={{1,6},{3,4},{4,3},{5,10},{6,1},{7,8},{8,7},{9,14},{10,5},{11,12},{... | collective-permute-start | bytes 49160 | tf_op jit(solution)/shard_map/ppermute | solution.py:849
  11.9 1.9 %collective-permute-done.3.after_ref.refs_0_ = f32[80,128]{1,0:T(8,128)S(1)} collective-permute-done((f32[80,128]{1,0:T(8,128)S(1)}, f32[80,128]{1,0:T(8,128)S(1)}, u32[]{:S(2)}, u32[]{:S(2)}) %collective-permute-start.3) | collective-permute-done | bytes 40992 | tf_op jit(solution)/shard_map/ppermute | solution.py:849
  13.7 0.0 collective-permute-done.got_ref
  13.7 0.1 shard_map.106
  13.8 0.3 %shard_map.108 = (f32[56,384]{1,0:T(8,128)S(1)}, f32[56,384]{1,0:T(8,128)S(1)}, f32[56,384]{1,0:T(8,128)S(1)}, f32[56,384]{1,0:T(8,128)S(1)}, f32[56,384]{1,0:T(...) custom-call(f32[3,128]{1,0:T(4,128)S(1)} %select_maximum_fusion.tab, ...), custom_call_target="tpu_custom_call" | custom-call | tf_op jit(solution)/shard_map/pallas_call | solution.py:39
  14.2 2.3 %shard_map.107 = (f32[296,896]{1,0:T(8,128)S(1)}, f32[296,896]{1,0:T(8,128)S(1)}, f32[296,896]{1,0:T(8,128)S(1)}, f32[296,896]{1,0:T(8,128)S(1)}, f32[296,896]{1...) custom-call(f32[3,128]{1,0:T(4,128)S(1)} %select_maximum_fusion.tab, ...), custom_call_target="tpu_custom_call" | custom-call | tf_op jit(solution)/shard_map/pallas_call | solution.py:39
  16.5 0.0 collective-permute-done.5.refs_1_
  16.5 0.0 collective-permute-done.4.zr_ref
  16.5 1.8 %shard_map.109 = (f32[32,384]{1,0:T(8,128)S(1)}, f32[24,384]{1,0:T(8,128)S(1)}, f32[96,256]{1,0:T(8,128)S(1)}) custom-call(f32[3,128]{1,0:T(4,128)S(1)} %select_maximum_fusion.tab, f32[168,768]{1,0:T(8,128)S(1)} %collective-permute-done.4.zr_ref, f32[80,128]{1,0:T(8,128)S(1)} %collective-permute-done.3.after_ref.refs_0_, ...), custom_call_target="tpu_custom_call" | custom-call | tf_op jit(solution)/shard_map/pallas_call | solution.py:39
  18.3 1.4 %collective-permute-start.6 = (f32[32,384]{1,0:T(8,128)S(1)}, f32[32,384]{1,0:T(8,128)S(1)}, u32[]{:S(2)}, u32[]{:S(2)}) collective-permute-start(f32[32,384]{1,0:T(8,128)S(1)} %get-tuple-element.63), channel_id=1, source_target_pairs={{0,1},{1,0},{2,3},{3,2},{4,5},{5,4},{6,7},{7,6},{8,9},{9,8},{10,11... | collective-permute-start | bytes 147464 | tf_op jit(solution)/shard_map/ppermute | solution.py:849
  19.7 0.9 %collective-permute-done.6.xr_ref = f32[32,384]{1,0:T(8,128)S(1)} collective-permute-done((f32[32,384]{1,0:T(8,128)S(1)}, f32[32,384]{1,0:T(8,128)S(1)}, u32[]{:S(2)}, u32[]{:S(2)}) %collective-permute-start.6) | collective-permute-done | bytes 49184 | tf_op jit(solution)/shard_map/ppermute | solution.py:849
  20.6 0.8 %shard_map.110 = (f32[8,24,384]{2,1,0:T(8,128)}, f32[3,6,4,256]{3,2,1,0:T(4,128)}, f32[24,384]{1,0:T(8,128)}) custom-call(f32[296,896]{1,0:T(8,128)S(1)} %get-tuple-element.43.refs_7_.t_in, f32[24,384]{1,0:T(8,128)S(1)} %get-tuple-element.62.keep_ref, f32[32,384]{1,0:T(8,128)S(1)} %collective-permute-done.6.xr_ref, f32[96,256]{1,0:T(8,128)S(1)} %get-tuple-element.64.u_in), custom_call_target="tpu_custom_call" | custom-call | tf_op jit(solution)/shard_map/pallas_call | solution.py:39
  (5 shorter events, 0.0 us)
Async XLA Ops:
  0.6 1.2 %copy-start = (s32[8,24,384]{2,1,0:T(8,128)S(1)}, s32[8,24,384]{2,1,0:T(8,128)}, u32[]{:S(2)}) copy-start(s32[8,24,384]{2,1,0:T(8,128)} %id_ref.1) | copy-start | bytes 884740
  0.6 2.1 %copy-start.2 = (s32[6,4,256]{2,1,0:T(4,128)S(1)}, s32[6,4,256]{2,1,0:T(4,128)}, u32[]{:S(2)}) copy-start(s32[6,4,256]{2,1,0:T(4,128)} %mat_ref.1) | copy-start | bytes 73732
  0.7 2.1 %copy-start.1 = (f32[3,6,4,256]{3,2,1,0:T(4,128)S(1)}, f32[3,6,4,256]{3,2,1,0:T(4,128)}, u32[]{:S(2)}) copy-start(f32[3,6,4,256]{3,2,1,0:T(4,128)} %u_ref.1) | copy-start | bytes 221188
  1.8 1.2 %copy-start.3 = (f32[16]{0:T(128)S(1)}, f32[16]{0:T(128)}, u32[]{:S(2)}) copy-start(f32[16]{0:T(128)} %param.15) | copy-start | bytes 196
  1.8 1.2 %copy-start.4 = (f32[16]{0:T(128)S(1)}, f32[16]{0:T(128)}, u32[]{:S(2)}) copy-start(f32[16]{0:T(128)} %param.14) | copy-start | bytes 196
  1.8 1.2 %copy-start.5 = (f32[16]{0:T(128)S(1)}, f32[16]{0:T(128)}, u32[]{:S(2)}) copy-start(f32[16]{0:T(128)} %param.13) | copy-start | bytes 196
  2.2 1.9 %collective-permute-start.1 = (f32[608,128]{1,0:T(8,128)S(1)}, f32[608,128]{1,0:T(8,128)S(1)}, u32[]{:S(2)}, u32[]{:S(2)}) collective-permute-start(f32[608,128]{1,0:T(8,128)S(1)} %get-tuple-element.37), channel_id=1, source_target_pairs={{0,1},{1,0},{2,3},{3,2},{4,5},{5,4},{6,7},{7,6},{8,9},{9,8},{10,11... | collective-permute-start | bytes 933896 | tf_op jit(solution)/shard_map/ppermute | solution.py:849
  2.9 1.2 %collective-permute-start.2 = (f32[8,128]{1,0:T(8,128)S(1)}, f32[8,128]{1,0:T(8,128)S(1)}, u32[]{:S(2)}, u32[]{:S(2)}) collective-permute-start(f32[8,128]{1,0:T(8,128)S(1)} %get-tuple-element.38), channel_id=1, source_target_pairs={{0,1},{1,0},{2,3},{3,2},{4,5},{5,4},{6,7},{7,6},{8,9},{9,8},{10,11... | collective-permute-start | bytes 12296 | tf_op jit(solution)/shard_map/ppermute | solution.py:849
  4.8 11.6 %collective-permute-start.4 = (f32[168,768]{1,0:T(8,128)S(1)}, f32[168,768]{1,0:T(8,128)S(1)}, u32[]{:S(2)}, u32[]{:S(2)}) collective-permute-start(f32[168,768]{1,0:T(8,128)S(1)} %get-tuple-element.44), channel_id=1, source_target_pairs={{1,4},{3,6},{4,1},{5,8},{6,3},{7,10},{8,5},{9,12},{10,7},{11,14},{... | collective-permute-start | bytes 1548296 | tf_op jit(solution)/shard_map/ppermute | solution.py:849
  5.5 8.2 %collective-permute-start = (f32[840,128]{1,0:T(8,128)S(1)}, f32[840,128]{1,0:T(8,128)S(1)}, u32[]{:S(2)}, u32[]{:S(2)}) collective-permute-start(f32[840,128]{1,0:T(8,128)S(1)} %get-tuple-element.35), channel_id=1, source_target_pairs={{0,1},{1,0},{2,3},{3,2},{4,5},{5,4},{6,7},{7,6},{8,9},{9,8},{10,11... | collective-permute-start | bytes 1290248 | tf_op jit(solution)/shard_map/ppermute | solution.py:849
  9.7 4.0 %collective-permute-start.3 = (f32[80,128]{1,0:T(8,128)S(1)}, f32[80,128]{1,0:T(8,128)S(1)}, u32[]{:S(2)}, u32[]{:S(2)}) collective-permute-start(f32[80,128]{1,0:T(8,128)S(1)} %get-tuple-element.40), channel_id=1, source_target_pairs={{0,2},{1,3},{2,0},{3,1},{4,6},{5,7},{6,4},{7,5},{8,10},{9,11},{10,... | collective-permute-start | bytes 122888 | tf_op jit(solution)/shard_map/ppermute | solution.py:849
  11.2 5.3 %collective-permute-start.5 = (f32[32,128]{1,0:T(8,128)S(1)}, f32[32,128]{1,0:T(8,128)S(1)}, u32[]{:S(2)}, u32[]{:S(2)}) collective-permute-start(f32[32,128]{1,0:T(8,128)S(1)} %get-tuple-element.45), channel_id=1, source_target_pairs={{1,6},{3,4},{4,3},{5,10},{6,1},{7,8},{8,7},{9,14},{10,5},{11,12},{... | collective-permute-start | bytes 49160 | tf_op jit(solution)/shard_map/ppermute | solution.py:849
  18.3 2.3 %collective-permute-start.6 = (f32[32,384]{1,0:T(8,128)S(1)}, f32[32,384]{1,0:T(8,128)S(1)}, u32[]{:S(2)}, u32[]{:S(2)}) collective-permute-start(f32[32,384]{1,0:T(8,128)S(1)} %get-tuple-element.63), channel_id=1, source_target_pairs={{0,1},{1,0},{2,3},{3,2},{4,5},{5,4},{6,7},{7,6},{8,9},{9,8},{10,11... | collective-permute-start | bytes 147464 | tf_op jit(solution)/shard_map/ppermute | solution.py:849

commit v4 on v3

--- a/solution.py
+++ b/solution.py
@@ -27,7 +27,8 @@
 SPAN = 16
 MSPAN = 8
 NMAT = 16
-FAR = 1
+FAR = 2
+EDGE_COST = 10**10
 FAR_ROW = 9 - 3 * FAR
 NEAR = FAR_ROW + 2
 ZMECH = 4 * ML
@@ -35,12 +36,14 @@
 UNROLL_STRAIN = 3
 
 
-def call(kernel, outs, args, scratch=(), specs=None):
+def call(kernel, outs, args, scratch=(), specs=None, aliases=None, cost=0):
     return pl.pallas_call(
         kernel,
         out_shape=[jax.ShapeDtypeStruct(s, jnp.float32) for s in outs],
         in_specs=specs or [VMEM] * len(args),
         out_specs=[VMEM] * len(outs),
+        input_output_aliases=aliases or {},
+        cost_estimate=pl.CostEstimate(flops=cost, bytes_accessed=0, transcendentals=0) if cost else None,
         scratch_shapes=[pltpu.VMEM(s, jnp.float32) if isinstance(s, tuple) else s for s in scratch],
         compiler_params=pltpu.CompilerParams(vmem_limit_bytes=16 * 1024 * 1024),
     )(*args)
@@ -259,7 +262,7 @@
     m = 16 * NEAR
     z_ref[0:m, :] = w_ref[0:m, :]
     z_ref[m + ZMECH : m + ZMECH + 8, :] = w_ref[n : n + 8, :]
-    z_ref[m + ZMECH + 8 : m + ZMECH + 16, :] = jnp.zeros((8, wide), jnp.float32)
+    z_ref[m + ZMECH + 8 :, :] = jnp.zeros((z_ref.shape[0] - m - ZMECH - 8, wide), jnp.float32)
     for g in range(MHALO):
         for f in range(4):
             at = m + ML * f
@@ -278,9 +281,8 @@
             far.append(jnp.where(core == side, x, got_ref[at : at + 8, :]))
         far += packed(side, fields[4 * MHALO :], MSPAN, MHALO)
         far.append(strip_ref[8 * e : 8 * e + 8, :])
-        at = FAR * mcols + far_tiles() * LANES * e
         for k, x in enumerate(packed(side, blocks[2 * NEAR : 2 * HALO] + blocks[2 * HALO + 1 :], SPAN, HALO)):
-            z_ref[m + ZMECH + 8 : m + ZMECH + 16, at + LANES * k : at + LANES * (k + 1)] = x
+            z_ref[far_place(e, k, wide, mcols)] = x
         for k, x in enumerate(near + far):
             c_ref[8 * k : 8 * k + 8, :] = x
         for k, x in enumerate(near):
@@ -315,7 +317,15 @@
     return -(-(2 * (HALO - NEAR) + 1) * SPAN // LANES)
 
 
-def k_chip(rows, in_ref, a_ref, got_ref, mg_ref, z_ref, after_ref, w_ref, src_ref, mw_ref):
+def far_place(e, k, wide, mcols):
+    q = FAR * mcols // LANES + far_tiles() * e + k
+    at = 16 * NEAR + ZMECH + 8 + 8 * (q // (wide // LANES))
+    return slice(at, at + 8), tile_lanes(q % (wide // LANES))
+
+
+def k_chip(rows, in_ref, a_ref, got_ref, mg_ref, z_ref, *refs):
+    count = (len(refs) - 3) // 2
+    w_ref, src_ref, mw_ref = refs[count : count + 3]
     core = lax.axis_index(CORE)
     n_t = w_ref.shape[1] // LANES // 2
     mrows = mg_ref.shape[0] // 32
@@ -575,8 +585,7 @@
     per = LANES // SPAN
 
     def strip(i):
-        at = FAR * mcols + LANES * (far_tiles() * e + i // per)
-        x = zr_ref[zsrc + 8 : zsrc + 16, at : at + LANES]
+        x = zr_ref[far_place(e, i // per, zr_ref.shape[1], mcols)]
         return pltpu.roll(x, LANES - SPAN * (i % per) - side * HALO, 1)
 
     def cell(j, kind):
@@ -879,9 +888,17 @@
     n_c = 32 + n_far - 8 * (-4 * (mrows - MHALO) * MSPAN // LANES) + 8
     z, first_rows, *edges = call(
         functools.partial(k_edge, n_edges),
-        [(16 * NEAR + ZMECH + 16, wide), (n + 16, wide)] + [(n_c, LANES), (32, LANES)] * n_edges,
+        [(far_place(n_edges, -1, wide, mcols)[0].stop, wide), (n + 16, wide)] + [(n_c, LANES), (32, LANES)] * n_edges,
         [tab, both, cells, got1, mg, strip],
+        cost=EDGE_COST,
         scratch=[(8 * HALO, wide)] * 4,
+    )
+    leaving = [z, *edges]
+    w, src, mw, z, *edges = call(
+        functools.partial(k_chip, rows),
+        [(16 * rows, wide), (rows, wide), (32 * (mrows + MHALO), mcols)] + [x.shape for x in leaving],
+        [both, cells, got2, mg, first_rows] + leaving,
+        aliases={5 + k: 3 + k for k in range(len(leaving))},
     )
     zr = send(z, along)
     if n_edges == 1:
@@ -893,11 +910,6 @@
             send(edges[1], lambda r, c, a: along(r, c + 1, a)),
             send(edges[3], lambda r, c, a: along(r, c - 1, a)),
         ]
-    w, src, mw = call(
-        functools.partial(k_chip, rows),
-        [(16 * rows, wide), (rows, wide), (32 * (mrows + MHALO), mcols)],
-        [both, cells, got2, mg, first_rows, sides[0]],
-    )
     width = wide + LANES
     mwidth = mcols + LANES
     n_w = 8 * (rows + FRONT + 4)

time: 21.6 us -> 20.8 us (0.963)
  waiting for transfers between devices: 3.76 us -> 2.78 us
    ppermute x7, waiting for transfers between devices: 3.76 us -> 2.78 us  [send(): return lax.ppermute(x, axes, pairs(dims, sends))]
  transfers between devices with their start and end apart: 7 -> 7, of which waited for: 3 -> 3; matrix products, arithmetic and copies ran while one was open for 0% -> 0% of each run, Pallas kernels for 13% -> 18%
where the time goes in v4:
time: 20.8 us; the launch traced here: 20.6 us
  starting transfers between devices  9.19 us (44%)
  Pallas kernels  6.62 us (32%)
  waiting for transfers between devices  2.78 us (13%)
  other arithmetic  1.22 us (6%)
  between operations  0.79 us (4%)
    ppermute x7, starting transfers between devices, send(): return lax.ppermute(x, axes, pairs(dims, sends))  9.19 us
    pallas_call x8, Pallas kernels, call(): pl.pallas_call(kernel, out_shape=[jax.ShapeDtypeStruct(s, jnp.float32) fo...  6.62 us
    ppermute x7, waiting for transfers between devices, send(): return lax.ppermute(x, axes, pairs(dims, sends))  2.78 us
    select_n x1, other arithmetic, per_device(): both = jnp.where(kind == 0, temp[None], power[None, None])  1.14 us
  transfers between devices with their start and end apart: 7, of which 3 were waited for; matrix products, arithmetic and copies ran while one was open for 0% of the time, Pallas kernels for 18%

profile of v4, /device:TPU:0, one launch (start us, length us, event | category | flops | bytes accessed | tf_op | source)
XLA Modules:
  0.0 20.6 jit_solution(5368233423972416750)
XLA Ops:
  0.6 0.0 copy-start
  0.6 0.0 copy-start.2
  0.7 0.0 copy-start.1
  0.7 1.1 %broadcast_select_fusion.in_ref = f32[2,8,24,384]{3,2,1,0:T(8,128)S(1)} fusion(f32[24,384]{1,0:T(8,128)} %param.10, f32[8,24,384]{2,1,0:T(8,128)} %param.8, pred[2]{0:T(512)(128)(4,1)S(1)} %iota_compare_fusion.2), kind=kLoop, calls=%fused_computation | loop fusion | flops 147456 | bytes 921602 | tf_op jit(solution)/shard_map/jit(_where)/select_n | solution.py:869
  1.8 0.0 copy-done
  1.8 0.0 copy-start.3
  1.8 0.0 copy-start.4
  1.8 0.0 copy-start.5
  1.9 0.3 %shard_map.103 = (f32[1152,128]{1,0:T(8,128)S(1)}, f32[608,128]{1,0:T(8,128)S(1)}) custom-call(f32[2,8,24,384]{3,2,1,0:T(8,128)S(1)} %broadcast_select_fusion.in_ref, s32[8,24,384]{2,1,0:T(8,128)S(1)} %copy-done), custom_call_target="tpu_custom_call" | custom-call | tf_op jit(solution)/shard_map/pallas_call | solution.py:40
  2.2 0.5 %collective-permute-start.1 = (f32[608,128]{1,0:T(8,128)S(1)}, f32[608,128]{1,0:T(8,128)S(1)}, u32[]{:S(2)}, u32[]{:S(2)}) collective-permute-start(f32[608,128]{1,0:T(8,128)S(1)} %get-tuple-element.40), channel_id=1, source_target_pairs={{0,1},{1,0},{2,3},{3,2},{4,5},{5,4},{6,7},{7,6},{8,9},{9,8},{10,11... | collective-permute-start | bytes 933896 | tf_op jit(solution)/shard_map/ppermute | solution.py:858
  2.7 0.2 shard_map.104
  2.9 0.1 collective-permute-start.2
  3.0 0.4 %collective-permute-start = (f32[840,128]{1,0:T(8,128)S(1)}, f32[840,128]{1,0:T(8,128)S(1)}, u32[]{:S(2)}, u32[]{:S(2)}) collective-permute-start(f32[840,128]{1,0:T(8,128)S(1)} %get-tuple-element.38), channel_id=1, source_target_pairs={{0,1},{1,0},{2,3},{3,2},{4,5},{5,4},{6,7},{7,6},{8,9},{9,8},{10,11... | collective-permute-start | bytes 1290248 | tf_op jit(solution)/shard_map/ppermute | solution.py:858
  3.5 0.0 copy-done.4
  3.5 0.1 select_maximum_fusion.tab
  3.5 0.6 %collective-permute-done.2.strip_ref = f32[8,128]{1,0:T(8,128)S(1)} collective-permute-done((f32[8,128]{1,0:T(8,128)S(1)}, f32[8,128]{1,0:T(8,128)S(1)}, u32[]{:S(2)}, u32[]{:S(2)}) %collective-permute-start.2) | collective-permute-done | bytes 4128 | tf_op jit(solution)/shard_map/ppermute | solution.py:858
  4.1 0.0 collective-permute-done.1.got_ref
  4.1 1.0 %shard_map.105 = (f32[120,768]{1,0:T(8,128)S(1)}, f32[192,768]{1,0:T(8,128)S(1)}, f32[80,128]{1,0:T(8,128)S(1)}, f32[32,128]{1,0:T(8,128)S(1)}) custom-call(f32[3,128]{1,0:T(4,128)S(1)} %select_maximum_fusion.tab, f32[2,8,24,384]{3,2,1,0:T(8,128)S(1)} %broadcast_select_fusion.in_ref, f32[1152,128]{1,0:T(8,128)S(1)} %get-tuple-element.37.a_ref, ...), custom_call_target="tpu_custom_call" | custom-call | flops 10000000000 | tf_op jit(solution)/shard_map/pallas_call | solution.py:40
  5.1 0.0 collective-permute-done.got_ref
  5.1 0.1 shard_map.106
  5.2 0.7 %collective-permute-start.4 = (f32[120,768]{1,0:T(8,128)S(1)}, f32[120,768]{1,0:T(8,128)S(1)}, u32[]{:S(2)}, u32[]{:S(2)}) collective-permute-start(f32[120,768]{1,0:T(8,128)S(1)} %get-tuple-element.50), channel_id=1, source_target_pairs={{1,4},{3,6},{4,1},{5,8},{6,3},{7,10},{8,5},{9,12},{10,7},{11,14},{... | collective-permute-start | bytes 1105928 | tf_op jit(solution)/shard_map/ppermute | solution.py:858
  5.9 2.8 %collective-permute-start.3 = (f32[80,128]{1,0:T(8,128)S(1)}, f32[80,128]{1,0:T(8,128)S(1)}, u32[]{:S(2)}, u32[]{:S(2)}) collective-permute-start(f32[80,128]{1,0:T(8,128)S(1)} %get-tuple-element.48), channel_id=1, source_target_pairs={{0,2},{1,3},{2,0},{3,1},{4,6},{5,7},{6,4},{7,5},{8,10},{9,11},{10,... | collective-permute-start | bytes 122888 | tf_op jit(solution)/shard_map/ppermute | solution.py:858
  8.7 0.7 %collective-permute-start.5 = (f32[32,128]{1,0:T(8,128)S(1)}, f32[32,128]{1,0:T(8,128)S(1)}, u32[]{:S(2)}, u32[]{:S(2)}) collective-permute-start(f32[32,128]{1,0:T(8,128)S(1)} %get-tuple-element.51), channel_id=1, source_target_pairs={{1,6},{3,4},{4,3},{5,10},{6,1},{7,8},{8,7},{9,14},{10,5},{11,12},{... | collective-permute-start | bytes 49160 | tf_op jit(solution)/shard_map/ppermute | solution.py:858
  9.3 1.3 %collective-permute-done.3.refs_0_ = f32[80,128]{1,0:T(8,128)S(1)} collective-permute-done((f32[80,128]{1,0:T(8,128)S(1)}, f32[80,128]{1,0:T(8,128)S(1)}, u32[]{:S(2)}, u32[]{:S(2)}) %collective-permute-start.3) | collective-permute-done | bytes 40992 | tf_op jit(solution)/shard_map/ppermute | solution.py:858
  10.7 0.3 %shard_map.108 = (f32[56,384]{1,0:T(8,128)S(1)}, f32[56,384]{1,0:T(8,128)S(1)}, f32[56,384]{1,0:T(8,128)S(1)}, f32[56,384]{1,0:T(8,128)S(1)}, f32[56,384]{1,0:T(...) custom-call(f32[3,128]{1,0:T(4,128)S(1)} %select_maximum_fusion.tab, ...), custom_call_target="tpu_custom_call" | custom-call | tf_op jit(solution)/shard_map/pallas_call | solution.py:40
  11.0 2.3 %shard_map.107 = (f32[296,896]{1,0:T(8,128)S(1)}, f32[296,896]{1,0:T(8,128)S(1)}, f32[296,896]{1,0:T(8,128)S(1)}, f32[296,896]{1,0:T(8,128)S(1)}, f32[296,896]{1...) custom-call(f32[3,128]{1,0:T(4,128)S(1)} %select_maximum_fusion.tab, ...), custom_call_target="tpu_custom_call" | custom-call | tf_op jit(solution)/shard_map/pallas_call | solution.py:40
  13.3 0.0 collective-permute-done.5.refs_1_
  13.3 0.0 collective-permute-done.4.zr_ref
  13.3 1.6 %shard_map.109 = (f32[32,384]{1,0:T(8,128)S(1)}, f32[24,384]{1,0:T(8,128)S(1)}, f32[96,256]{1,0:T(8,128)S(1)}) custom-call(f32[3,128]{1,0:T(4,128)S(1)} %select_maximum_fusion.tab, f32[120,768]{1,0:T(8,128)S(1)} %collective-permute-done.4.zr_ref, f32[80,128]{1,0:T(8,128)S(1)} %collective-permute-done.3.refs_0_, ...), custom_call_target="tpu_custom_call" | custom-call | tf_op jit(solution)/shard_map/pallas_call | solution.py:40
  14.9 4.0 %collective-permute-start.6 = (f32[32,384]{1,0:T(8,128)S(1)}, f32[32,384]{1,0:T(8,128)S(1)}, u32[]{:S(2)}, u32[]{:S(2)}) collective-permute-start(f32[32,384]{1,0:T(8,128)S(1)} %get-tuple-element.69), channel_id=1, source_target_pairs={{0,1},{1,0},{2,3},{3,2},{4,5},{5,4},{6,7},{7,6},{8,9},{9,8},{10,11... | collective-permute-start | bytes 147464 | tf_op jit(solution)/shard_map/ppermute | solution.py:858
  18.9 0.9 %collective-permute-done.6.xr_ref = f32[32,384]{1,0:T(8,128)S(1)} collective-permute-done((f32[32,384]{1,0:T(8,128)S(1)}, f32[32,384]{1,0:T(8,128)S(1)}, u32[]{:S(2)}, u32[]{:S(2)}) %collective-permute-start.6) | collective-permute-done | bytes 49184 | tf_op jit(solution)/shard_map/ppermute | solution.py:858
  19.8 0.8 %shard_map.110 = (f32[8,24,384]{2,1,0:T(8,128)}, f32[3,6,4,256]{3,2,1,0:T(4,128)}, f32[24,384]{1,0:T(8,128)}) custom-call(f32[296,896]{1,0:T(8,128)S(1)} %get-tuple-element.49.refs_7_.t_in, f32[24,384]{1,0:T(8,128)S(1)} %get-tuple-element.68.keep_ref, f32[32,384]{1,0:T(8,128)S(1)} %collective-permute-done.6.xr_ref, f32[96,256]{1,0:T(8,128)S(1)} %get-tuple-element.70.u_in), custom_call_target="tpu_custom_call" | custom-call | tf_op jit(solution)/shard_map/pallas_call | solution.py:40
  (5 shorter events, 0.0 us)
Async XLA Ops:
  0.6 1.2 %copy-start = (s32[8,24,384]{2,1,0:T(8,128)S(1)}, s32[8,24,384]{2,1,0:T(8,128)}, u32[]{:S(2)}) copy-start(s32[8,24,384]{2,1,0:T(8,128)} %id_ref.1) | copy-start | bytes 884740
  0.6 2.1 %copy-start.2 = (s32[6,4,256]{2,1,0:T(4,128)S(1)}, s32[6,4,256]{2,1,0:T(4,128)}, u32[]{:S(2)}) copy-start(s32[6,4,256]{2,1,0:T(4,128)} %mat_ref.1) | copy-start | bytes 73732
  0.7 2.1 %copy-start.1 = (f32[3,6,4,256]{3,2,1,0:T(4,128)S(1)}, f32[3,6,4,256]{3,2,1,0:T(4,128)}, u32[]{:S(2)}) copy-start(f32[3,6,4,256]{3,2,1,0:T(4,128)} %u_ref.1) | copy-start | bytes 221188
  1.8 1.6 %copy-start.3 = (f32[16]{0:T(128)S(1)}, f32[16]{0:T(128)}, u32[]{:S(2)}) copy-start(f32[16]{0:T(128)} %param.15) | copy-start | bytes 196
  1.8 1.6 %copy-start.4 = (f32[16]{0:T(128)S(1)}, f32[16]{0:T(128)}, u32[]{:S(2)}) copy-start(f32[16]{0:T(128)} %param.14) | copy-start | bytes 196
  1.8 1.6 %copy-start.5 = (f32[16]{0:T(128)S(1)}, f32[16]{0:T(128)}, u32[]{:S(2)}) copy-start(f32[16]{0:T(128)} %param.13) | copy-start | bytes 196
  2.2 1.9 %collective-permute-start.1 = (f32[608,128]{1,0:T(8,128)S(1)}, f32[608,128]{1,0:T(8,128)S(1)}, u32[]{:S(2)}, u32[]{:S(2)}) collective-permute-start(f32[608,128]{1,0:T(8,128)S(1)} %get-tuple-element.40), channel_id=1, source_target_pairs={{0,1},{1,0},{2,3},{3,2},{4,5},{5,4},{6,7},{7,6},{8,9},{9,8},{10,11... | collective-permute-start | bytes 933896 | tf_op jit(solution)/shard_map/ppermute | solution.py:858
  2.9 1.2 %collective-permute-start.2 = (f32[8,128]{1,0:T(8,128)S(1)}, f32[8,128]{1,0:T(8,128)S(1)}, u32[]{:S(2)}, u32[]{:S(2)}) collective-permute-start(f32[8,128]{1,0:T(8,128)S(1)} %get-tuple-element.41), channel_id=1, source_target_pairs={{0,1},{1,0},{2,3},{3,2},{4,5},{5,4},{6,7},{7,6},{8,9},{9,8},{10,11... | collective-permute-start | bytes 12296 | tf_op jit(solution)/shard_map/ppermute | solution.py:858
  3.0 2.1 %collective-permute-start = (f32[840,128]{1,0:T(8,128)S(1)}, f32[840,128]{1,0:T(8,128)S(1)}, u32[]{:S(2)}, u32[]{:S(2)}) collective-permute-start(f32[840,128]{1,0:T(8,128)S(1)} %get-tuple-element.38), channel_id=1, source_target_pairs={{0,1},{1,0},{2,3},{3,2},{4,5},{5,4},{6,7},{7,6},{8,9},{9,8},{10,11... | collective-permute-start | bytes 1290248 | tf_op jit(solution)/shard_map/ppermute | solution.py:858
  5.2 8.1 %collective-permute-start.4 = (f32[120,768]{1,0:T(8,128)S(1)}, f32[120,768]{1,0:T(8,128)S(1)}, u32[]{:S(2)}, u32[]{:S(2)}) collective-permute-start(f32[120,768]{1,0:T(8,128)S(1)} %get-tuple-element.50), channel_id=1, source_target_pairs={{1,4},{3,6},{4,1},{5,8},{6,3},{7,10},{8,5},{9,12},{10,7},{11,14},{... | collective-permute-start | bytes 1105928 | tf_op jit(solution)/shard_map/ppermute | solution.py:858
  5.9 4.7 %collective-permute-start.3 = (f32[80,128]{1,0:T(8,128)S(1)}, f32[80,128]{1,0:T(8,128)S(1)}, u32[]{:S(2)}, u32[]{:S(2)}) collective-permute-start(f32[80,128]{1,0:T(8,128)S(1)} %get-tuple-element.48), channel_id=1, source_target_pairs={{0,2},{1,3},{2,0},{3,1},{4,6},{5,7},{6,4},{7,5},{8,10},{9,11},{10,... | collective-permute-start | bytes 122888 | tf_op jit(solution)/shard_map/ppermute | solution.py:858
  8.7 4.6 %collective-permute-start.5 = (f32[32,128]{1,0:T(8,128)S(1)}, f32[32,128]{1,0:T(8,128)S(1)}, u32[]{:S(2)}, u32[]{:S(2)}) collective-permute-start(f32[32,128]{1,0:T(8,128)S(1)} %get-tuple-element.51), channel_id=1, source_target_pairs={{1,6},{3,4},{4,3},{5,10},{6,1},{7,8},{8,7},{9,14},{10,5},{11,12},{... | collective-permute-start | bytes 49160 | tf_op jit(solution)/shard_map/ppermute | solution.py:858
  14.9 4.9 %collective-permute-start.6 = (f32[32,384]{1,0:T(8,128)S(1)}, f32[32,384]{1,0:T(8,128)S(1)}, u32[]{:S(2)}, u32[]{:S(2)}) collective-permute-start(f32[32,384]{1,0:T(8,128)S(1)} %get-tuple-element.69), channel_id=1, source_target_pairs={{0,1},{1,0},{2,3},{3,2},{4,5},{5,4},{6,7},{7,6},{8,9},{9,8},{10,11... | collective-permute-start | bytes 147464 | tf_op jit(solution)/shard_map/ppermute | solution.py:858

commit v5 on v4

--- a/solution.py
+++ b/solution.py
@@ -24,14 +24,14 @@
 FRONT = 9
 AHEAD = 5
 STEP = 3
-SPAN = 16
+SPAN = 11
 MSPAN = 8
 NMAT = 16
 FAR = 2
 EDGE_COST = 10**10
 FAR_ROW = 9 - 3 * FAR
-NEAR = FAR_ROW + 2
-ZMECH = 4 * ML
+KEEP = 3
+Z_TEMP, Z_CODE, Z_HEAT, Z_STRAIN, Z_SOLID, Z_POWER, Z_FAR = 0, 16, 40, 56, 64, 88, 96
 CORE = "lay"
 UNROLL_STRAIN = 3
 
@@ -145,7 +145,7 @@
         one_ref[to : to + 8, :] = x
 
 
-def k_rest(n_edges, in_ref, a_ref, u_ref, mat_ref, two_ref, mg_ref, strip_ref, m_ref):
+def k_rest(n_edges, in_ref, a_ref, u_ref, mat_ref, two_ref, mg_ref, m_ref):
     core = lax.axis_index(CORE)
     other = 1 - core
     rows = in_ref.shape[2]
@@ -169,7 +169,8 @@
         for g in range(MHALO):
             i = 32 * (mrows * side * (m_t - 1) + turned(core, mrows - 1, mrows - 1 - g))
             fields += [m_ref[pl.ds(pl.multiple_of(i + 8 * f, 8), 8), :] for f in range(4)]
-        (strip_ref[8 * e : 8 * e + 8, :],) = packed(side, fields, MSPAN, MHALO)
+        at = two_ref.shape[0] - 8 * (n_edges - e)
+        (two_ref[at : at + 8, :],) = packed(side, fields, MSPAN, MHALO)
     rest = 16 * (rows - HALO)
     for t in range(n_t):
         to = (rest + rows - 16) * t
@@ -226,18 +227,17 @@
 
 
 def far_rows(rows):
-    return -(-(2 * (rows - 1 - HALO) + rows // 8 - 2) * SPAN // LANES)
-
-
-def k_edge(n_edges, tab, in_ref, a_ref, got_ref, mg_ref, strip_ref, z_ref, w_ref, *refs):
+    return -(-(2 * (rows - 1 - HALO) + rows // 8 - 2) // (LANES // SPAN))
+
+
+def k_edge(n_edges, tab, in_ref, a_ref, got_ref, mg_ref, z_ref, w_ref, *refs):
     core = lax.axis_index(CORE)
     wide = z_ref.shape[1]
     n_t = wide // LANES // 2
     rows = in_ref.shape[2]
     mcols = mg_ref.shape[1]
-    mrows = mg_ref.shape[0] // 32
     n = 16 * HALO
-    edge_refs, (s_ref, q0_ref, q1_ref, di_ref) = refs[: 2 * n_edges], refs[2 * n_edges :]
+    edge_refs, (s_ref, q0_ref, q1_ref, di_ref) = refs[:n_edges], refs[n_edges:]
 
     def build(first):
         for t in range(n_t):
@@ -259,80 +259,95 @@
     def _():
         build(False)
 
-    m = 16 * NEAR
-    z_ref[0:m, :] = w_ref[0:m, :]
-    z_ref[m + ZMECH : m + ZMECH + 8, :] = w_ref[n : n + 8, :]
-    z_ref[m + ZMECH + 8 :, :] = jnp.zeros((z_ref.shape[0] - m - ZMECH - 8, wide), jnp.float32)
+    for g in range(2):
+        z_ref[Z_TEMP + 8 * g : Z_TEMP + 8 * g + 8, :] = w_ref[16 * g : 16 * g + 8, :]
+    for g in range(3):
+        z_ref[Z_CODE + 8 * g : Z_CODE + 8 * g + 8, :] = w_ref[16 * g + 8 : 16 * g + 16, :]
+    z_ref[Z_POWER : Z_POWER + 8, :] = w_ref[n : n + 8, :]
+    z_ref[Z_FAR:, :] = jnp.zeros((z_ref.shape[0] - Z_FAR, wide), jnp.float32)
     for g in range(MHALO):
         for f in range(4):
-            at = m + ML * f
+            at = Z_SOLID + ML * f
             z_ref[at : at + ML, mcols * g : mcols * (g + 1)] = mg_ref[32 * g + 8 * f : 32 * g + 8 * f + ML, :]
     for e in range(n_edges):
-        c_ref, d_ref = edge_refs[2 * e], edge_refs[2 * e + 1]
         side = edge_side(n_edges, e)
         lanes, mlanes = edge_tile(side, wide), edge_tile(side, mcols)
         blocks = [w_ref[8 * i : 8 * i + 8, lanes] for i in range(2 * HALO)]
         blocks += [w_ref[n + 8 * b : n + 8 * b + 8, lanes] for b in range(2)]
-        fields = [mg_ref[8 * i : 8 * i + 8, mlanes] for i in range(4 * mrows)]
-        near = packed(side, blocks, SPAN, HALO) + packed(side, fields[: 4 * MHALO], MSPAN, MHALO)
-        far = []
-        for k, x in enumerate(far_strip(in_ref, a_ref, core, side * (n_t - 1), side)):
-            at = (n + 16) * n_t + 8 * k
-            far.append(jnp.where(core == side, x, got_ref[at : at + 8, :]))
-        far += packed(side, fields[4 * MHALO :], MSPAN, MHALO)
-        far.append(strip_ref[8 * e : 8 * e + 8, :])
-        for k, x in enumerate(packed(side, blocks[2 * NEAR : 2 * HALO] + blocks[2 * HALO + 1 :], SPAN, HALO)):
+        fields = [mg_ref[8 * i : 8 * i + 8, mlanes] for i in range(4 * MHALO)]
+        near = packed(side, blocks, SPAN, HALO) + packed(side, fields, MSPAN, MHALO)
+        strip = blocks[4 : 2 * HALO : 2] + blocks[7 : 2 * HALO : 2] + blocks[2 * HALO + 1 :]
+        for k, x in enumerate(packed(side, strip, SPAN, HALO)):
             z_ref[far_place(e, k, wide, mcols)] = x
-        for k, x in enumerate(near + far):
-            c_ref[8 * k : 8 * k + 8, :] = x
         for k, x in enumerate(near):
-            d_ref[8 * k : 8 * k + 8, :] = x
+            edge_refs[e][8 * k : 8 * k + 8, :] = x
     t_s = jnp.sqrt(table_of(tab, 0))
     t_al = table_of(tab, 1)
     v_s = splats(t_s, NMAT)
     codes = {}
-    for g in range(FAR_ROW - 2, HALO):
+    for g in range(HALO):
         codes[g] = w_ref[16 * g + 8 : 16 * g + 16, :]
-        (x,) = choose([v_s], codes[g])
+        x = lookup(t_s, codes[g]) if g % 2 else choose([v_s], codes[g])[0]
         s_ref[at8(g), :] = x
         q0_ref[at8(g), :] = x * w_ref[16 * g : 16 * g + 8, :]
     h = sink(wide)
     top = sub_iota(wide) == 0
     powers = {
-        g: jnp.where(top, jnp.broadcast_to(w_ref[n + g : n + g + 1, :], (8, wide)), 0.0)
-        for g in range(FAR_ROW - 1, HALO - 1)
+        g: jnp.where(top, jnp.broadcast_to(w_ref[n + g : n + g + 1, :], (8, wide)), 0.0) for g in range(1, HALO - 1)
     }
-    for g in range(FAR_ROW - 1, HALO - 1):
+    for g in range(1, HALO - 1):
         di_ref[at8(g), :], q1_ref[at8(g), :] = first_sweep(s_ref, q0_ref, g, powers[g], h, True)
+    z_ref[Z_HEAT : Z_HEAT + 16, :] = q1_ref[8:24, :]
+
+    def expansion(g):
+        return lookup(t_al, codes[g]) * second_sweep(s_ref, q1_ref, di_ref, g, powers[g], True)
+
+    z_ref[Z_STRAIN : Z_STRAIN + 8, :] = expansion(2)
     for f in range(FAR):
-        x = None
-        for g in range(FAR_ROW + 3 * f, FAR_ROW + 3 * f + 3):
-            t2 = second_sweep(s_ref, q1_ref, di_ref, g, powers[g], True)
-            ea = lookup(t_al, codes[g]) * t2
-            x = ea if x is None else x + ea
-        z_ref[m + ZMECH + 8 : m + ZMECH + 16, mcols * f : mcols * (f + 1)] = restrict_main(x)
+        g = FAR_ROW + 3 * f
+        x = expansion(g) + expansion(g + 1) + expansion(g + 2)
+        z_ref[Z_FAR : Z_FAR + 8, mcols * f : mcols * (f + 1)] = restrict_main(x)
 
 
 def far_tiles():
-    return -(-(2 * (HALO - NEAR) + 1) * SPAN // LANES)
+    return -(-(2 * HALO - 4) // (LANES // SPAN))
 
 
 def far_place(e, k, wide, mcols):
     q = FAR * mcols // LANES + far_tiles() * e + k
-    at = 16 * NEAR + ZMECH + 8 + 8 * (q // (wide // LANES))
+    at = Z_FAR + 8 * (q // (wide // LANES))
     return slice(at, at + 8), tile_lanes(q % (wide // LANES))
 
 
-def k_chip(rows, in_ref, a_ref, got_ref, mg_ref, z_ref, *refs):
-    count = (len(refs) - 3) // 2
-    w_ref, src_ref, mw_ref = refs[count : count + 3]
+def k_beside(n_edges, rows, in_ref, a_ref, one_ref, got_ref, mg_ref, z_ref, *refs):
+    near_refs, c_refs = refs[:n_edges], refs[n_edges : 2 * n_edges]
+    core = lax.axis_index(CORE)
+    n_t = in_ref.shape[3] // LANES
+    mrows = mg_ref.shape[0] // 32
+    n = 16 * HALO
+    for e in range(n_edges):
+        side = edge_side(n_edges, e)
+        mlanes = edge_tile(side, mg_ref.shape[1])
+        fields = [mg_ref[8 * i : 8 * i + 8, mlanes] for i in range(4 * MHALO, 4 * mrows)]
+        far = [near_refs[e][8 * k : 8 * k + 8, :] for k in range(4)]
+        for k, x in enumerate(far_strip(in_ref, a_ref, core, side * (n_t - 1), side)):
+            at = (n + 16) * n_t + 8 * k
+            far.append(jnp.where(core == side, x, one_ref[at : at + 8, :]))
+        far += packed(side, fields, MSPAN, MHALO)
+        at = got_ref.shape[0] - 8 * (n_edges - e)
+        far.append(got_ref[at : at + 8, :])
+        for k, x in enumerate(far):
+            c_refs[e][8 * k : 8 * k + 8, :] = x
+
+
+def k_chip(rows, in_ref, a_ref, got_ref, mg_ref, first_ref, w_ref, src_ref, mw_ref):
     core = lax.axis_index(CORE)
     n_t = w_ref.shape[1] // LANES // 2
     mrows = mg_ref.shape[0] // 32
     n = 16 * HALO
-    w_ref[0:n, :] = z_ref[0:n, :]
-    src_ref[0:16, :] = z_ref[n : n + 16, :]
     rest = 16 * (rows - HALO)
+    w_ref[0:n, :] = first_ref[0:n, :]
+    src_ref[0:16, :] = first_ref[n : n + 16, :]
 
     def build(first):
         for t in range(n_t):
@@ -581,7 +596,6 @@
     lanes = edge_tile(side, zr_ref.shape[1])
     lane = lane_iota()
     mine = ((lane >= LANES - HALO) & (side == 1)) | ((lane < HALO) & (side == 0))
-    zsrc = 16 * NEAR + ZMECH
     per = LANES // SPAN
 
     def strip(i):
@@ -589,19 +603,23 @@
         return pltpu.roll(x, LANES - SPAN * (i % per) - side * HALO, 1)
 
     def cell(j, kind):
-        x = zr_ref[16 * j + 8 * kind : 16 * j + 8 * kind + 8, lanes] if j < NEAR else strip(2 * (j - NEAR) + kind)
+        held = 2 + kind
+        if j < held:
+            at = (Z_TEMP, Z_CODE)[kind] + 8 * j
+            x = zr_ref[at : at + 8, lanes]
+        else:
+            x = strip(kind * (HALO - 2) + j - held)
         return jnp.where(mine, x, corners.cell(j, kind))
 
-    first = FAR_ROW - 2
     codes = {}
-    for j in range(first, HALO):
+    for j in range(HALO):
         codes[j] = cell(j, 1)
         (s,) = choose([v_s], codes[j])
-        s_ref[at8(j - first), :] = s
-        q0_ref[at8(j - first), :] = s * cell(j, 0)
+        s_ref[at8(j), :] = s
+        q0_ref[at8(j), :] = s * cell(j, 0)
     power = [
-        jnp.where(mine, zr_ref[zsrc : zsrc + 8, lanes], corners.power(0)),
-        jnp.where(mine, strip(2 * (HALO - NEAR)), corners.power(1)),
+        jnp.where(mine, zr_ref[Z_POWER : Z_POWER + 8, lanes], corners.power(0)),
+        jnp.where(mine, strip(2 * HALO - 5), corners.power(1)),
     ]
     top = sub_iota(LANES) == 0
     h = sink(LANES)
@@ -610,16 +628,18 @@
         x = power[j // 8][j % 8 : j % 8 + 1, :]
         return jnp.where(top, jnp.broadcast_to(x, (8, LANES)), 0.0)
 
-    for j in range(first + 1, HALO - 1):
-        at = at8(j - first)
-        di_ref[at, :], q1_ref[at, :] = first_sweep(s_ref, q0_ref, j - first, power_of(j), h)
-    out = []
+    heat = {}
+    for j in range(1, HALO - 1):
+        di_ref[at8(j), :], heat[j] = first_sweep(s_ref, q0_ref, j, power_of(j), h)
+        q1_ref[at8(j), :] = heat[j]
+
+    def expansion(j):
+        return lookup(t_al, codes[j]) * second_sweep(s_ref, q1_ref, di_ref, j, power_of(j))
+
+    out = [heat[1], heat[2], expansion(2)]
     for f in range(FAR):
-        x = None
-        for j in range(FAR_ROW + 3 * f, FAR_ROW + 3 * f + 3):
-            ea = lookup(t_al, codes[j]) * second_sweep(s_ref, q1_ref, di_ref, j - first, power_of(j))
-            x = ea if x is None else x + ea
-        out.append(restrict_sides(x))
+        j = FAR_ROW + 3 * f
+        out.append(restrict_sides(expansion(j) + expansion(j + 1) + expansion(j + 2)))
     return out
 
 
@@ -638,12 +658,10 @@
     wide = zr_ref.shape[1]
     half = wide // 2
     width = wide + LANES
+    mcols = mod_in.shape[1] - LANES
     t_s = jnp.sqrt(table_of(tab, 0))
     t_al = table_of(tab, 1)
     v_s = splats(t_s, NMAT)
-    zmech = 16 * NEAR
-    zsrc = zmech + ZMECH
-    zfar = zsrc + 8
     for g in range(3):
         k = AHEAD - 1 - g
         for dst, src in ((s_ref, s_in), (al_ref, al_in), (q0_ref, q0_in)):
@@ -654,7 +672,7 @@
     di_ref[at8(AHEAD - 2), :] = row8(di_in, FRONT + 1)
     n_p = s_ref.shape[0] // 8
     near = jnp.concatenate([src_ref[0:8, :], sides.power(0)], axis=1)
-    far = jnp.concatenate([zr_ref[zsrc : zsrc + 8, :], corners.power(0)], axis=1)
+    far = jnp.concatenate([zr_ref[Z_POWER : Z_POWER + 8, :], corners.power(0)], axis=1)
     spread_power(
         pw_ref,
         n_p,
@@ -662,23 +680,37 @@
     )
     h = sink(width)
 
-    for i in range(0, NEAR + 2 * STEP + 1, STEP):
-        later = []
-        for j in range(i, min(i + STEP, NEAR)):
-            temp = jnp.concatenate([zr_ref[16 * j : 16 * j + 8, :], corners.cell(j, 0)], axis=1)
-            code = jnp.concatenate([zr_ref[16 * j + 8 : 16 * j + 16, :], corners.cell(j, 1)], axis=1)
-            s, al = choose([v_s], code)[0], lookup(t_al, code)
-            later += [(s_ref, AHEAD + j, s), (q0_ref, AHEAD + j, s * temp), (al_ref, AHEAD + j, al)]
-        for j in range(max(-1, i - STEP - 1), min(i - 1, NEAR - 1)):
-            r = AHEAD + j
-            inv, q1 = first_sweep(s_ref, q0_ref, r, power_row(pw_ref, n_p, r), h)
-            later += [(di_ref, r, inv), (q1_ref, r, q1)]
-        for j in range(max(-2, i - 2 * STEP - 2), min(i - STEP - 2, NEAR - 2)):
-            r = AHEAD + j
-            t2 = second_sweep(s_ref, q1_ref, di_ref, r, power_row(pw_ref, n_p, r))
-            later += [(t_keep, r, t2), (ea_ref, r, row8(al_ref, r) * t2)]
-        for ref, r, x in later:
-            ref[at8(r), :] = x
+    lane = lane_iota()
+    has_left, has_right = sides.side > 0, sides.side < n_col - 1
+    patches = [edge_patch(n_edges, e, corners, zr_ref, mcols, v_s, t_al, rest[41:45]) for e in range(n_edges)]
+
+    def mend(x, k, near, reach):
+        pieces = tiles(x)
+        right, left = patches[0][k], patches[-1][k]
+        pieces[0] = jnp.where((lane < near) & has_left, left, pieces[0])
+        pieces[-1] = jnp.where((lane >= LANES - near) & has_right, right, pieces[-1])
+        beside = jnp.where((lane < reach) & has_right, right, jnp.where((lane >= LANES - reach) & has_left, left, 0.0))
+        return jnp.concatenate(pieces + [beside], axis=1)
+
+    for j in range(KEEP):
+        code = jnp.concatenate([zr_ref[Z_CODE + 8 * j : Z_CODE + 8 * j + 8, :], corners.cell(j, 1)], axis=1)
+        s = choose([v_s], code)[0]
+        s_ref[at8(AHEAD + j), :] = s
+        if j < 2:
+            temp = jnp.concatenate([zr_ref[Z_TEMP + 8 * j : Z_TEMP + 8 * j + 8, :], corners.cell(j, 0)], axis=1)
+            q0_ref[at8(AHEAD + j), :] = s * temp
+            al_ref[at8(AHEAD + j), :] = lookup(t_al, code)
+            at = Z_HEAT + 8 * j
+            q1_ref[at8(AHEAD + 1 + j), :] = mend(zr_ref[at : at + 8, :], j, KEEP, HALO)
+    for r in (AHEAD - 1, AHEAD):
+        di_ref[at8(r), :], q1_ref[at8(r), :] = first_sweep(s_ref, q0_ref, r, power_row(pw_ref, n_p, r), h)
+    r = AHEAD + 1
+    di_ref[at8(r), :] = 1.0 / (h + row8(s_ref, r) * conduct_sum(s_ref, r))
+    for r in range(AHEAD - 2, AHEAD + 2):
+        t2 = second_sweep(s_ref, q1_ref, di_ref, r, power_row(pw_ref, n_p, r))
+        t_keep[at8(r), :] = t2
+        ea_ref[at8(r), :] = row8(al_ref, r) * t2
+    ea_ref[at8(AHEAD + 2), :] = mend(zr_ref[Z_STRAIN : Z_STRAIN + 8, :], 2, KEEP, HALO)
 
     core = lax.axis_index(CORE)
 
@@ -697,22 +729,14 @@
     count = mod_in.shape[0] // 8
     mrows = count - MHALO
     mwidth = mod_in.shape[1]
-    mcols = mwidth - LANES
     n_m = count + MHALO
     for m in range(MHALO + 1 - FAR):
         i = AHEAD - 3 + 3 * m
         x = row8(ea_ref, i) + row8(ea_ref, i + 1) + row8(ea_ref, i + 2)
         st_ref[at8(MHALO - m), :] = restrict_columns(x)
-    lane = lane_iota()
-    has_left, has_right = sides.side > 0, sides.side < n_col - 1
-    patches = [edge_patch(n_edges, e, corners, zr_ref, mcols, v_s, t_al, rest[41:45]) for e in range(n_edges)]
     for f in range(FAR):
-        pieces = tiles(zr_ref[zfar : zfar + 8, mcols * f : mcols * (f + 1)])
-        right, left = patches[0][f], patches[-1][f]
-        pieces[0] = jnp.where((lane == 0) & has_left, left, pieces[0])
-        pieces[-1] = jnp.where((lane == LANES - 1) & has_right, right, pieces[-1])
-        beside = jnp.where((lane < MHALO) & has_right, right, jnp.where((lane >= LANES - MHALO) & has_left, left, 0.0))
-        st_ref[at8(FAR - 1 - f), :] = jnp.concatenate(pieces + [beside], axis=1)
+        x = zr_ref[Z_FAR : Z_FAR + 8, mcols * f : mcols * (f + 1)]
+        st_ref[at8(FAR - 1 - f), :] = mend(x, 3 + f, 1, MHALO)
     for m in range(1, count):
         st_ref[at8(MHALO + m), :] = row8(strain_in, m)
     values = splats(table_of(tab, 2), NMAT)
@@ -720,7 +744,7 @@
         j = MHALO - 1 - i
         fields = []
         for f in range(4):
-            body = zr_ref[zmech + ML * f : zmech + ML * f + 8, mcols * j : mcols * (j + 1)]
+            body = zr_ref[Z_SOLID + ML * f : Z_SOLID + ML * f + 8, mcols * j : mcols * (j + 1)]
             body = jnp.where(sub_iota(mcols) < ML, body, 0.0)
             side = corners.field(j, f)
             fields.append(jnp.concatenate([body, side], axis=1))
@@ -873,43 +897,47 @@
     n_far = 8 * far_rows(rows)
     cells, one = call(k_rows, [(16 * rows * n_t, LANES), ((n + 16) * n_t + n_far, LANES)], [both, ids])
     got1 = send(one, swap)
-    two, mg, strip = call(
+    two, mg = call(
         functools.partial(k_rest, n_edges),
         [
-            ((16 * (rows - HALO) + rows - 16) * n_t + 32 * MHALO * m_t, LANES),
+            ((16 * (rows - HALO) + rows - 16) * n_t + 32 * MHALO * m_t + 8 * n_edges, LANES),
             (32 * mrows, mcols),
-            (8 * n_edges, LANES),
         ],
         [both, cells, offset, mat],
         scratch=[(32 * mrows * m_t, LANES)],
     )
-    strip = send(strip, swap)
     got2 = send(two, swap)
     n_c = 32 + n_far - 8 * (-4 * (mrows - MHALO) * MSPAN // LANES) + 8
     z, first_rows, *edges = call(
         functools.partial(k_edge, n_edges),
-        [(far_place(n_edges, -1, wide, mcols)[0].stop, wide), (n + 16, wide)] + [(n_c, LANES), (32, LANES)] * n_edges,
-        [tab, both, cells, got1, mg, strip],
+        [(far_place(n_edges, -1, wide, mcols)[0].stop, wide), (n + 16, wide)] + [(32, LANES)] * n_edges,
+        [tab, both, cells, got1, mg],
         cost=EDGE_COST,
         scratch=[(8 * HALO, wide)] * 4,
     )
     leaving = [z, *edges]
-    w, src, mw, z, *edges = call(
-        functools.partial(k_chip, rows),
-        [(16 * rows, wide), (rows, wide), (32 * (mrows + MHALO), mcols)] + [x.shape for x in leaving],
-        [both, cells, got2, mg, first_rows] + leaving,
-        aliases={5 + k: 3 + k for k in range(len(leaving))},
+    leaving = call(
+        functools.partial(k_beside, n_edges, rows),
+        [(n_c, LANES)] * n_edges + [x.shape for x in leaving],
+        [both, cells, got1, got2, mg] + leaving,
+        aliases={5 + k: n_edges + k for k in range(len(leaving))},
     )
+    beside, z, near = leaving[:n_edges], leaving[n_edges], leaving[n_edges + 1 :]
     zr = send(z, along)
     if n_edges == 1:
-        sides = [send(edges[0], lambda r, c, a: (r, 1 - c, a))]
-        corners = [send(edges[1], lambda r, c, a: along(r, 1 - c, a))]
+        sides = [send(beside[0], lambda r, c, a: (r, 1 - c, a))]
+        corners = [send(near[0], lambda r, c, a: along(r, 1 - c, a))]
     else:
-        sides = [send(edges[0], lambda r, c, a: (r, c + 1, a)), send(edges[2], lambda r, c, a: (r, c - 1, a))]
+        sides = [send(beside[0], lambda r, c, a: (r, c + 1, a)), send(beside[1], lambda r, c, a: (r, c - 1, a))]
         corners = [
-            send(edges[1], lambda r, c, a: along(r, c + 1, a)),
-            send(edges[3], lambda r, c, a: along(r, c - 1, a)),
+            send(near[0], lambda r, c, a: along(r, c + 1, a)),
+            send(near[1], lambda r, c, a: along(r, c - 1, a)),
         ]
+    w, src, mw = call(
+        functools.partial(k_chip, rows),
+        [(16 * rows, wide), (rows, wide), (32 * (mrows + MHALO), mcols)],
+        [both, cells, got2, mg, first_rows],
+    )
     width = wide + LANES
     mwidth = mcols + LANES
     n_w = 8 * (rows + FRONT + 4)

time: 20.8 us -> 20.4 us (0.981)
  Pallas kernels: 6.62 us -> 6.3 us
    pallas_call x8 -> x9, Pallas kernels: 6.62 us -> 6.3 us  [call(): pl.pallas_call(kernel, out_shape=[jax.ShapeDtypeStruct(s, jnp.float32) fo...]
    ppermute x7 -> x6, starting transfers between devices: 9.19 us -> 9.03 us  [send(): return lax.ppermute(x, axes, pairs(dims, sends))]
    ppermute x7 -> x6, waiting for transfers between devices: 2.78 us -> 2.9 us  [send(): return lax.ppermute(x, axes, pairs(dims, sends))]
  transfers between devices with their start and end apart: 7 -> 6, of which waited for: 3 -> 3; matrix products, arithmetic and copies ran while one was open for 0% -> 0% of each run, Pallas kernels for 18% -> 19%
where the time goes in v5:
time: 20.4 us; the launch traced here: 20.3 us
  starting transfers between devices  9.03 us (44%)
  Pallas kernels  6.3 us (31%)
  waiting for transfers between devices  2.9 us (14%)
  other arithmetic  1.22 us (6%)
  between operations  0.79 us (4%)
    ppermute x6, starting transfers between devices, send(): return lax.ppermute(x, axes, pairs(dims, sends))  9.03 us
    pallas_call x9, Pallas kernels, call(): pl.pallas_call(kernel, out_shape=[jax.ShapeDtypeStruct(s, jnp.float32) fo...  6.3 us
    ppermute x6, waiting for transfers between devices, send(): return lax.ppermute(x, axes, pairs(dims, sends))  2.9 us
    select_n x1, other arithmetic, per_device(): both = jnp.where(kind == 0, temp[None], power[None, None])  1.14 us
  transfers between devices with their start and end apart: 6, of which 3 were waited for; matrix products, arithmetic and copies ran while one was open for 0% of the time, Pallas kernels for 19%

profile of v5, /device:TPU:0, one launch (start us, length us, event | category | flops | bytes accessed | tf_op | source)
XLA Modules:
  0.0 20.3 jit_solution(12724376408379730339)
XLA Ops:
  0.6 0.0 copy-start
  0.6 0.0 copy-start.2
  0.7 0.0 copy-start.1
  0.7 1.1 %broadcast_select_fusion.in_ref = f32[2,8,24,384]{3,2,1,0:T(8,128)S(1)} fusion(f32[24,384]{1,0:T(8,128)} %param.10, f32[8,24,384]{2,1,0:T(8,128)} %param.8, pred[2]{0:T(512)(128)(4,1)S(1)} %iota_compare_fusion.2), kind=kLoop, calls=%fused_computation | loop fusion | flops 147456 | bytes 921602 | tf_op jit(solution)/shard_map/jit(_where)/select_n | solution.py:893
  1.8 0.0 copy-done
  1.8 0.0 copy-start.3
  1.8 0.0 copy-start.4
  1.8 0.0 copy-start.5
  1.9 0.3 %shard_map.103 = (f32[1152,128]{1,0:T(8,128)S(1)}, f32[600,128]{1,0:T(8,128)S(1)}) custom-call(f32[2,8,24,384]{3,2,1,0:T(8,128)S(1)} %broadcast_select_fusion.in_ref, s32[8,24,384]{2,1,0:T(8,128)S(1)} %copy-done), custom_call_target="tpu_custom_call" | custom-call | tf_op jit(solution)/shard_map/pallas_call | solution.py:40
  2.2 0.5 %collective-permute-start.1 = (f32[600,128]{1,0:T(8,128)S(1)}, f32[600,128]{1,0:T(8,128)S(1)}, u32[]{:S(2)}, u32[]{:S(2)}) collective-permute-start(f32[600,128]{1,0:T(8,128)S(1)} %get-tuple-element.38), channel_id=1, source_target_pairs={{0,1},{1,0},{2,3},{3,2},{4,5},{5,4},{6,7},{7,6},{8,9},{9,8},{10,11... | collective-permute-start | bytes 921608 | tf_op jit(solution)/shard_map/ppermute | solution.py:882
  2.7 0.0 copy-done.2
  2.7 0.2 shard_map.104
  2.9 0.1 collective-permute-start
  3.0 0.0 copy-done.4
  3.0 0.1 select_maximum_fusion.tab
  3.1 0.8 %collective-permute-done.1.got_ref.one_ref = f32[600,128]{1,0:T(8,128)S(1)} collective-permute-done((f32[600,128]{1,0:T(8,128)S(1)}, f32[600,128]{1,0:T(8,128)S(1)}, u32[]{:S(2)}, u32[]{:S(2)}) %collective-permute-start.1) | collective-permute-done | bytes 307232 | tf_op jit(solution)/shard_map/ppermute | solution.py:882
  3.9 1.0 %shard_map.105 = (f32[104,768]{1,0:T(8,128)S(1)}, f32[192,768]{1,0:T(8,128)S(1)}, f32[32,128]{1,0:T(8,128)S(1)}) custom-call(f32[3,128]{1,0:T(4,128)S(1)} %select_maximum_fusion.tab, f32[2,8,24,384]{3,2,1,0:T(8,128)S(1)} %broadcast_select_fusion.in_ref, f32[1152,128]{1,0:T(8,128)S(1)} %get-tuple-element.35.a_ref, ...), custom_call_target="tpu_custom_call" | custom-call | flops 10000000000 | tf_op jit(solution)/shard_map/pallas_call | solution.py:40
  5.0 0.0 collective-permute-done.got_ref
  5.0 0.1 shard_map.107
  5.1 0.7 %collective-permute-start.3 = (f32[104,768]{1,0:T(8,128)S(1)}, f32[104,768]{1,0:T(8,128)S(1)}, u32[]{:S(2)}, u32[]{:S(2)}) collective-permute-start(f32[104,768]{1,0:T(8,128)S(1)} %get-tuple-element.46), channel_id=1, source_target_pairs={{1,4},{3,6},{4,1},{5,8},{6,3},{7,10},{8,5},{9,12},{10,7},{11,14},{... | collective-permute-start | bytes 958472 | tf_op jit(solution)/shard_map/ppermute | solution.py:882
  5.8 2.9 %collective-permute-start.2 = (f32[72,128]{1,0:T(8,128)S(1)}, f32[72,128]{1,0:T(8,128)S(1)}, u32[]{:S(2)}, u32[]{:S(2)}) collective-permute-start(f32[72,128]{1,0:T(8,128)S(1)} %get-tuple-element.44), channel_id=1, source_target_pairs={{0,2},{1,3},{2,0},{3,1},{4,6},{5,7},{6,4},{7,5},{8,10},{9,11},{10,... | collective-permute-start | bytes 110600 | tf_op jit(solution)/shard_map/ppermute | solution.py:882
  8.7 0.7 %collective-permute-start.4 = (f32[32,128]{1,0:T(8,128)S(1)}, f32[32,128]{1,0:T(8,128)S(1)}, u32[]{:S(2)}, u32[]{:S(2)}) collective-permute-start(f32[32,128]{1,0:T(8,128)S(1)} %get-tuple-element.47), channel_id=1, source_target_pairs={{1,6},{3,4},{4,3},{5,10},{6,1},{7,8},{8,7},{9,14},{10,5},{11,12},{... | collective-permute-start | bytes 49160 | tf_op jit(solution)/shard_map/ppermute | solution.py:882
  9.4 0.1 shard_map.106
  9.5 1.2 %collective-permute-done.2.refs_0_ = f32[72,128]{1,0:T(8,128)S(1)} collective-permute-done((f32[72,128]{1,0:T(8,128)S(1)}, f32[72,128]{1,0:T(8,128)S(1)}, u32[]{:S(2)}, u32[]{:S(2)}) %collective-permute-start.2) | collective-permute-done | bytes 36896 | tf_op jit(solution)/shard_map/ppermute | solution.py:882
  10.6 0.3 %shard_map.109 = (f32[56,384]{1,0:T(8,128)S(1)}, f32[56,384]{1,0:T(8,128)S(1)}, f32[56,384]{1,0:T(8,128)S(1)}, f32[56,384]{1,0:T(8,128)S(1)}, f32[56,384]{1,0:T(...) custom-call(f32[3,128]{1,0:T(4,128)S(1)} %select_maximum_fusion.tab, ...), custom_call_target="tpu_custom_call" | custom-call | tf_op jit(solution)/shard_map/pallas_call | solution.py:40
  11.0 2.2 %shard_map.108 = (f32[296,896]{1,0:T(8,128)S(1)}, f32[296,896]{1,0:T(8,128)S(1)}, f32[296,896]{1,0:T(8,128)S(1)}, f32[296,896]{1,0:T(8,128)S(1)}, f32[296,896]{1...) custom-call(f32[3,128]{1,0:T(4,128)S(1)} %select_maximum_fusion.tab, ...), custom_call_target="tpu_custom_call" | custom-call | tf_op jit(solution)/shard_map/pallas_call | solution.py:40
  13.2 0.0 collective-permute-done.4.refs_1_
  13.2 0.0 collective-permute-done.3.zr_ref
  13.2 1.2 %shard_map.110 = (f32[32,384]{1,0:T(8,128)S(1)}, f32[24,384]{1,0:T(8,128)S(1)}, f32[96,256]{1,0:T(8,128)S(1)}) custom-call(f32[3,128]{1,0:T(4,128)S(1)} %select_maximum_fusion.tab, f32[104,768]{1,0:T(8,128)S(1)} %collective-permute-done.3.zr_ref, f32[72,128]{1,0:T(8,128)S(1)} %collective-permute-done.2.refs_0_, ...), custom_call_target="tpu_custom_call" | custom-call | tf_op jit(solution)/shard_map/pallas_call | solution.py:40
  14.4 4.1 %collective-permute-start.5 = (f32[32,384]{1,0:T(8,128)S(1)}, f32[32,384]{1,0:T(8,128)S(1)}, u32[]{:S(2)}, u32[]{:S(2)}) collective-permute-start(f32[32,384]{1,0:T(8,128)S(1)} %get-tuple-element.65), channel_id=1, source_target_pairs={{0,1},{1,0},{2,3},{3,2},{4,5},{5,4},{6,7},{7,6},{8,9},{9,8},{10,11... | collective-permute-start | bytes 147464 | tf_op jit(solution)/shard_map/ppermute | solution.py:882
  18.6 0.9 %collective-permute-done.5.xr_ref = f32[32,384]{1,0:T(8,128)S(1)} collective-permute-done((f32[32,384]{1,0:T(8,128)S(1)}, f32[32,384]{1,0:T(8,128)S(1)}, u32[]{:S(2)}, u32[]{:S(2)}) %collective-permute-start.5) | collective-permute-done | bytes 49184 | tf_op jit(solution)/shard_map/ppermute | solution.py:882
  19.4 0.8 %shard_map.111 = (f32[8,24,384]{2,1,0:T(8,128)}, f32[3,6,4,256]{3,2,1,0:T(4,128)}, f32[24,384]{1,0:T(8,128)}) custom-call(f32[296,896]{1,0:T(8,128)S(1)} %get-tuple-element.45.refs_7_.t_in, f32[24,384]{1,0:T(8,128)S(1)} %get-tuple-element.64.keep_ref, f32[32,384]{1,0:T(8,128)S(1)} %collective-permute-done.5.xr_ref, f32[96,256]{1,0:T(8,128)S(1)} %get-tuple-element.66.u_in), custom_call_target="tpu_custom_call" | custom-call | tf_op jit(solution)/shard_map/pallas_call | solution.py:40
  (4 shorter events, 0.0 us)
Async XLA Ops:
  0.6 1.2 %copy-start = (s32[8,24,384]{2,1,0:T(8,128)S(1)}, s32[8,24,384]{2,1,0:T(8,128)}, u32[]{:S(2)}) copy-start(s32[8,24,384]{2,1,0:T(8,128)} %id_ref.1) | copy-start | bytes 884740
  0.6 2.1 %copy-start.2 = (s32[6,4,256]{2,1,0:T(4,128)S(1)}, s32[6,4,256]{2,1,0:T(4,128)}, u32[]{:S(2)}) copy-start(s32[6,4,256]{2,1,0:T(4,128)} %mat_ref.1) | copy-start | bytes 73732
  0.7 2.1 %copy-start.1 = (f32[3,6,4,256]{3,2,1,0:T(4,128)S(1)}, f32[3,6,4,256]{3,2,1,0:T(4,128)}, u32[]{:S(2)}) copy-start(f32[3,6,4,256]{3,2,1,0:T(4,128)} %u_ref.1) | copy-start | bytes 221188
  1.8 1.2 %copy-start.3 = (f32[16]{0:T(128)S(1)}, f32[16]{0:T(128)}, u32[]{:S(2)}) copy-start(f32[16]{0:T(128)} %param.15) | copy-start | bytes 196
  1.8 1.2 %copy-start.4 = (f32[16]{0:T(128)S(1)}, f32[16]{0:T(128)}, u32[]{:S(2)}) copy-start(f32[16]{0:T(128)} %param.14) | copy-start | bytes 196
  1.8 1.2 %copy-start.5 = (f32[16]{0:T(128)S(1)}, f32[16]{0:T(128)}, u32[]{:S(2)}) copy-start(f32[16]{0:T(128)} %param.13) | copy-start | bytes 196
  2.2 1.7 %collective-permute-start.1 = (f32[600,128]{1,0:T(8,128)S(1)}, f32[600,128]{1,0:T(8,128)S(1)}, u32[]{:S(2)}, u32[]{:S(2)}) collective-permute-start(f32[600,128]{1,0:T(8,128)S(1)} %get-tuple-element.38), channel_id=1, source_target_pairs={{0,1},{1,0},{2,3},{3,2},{4,5},{5,4},{6,7},{7,6},{8,9},{9,8},{10,11... | collective-permute-start | bytes 921608 | tf_op jit(solution)/shard_map/ppermute | solution.py:882
  2.9 2.1 %collective-permute-start = (f32[848,128]{1,0:T(8,128)S(1)}, f32[848,128]{1,0:T(8,128)S(1)}, u32[]{:S(2)}, u32[]{:S(2)}) collective-permute-start(f32[848,128]{1,0:T(8,128)S(1)} %get-tuple-element.36), channel_id=1, source_target_pairs={{0,1},{1,0},{2,3},{3,2},{4,5},{5,4},{6,7},{7,6},{8,9},{9,8},{10,11... | collective-permute-start | bytes 1302536 | tf_op jit(solution)/shard_map/ppermute | solution.py:882
  5.1 8.1 %collective-permute-start.3 = (f32[104,768]{1,0:T(8,128)S(1)}, f32[104,768]{1,0:T(8,128)S(1)}, u32[]{:S(2)}, u32[]{:S(2)}) collective-permute-start(f32[104,768]{1,0:T(8,128)S(1)} %get-tuple-element.46), channel_id=1, source_target_pairs={{1,4},{3,6},{4,1},{5,8},{6,3},{7,10},{8,5},{9,12},{10,7},{11,14},{... | collective-permute-start | bytes 958472 | tf_op jit(solution)/shard_map/ppermute | solution.py:882
  5.8 4.9 %collective-permute-start.2 = (f32[72,128]{1,0:T(8,128)S(1)}, f32[72,128]{1,0:T(8,128)S(1)}, u32[]{:S(2)}, u32[]{:S(2)}) collective-permute-start(f32[72,128]{1,0:T(8,128)S(1)} %get-tuple-element.44), channel_id=1, source_target_pairs={{0,2},{1,3},{2,0},{3,1},{4,6},{5,7},{6,4},{7,5},{8,10},{9,11},{10,... | collective-permute-start | bytes 110600 | tf_op jit(solution)/shard_map/ppermute | solution.py:882
  8.7 4.5 %collective-permute-start.4 = (f32[32,128]{1,0:T(8,128)S(1)}, f32[32,128]{1,0:T(8,128)S(1)}, u32[]{:S(2)}, u32[]{:S(2)}) collective-permute-start(f32[32,128]{1,0:T(8,128)S(1)} %get-tuple-element.47), channel_id=1, source_target_pairs={{1,6},{3,4},{4,3},{5,10},{6,1},{7,8},{8,7},{9,14},{10,5},{11,12},{... | collective-permute-start | bytes 49160 | tf_op jit(solution)/shard_map/ppermute | solution.py:882
  14.4 5.0 %collective-permute-start.5 = (f32[32,384]{1,0:T(8,128)S(1)}, f32[32,384]{1,0:T(8,128)S(1)}, u32[]{:S(2)}, u32[]{:S(2)}) collective-permute-start(f32[32,384]{1,0:T(8,128)S(1)} %get-tuple-element.65), channel_id=1, source_target_pairs={{0,1},{1,0},{2,3},{3,2},{4,5},{5,4},{6,7},{7,6},{8,9},{9,8},{10,11... | collective-permute-start | bytes 147464 | tf_op jit(solution)/shard_map/ppermute | solution.py:882

commit v6 on v5

--- a/solution.py
+++ b/solution.py
@@ -31,7 +31,7 @@
 EDGE_COST = 10**10
 FAR_ROW = 9 - 3 * FAR
 KEEP = 3
-Z_TEMP, Z_CODE, Z_HEAT, Z_STRAIN, Z_SOLID, Z_POWER, Z_FAR = 0, 16, 40, 56, 64, 88, 96
+Z_TEMP, Z_CODE, Z_HEAT, Z_STRAIN, Z_SUM, Z_SOLID, Z_POWER, Z_FAR = 0, 16, 40, 56, 64, 80, 104, 112
 CORE = "lay"
 UNROLL_STRAIN = 3
 
@@ -77,8 +77,20 @@
     return jnp.concatenate([gather_lanes(table, c.astype(jnp.int32)) for c in tiles(code)], axis=1)
 
 
-def splats(table, count):
-    return [jnp.broadcast_to(table[:, m : m + 1], (8, LANES)) for m in range(count + 1)]
+def k_tables(tab, out_ref):
+    for k, table in enumerate((jnp.sqrt(table_of(tab, 0)), table_of(tab, 2))):
+        for m in range(NMAT + 1):
+            at = 8 * ((NMAT + 1) * k + m)
+            out_ref[at : at + 8, :] = jnp.broadcast_to(table[:, m : m + 1], (8, LANES))
+    out_ref[16 * (NMAT + 1) : 16 * (NMAT + 1) + 8, :] = table_of(tab, 1)
+
+
+def splats(tab, k):
+    return [row8(tab, (NMAT + 1) * k + m) for m in range(NMAT + 1)]
+
+
+def expansion_table(tab):
+    return row8(tab, 2 * (NMAT + 1))
 
 
 def choose(lists, code):
@@ -171,10 +183,10 @@
             fields += [m_ref[pl.ds(pl.multiple_of(i + 8 * f, 8), 8), :] for f in range(4)]
         at = two_ref.shape[0] - 8 * (n_edges - e)
         (two_ref[at : at + 8, :],) = packed(side, fields, MSPAN, MHALO)
-    rest = 16 * (rows - HALO)
+    rest = 16 * (rows - 1 - HALO)
     for t in range(n_t):
         to = (rest + rows - 16) * t
-        for g in range(HALO, rows):
+        for g in range(HALO, rows - 1):
             i = 16 * (rows * t + turned(other, rows - 1, g))
             k = to + 16 * (g - HALO)
             two_ref[k : k + 16, :] = a_ref[pl.ds(pl.multiple_of(i, 16), 16), :]
@@ -230,14 +242,39 @@
     return -(-(2 * (rows - 1 - HALO) + rows // 8 - 2) // (LANES // SPAN))
 
 
-def k_edge(n_edges, tab, in_ref, a_ref, got_ref, mg_ref, z_ref, w_ref, *refs):
+def k_half(n_edges, tab, in_ref, a_ref, s_ref, q0_ref, al_ref, far_ref):
+    core = lax.axis_index(CORE)
+    rows = in_ref.shape[2]
+    n_t = in_ref.shape[3] // LANES
+    v_s = splats(tab, 0)
+    t_al = expansion_table(tab)
+    for t in range(n_t):
+        for g in range(HALO):
+            i = 16 * (rows * t + turned(core, rows - 1, g))
+            code = a_ref[pl.ds(pl.multiple_of(i + 8, 8), 8), :]
+            (x,) = choose([v_s], code)
+            s_ref[at8(g), tile_lanes(t)] = x
+            q0_ref[at8(g), tile_lanes(t)] = x * a_ref[pl.ds(pl.multiple_of(i, 16), 8), :]
+            if 2 <= g < 9:
+                al_ref[at8(g), tile_lanes(t)] = lookup(t_al, code)
+    for e in range(n_edges):
+        side = edge_side(n_edges, e)
+        for k, x in enumerate(far_strip(in_ref, a_ref, core, side * (n_t - 1), side)):
+            at = 8 * (far_rows(rows) * e + k)
+            far_ref[at : at + 8, :] = x
+
+
+def k_edge(n_edges, tab, in_ref, a_ref, got_ref, mg_ref, s_own, q0_own, al_own, z_ref, w_ref, *refs):
     core = lax.axis_index(CORE)
     wide = z_ref.shape[1]
-    n_t = wide // LANES // 2
+    half = wide // 2
+    n_t = half // LANES
     rows = in_ref.shape[2]
     mcols = mg_ref.shape[1]
     n = 16 * HALO
-    edge_refs, (s_ref, q0_ref, q1_ref, di_ref) = refs[:n_edges], refs[n_edges:]
+    edge_refs, (s_ref, q0_ref, al_ref, q1_ref, di_ref) = refs[:n_edges], refs[n_edges:]
+    v_s = splats(tab, 0)
+    t_al = expansion_table(tab)
 
     def build(first):
         for t in range(n_t):
@@ -250,6 +287,16 @@
             lanes = tile_lanes(n_t + t if first else t)
             at = (n + 16) * t
             w_ref[0 : n + 16, lanes] = got_ref[at : at + n + 16, :]
+            for g in range(HALO):
+                code = got_ref[at + 16 * g + 8 : at + 16 * g + 16, :]
+                (x,) = choose([v_s], code)
+                s_ref[at8(g), lanes] = x
+                q0_ref[at8(g), lanes] = x * got_ref[at + 16 * g : at + 16 * g + 8, :]
+                if 2 <= g < 9:
+                    al_ref[at8(g), lanes] = lookup(t_al, code)
+        lanes = slice(0, half) if first else slice(half, wide)
+        for dst, src in ((s_ref, s_own), (q0_ref, q0_own), (al_ref, al_own)):
+            dst[:, lanes] = src[...]
 
     @pl.when(core == 0)
     def _():
@@ -278,18 +325,9 @@
         near = packed(side, blocks, SPAN, HALO) + packed(side, fields, MSPAN, MHALO)
         strip = blocks[4 : 2 * HALO : 2] + blocks[7 : 2 * HALO : 2] + blocks[2 * HALO + 1 :]
         for k, x in enumerate(packed(side, strip, SPAN, HALO)):
-            z_ref[far_place(e, k, wide, mcols)] = x
+            z_ref[far_place(e, k, wide)] = x
         for k, x in enumerate(near):
             edge_refs[e][8 * k : 8 * k + 8, :] = x
-    t_s = jnp.sqrt(table_of(tab, 0))
-    t_al = table_of(tab, 1)
-    v_s = splats(t_s, NMAT)
-    codes = {}
-    for g in range(HALO):
-        codes[g] = w_ref[16 * g + 8 : 16 * g + 16, :]
-        x = lookup(t_s, codes[g]) if g % 2 else choose([v_s], codes[g])[0]
-        s_ref[at8(g), :] = x
-        q0_ref[at8(g), :] = x * w_ref[16 * g : 16 * g + 8, :]
     h = sink(wide)
     top = sub_iota(wide) == 0
     powers = {
@@ -300,29 +338,28 @@
     z_ref[Z_HEAT : Z_HEAT + 16, :] = q1_ref[8:24, :]
 
     def expansion(g):
-        return lookup(t_al, codes[g]) * second_sweep(s_ref, q1_ref, di_ref, g, powers[g], True)
+        return row8(al_ref, g) * second_sweep(s_ref, q1_ref, di_ref, g, powers[g], True)
 
     z_ref[Z_STRAIN : Z_STRAIN + 8, :] = expansion(2)
     for f in range(FAR):
         g = FAR_ROW + 3 * f
         x = expansion(g) + expansion(g + 1) + expansion(g + 2)
-        z_ref[Z_FAR : Z_FAR + 8, mcols * f : mcols * (f + 1)] = restrict_main(x)
+        z_ref[Z_SUM + 8 * f : Z_SUM + 8 * f + 8, :] = x
 
 
 def far_tiles():
     return -(-(2 * HALO - 4) // (LANES // SPAN))
 
 
-def far_place(e, k, wide, mcols):
-    q = FAR * mcols // LANES + far_tiles() * e + k
+def far_place(e, k, wide):
+    q = far_tiles() * e + k
     at = Z_FAR + 8 * (q // (wide // LANES))
     return slice(at, at + 8), tile_lanes(q % (wide // LANES))
 
 
-def k_beside(n_edges, rows, in_ref, a_ref, one_ref, got_ref, mg_ref, z_ref, *refs):
+def k_beside(n_edges, rows, n_t, far_ref, one_ref, got_ref, mg_ref, z_ref, *refs):
     near_refs, c_refs = refs[:n_edges], refs[n_edges : 2 * n_edges]
     core = lax.axis_index(CORE)
-    n_t = in_ref.shape[3] // LANES
     mrows = mg_ref.shape[0] // 32
     n = 16 * HALO
     for e in range(n_edges):
@@ -330,8 +367,9 @@
         mlanes = edge_tile(side, mg_ref.shape[1])
         fields = [mg_ref[8 * i : 8 * i + 8, mlanes] for i in range(4 * MHALO, 4 * mrows)]
         far = [near_refs[e][8 * k : 8 * k + 8, :] for k in range(4)]
-        for k, x in enumerate(far_strip(in_ref, a_ref, core, side * (n_t - 1), side)):
+        for k in range(far_rows(rows)):
             at = (n + 16) * n_t + 8 * k
+            x = row8(far_ref, far_rows(rows) * e + k)
             far.append(jnp.where(core == side, x, one_ref[at : at + 8, :]))
         far += packed(side, fields, MSPAN, MHALO)
         at = got_ref.shape[0] - 8 * (n_edges - e)
@@ -345,14 +383,14 @@
     n_t = w_ref.shape[1] // LANES // 2
     mrows = mg_ref.shape[0] // 32
     n = 16 * HALO
-    rest = 16 * (rows - HALO)
+    rest = 16 * (rows - 1 - HALO)
     w_ref[0:n, :] = first_ref[0:n, :]
     src_ref[0:16, :] = first_ref[n : n + 16, :]
 
     def build(first):
         for t in range(n_t):
             lanes = tile_lanes(t if first else n_t + t)
-            for g in range(HALO, rows):
+            for g in range(HALO, rows - 1):
                 i = 16 * (rows * t + (g if first else rows - 1 - g))
                 w_ref[16 * g : 16 * g + 16, lanes] = a_ref[i : i + 16, :]
             for b in range(2, rows // 8):
@@ -455,44 +493,36 @@
     return jnp.where(sub_iota(width) == DEPTH - 1, 2.0, 0.2).astype(jnp.float32)
 
 
-def column_sums(x):
-    width = x.shape[1]
-    return x + pltpu.roll(x, width - 1, 1) + pltpu.roll(x, width - 2, 1)
-
-
 def to_solid_layers(y):
     return jnp.where(sub_iota(y.shape[1]) < 3, y, next_sub(y)) * (1.0 / 9.0)
 
 
 def gather_main(pieces):
-    lane = lane_iota()
+    lane = 3 * lane_iota()
     out = []
     for j in range(len(pieces) // 3):
-        got = None
-        for t in range(3):
-            g = gather_lanes(pieces[3 * j + t], (3 * lane) & (LANES - 1))
-            got = g if got is None else jnp.where((3 * lane) >= LANES * t, g, got)
-        out.append(got)
+        total = None
+        for k in range(3):
+            got = None
+            for t in range(3):
+                g = gather_lanes(pieces[3 * j + t], (lane + k) & (LANES - 1))
+                got = g if got is None else jnp.where(lane + k >= LANES * t, g, got)
+            total = got if total is None else total + got
+        out.append(total)
     return out
 
 
 def gather_sides(piece):
     lane = lane_iota()
     first = LANES - MHALO
-    index = jnp.where(lane < MHALO, 3 * lane, jnp.where(lane >= first, LANES - 9 + 3 * (lane - first), 64))
-    return gather_lanes(piece, index)
-
-
-def restrict_main(x):
-    return to_solid_layers(jnp.concatenate(gather_main(tiles(column_sums(x))), axis=1))
-
-
-def restrict_sides(x):
-    return to_solid_layers(gather_sides(column_sums(x)))
+    inside = (lane < MHALO) | (lane >= first)
+    index = jnp.where(lane < MHALO, 3 * lane, jnp.where(lane >= first, LANES - 9 + 3 * (lane - first), 0))
+    total = gather_lanes(piece, index) + gather_lanes(piece, index + 1) + gather_lanes(piece, index + 2)
+    return jnp.where(inside, total, 0.0)
 
 
 def restrict_columns(x):
-    pieces = tiles(column_sums(x))
+    pieces = tiles(x)
     return to_solid_layers(jnp.concatenate(gather_main(pieces[:-1]) + [gather_sides(pieces[-1])], axis=1))
 
 
@@ -511,9 +541,8 @@
     s_ref, al_ref, q0_ref, q1_ref, di_ref, t_ref, ea_ref, strain_ref, pw_ref = refs[n_edges:]
     own = rows - 1
     width = src_ref.shape[1] + LANES
-    t_s = jnp.sqrt(table_of(tab, 0))
-    t_al = table_of(tab, 1)
-    v_s = splats(t_s, NMAT)
+    t_al = expansion_table(tab)
+    v_s = splats(tab, 0)
     side_power = jnp.concatenate([sides.power(k) for k in range(rows // 8)], axis=0)
     n_p = s_ref.shape[0] // 8
     spread_power(pw_ref, n_p, [(FRONT, jnp.concatenate([src_ref[...], side_power], axis=1))])
@@ -574,7 +603,7 @@
     mi_ref, mod_ref = refs[n_edges : n_edges + 2]
     uu_refs = refs[n_edges + 2 : n_edges + 5]
     pre_refs = refs[n_edges + 5 : n_edges + 8]
-    values = splats(table_of(tab, 2), NMAT)
+    values = splats(tab, 1)
     count = mw_ref.shape[0] // 32
     for m in range(count):
         fields = []
@@ -590,7 +619,7 @@
             pre_refs[d][at8(m), :] = near[d] * (1.0 / STIFF_DIAG) - row8(uu_refs[d], m)
 
 
-def edge_patch(n_edges, e, corners, zr_ref, mcols, v_s, t_al, scratch):
+def edge_patch(n_edges, e, corners, zr_ref, v_s, t_al, scratch):
     s_ref, q0_ref, q1_ref, di_ref = scratch
     side = edge_side(n_edges, e)
     lanes = edge_tile(side, zr_ref.shape[1])
@@ -599,7 +628,7 @@
     per = LANES // SPAN
 
     def strip(i):
-        x = zr_ref[far_place(e, i // per, zr_ref.shape[1], mcols)]
+        x = zr_ref[far_place(e, i // per, zr_ref.shape[1])]
         return pltpu.roll(x, LANES - SPAN * (i % per) - side * HALO, 1)
 
     def cell(j, kind):
@@ -639,7 +668,7 @@
     out = [heat[1], heat[2], expansion(2)]
     for f in range(FAR):
         j = FAR_ROW + 3 * f
-        out.append(restrict_sides(expansion(j) + expansion(j + 1) + expansion(j + 2)))
+        out.append(expansion(j) + expansion(j + 1) + expansion(j + 2))
     return out
 
 
@@ -659,9 +688,8 @@
     half = wide // 2
     width = wide + LANES
     mcols = mod_in.shape[1] - LANES
-    t_s = jnp.sqrt(table_of(tab, 0))
-    t_al = table_of(tab, 1)
-    v_s = splats(t_s, NMAT)
+    t_al = expansion_table(tab)
+    v_s = splats(tab, 0)
     for g in range(3):
         k = AHEAD - 1 - g
         for dst, src in ((s_ref, s_in), (al_ref, al_in), (q0_ref, q0_in)):
@@ -682,7 +710,7 @@
 
     lane = lane_iota()
     has_left, has_right = sides.side > 0, sides.side < n_col - 1
-    patches = [edge_patch(n_edges, e, corners, zr_ref, mcols, v_s, t_al, rest[41:45]) for e in range(n_edges)]
+    patches = [edge_patch(n_edges, e, corners, zr_ref, v_s, t_al, rest[41:45]) for e in range(n_edges)]
 
     def mend(x, k, near, reach):
         pieces = tiles(x)
@@ -735,11 +763,11 @@
         x = row8(ea_ref, i) + row8(ea_ref, i + 1) + row8(ea_ref, i + 2)
         st_ref[at8(MHALO - m), :] = restrict_columns(x)
     for f in range(FAR):
-        x = zr_ref[Z_FAR : Z_FAR + 8, mcols * f : mcols * (f + 1)]
-        st_ref[at8(FAR - 1 - f), :] = mend(x, 3 + f, 1, MHALO)
+        at = Z_SUM + 8 * f
+        st_ref[at8(FAR - 1 - f), :] = restrict_columns(mend(zr_ref[at : at + 8, :], 3 + f, KEEP, HALO))
     for m in range(1, count):
         st_ref[at8(MHALO + m), :] = row8(strain_in, m)
-    values = splats(table_of(tab, 2), NMAT)
+    values = splats(tab, 1)
     for i in range(MHALO):
         j = MHALO - 1 - i
         fields = []
@@ -893,6 +921,7 @@
     both = jnp.where(kind == 0, temp[None], power[None, None])
     tab = jnp.stack([heat_table, growth_table, modulus_table])
     tab = jnp.pad(tab, ((0, 0), (1, LANES - 1 - tab.shape[1])))
+    (tab,) = call(k_tables, [(16 * (NMAT + 1) + 8, LANES)], [tab])
     n = 16 * HALO
     n_far = 8 * far_rows(rows)
     cells, one = call(k_rows, [(16 * rows * n_t, LANES), ((n + 16) * n_t + n_far, LANES)], [both, ids])
@@ -900,27 +929,32 @@
     two, mg = call(
         functools.partial(k_rest, n_edges),
         [
-            ((16 * (rows - HALO) + rows - 16) * n_t + 32 * MHALO * m_t + 8 * n_edges, LANES),
+            ((16 * (rows - 1 - HALO) + rows - 16) * n_t + 32 * MHALO * m_t + 8 * n_edges, LANES),
             (32 * mrows, mcols),
         ],
         [both, cells, offset, mat],
         scratch=[(32 * mrows * m_t, LANES)],
     )
     got2 = send(two, swap)
+    *own_part, far = call(
+        functools.partial(k_half, n_edges),
+        [(8 * HALO, half)] * 3 + [(n_far * n_edges, LANES)],
+        [tab, both, cells],
+    )
     n_c = 32 + n_far - 8 * (-4 * (mrows - MHALO) * MSPAN // LANES) + 8
     z, first_rows, *edges = call(
         functools.partial(k_edge, n_edges),
-        [(far_place(n_edges, -1, wide, mcols)[0].stop, wide), (n + 16, wide)] + [(32, LANES)] * n_edges,
-        [tab, both, cells, got1, mg],
+        [(far_place(n_edges, -1, wide)[0].stop, wide), (n + 16, wide)] + [(32, LANES)] * n_edges,
+        [tab, both, cells, got1, mg, *own_part],
         cost=EDGE_COST,
-        scratch=[(8 * HALO, wide)] * 4,
+        scratch=[(8 * HALO, wide)] * 5,
     )
     leaving = [z, *edges]
     leaving = call(
-        functools.partial(k_beside, n_edges, rows),
+        functools.partial(k_beside, n_edges, rows, n_t),
         [(n_c, LANES)] * n_edges + [x.shape for x in leaving],
-        [both, cells, got1, got2, mg] + leaving,
-        aliases={5 + k: n_edges + k for k in range(len(leaving))},
+        [far, got1, got2, mg] + leaving,
+        aliases={4 + k: n_edges + k for k in range(len(leaving))},
     )
     beside, z, near = leaving[:n_edges], leaving[n_edges], leaving[n_edges + 1 :]
     zr = send(z, along)
@@ -935,7 +969,7 @@
         ]
     w, src, mw = call(
         functools.partial(k_chip, rows),
-        [(16 * rows, wide), (rows, wide), (32 * (mrows + MHALO), mcols)],
+        [(16 * own, wide), (rows, wide), (32 * (mrows + MHALO), mcols)],
         [both, cells, got2, mg, first_rows],
     )
     width = wide + LANES

time: 20.4 us -> 20 us (0.980)
  waiting for transfers between devices: 2.9 us -> 2.61 us
    ppermute x6, waiting for transfers between devices: 2.9 us -> 2.61 us  [send(): return lax.ppermute(x, axes, pairs(dims, sends))]
    pallas_call x9 -> x11, Pallas kernels: 6.3 us -> 6.24 us  [call(): pl.pallas_call(kernel, out_shape=[jax.ShapeDtypeStruct(s, jnp.float32) fo...]
  transfers between devices with their start and end apart: 6 -> 6, of which waited for: 3 -> 4; matrix products, arithmetic and copies ran while one was open for 0% -> 0% of each run, Pallas kernels for 19% -> 20%
where the time goes in v6:
time: 20 us; the launch traced here: 19.8 us
  starting transfers between devices  8.91 us (45%)
  Pallas kernels  6.24 us (31%)
  waiting for transfers between devices  2.61 us (13%)
  other arithmetic  1.22 us (6%)
  between operations  0.79 us (4%)
    ppermute x6, starting transfers between devices, send(): return lax.ppermute(x, axes, pairs(dims, sends))  8.91 us
    pallas_call x11, Pallas kernels, call(): pl.pallas_call(kernel, out_shape=[jax.ShapeDtypeStruct(s, jnp.float32) fo...  6.24 us
    ppermute x6, waiting for transfers between devices, send(): return lax.ppermute(x, axes, pairs(dims, sends))  2.61 us
    select_n x1, other arithmetic, per_device(): both = jnp.where(kind == 0, temp[None], power[None, None])  1.14 us
  transfers between devices with their start and end apart: 6, of which 4 were waited for; matrix products, arithmetic and copies ran while one was open for 0% of the time, Pallas kernels for 20%

profile of v6, /device:TPU:0, one launch (start us, length us, event | category | flops | bytes accessed | tf_op | source)
XLA Modules:
  0.0 19.8 jit_solution(2707945574829757339)
XLA Ops:
  0.6 0.0 copy-start
  0.6 0.0 copy-start.2
  0.7 1.1 %broadcast_select_fusion.in_ref = f32[2,8,24,384]{3,2,1,0:T(8,128)S(1)} fusion(f32[24,384]{1,0:T(8,128)} %param.10, f32[8,24,384]{2,1,0:T(8,128)} %param.8, pred[2]{0:T(512)(128)(4,1)S(1)} %iota_compare_fusion.2), kind=kLoop, calls=%fused_computation | loop fusion | flops 147456 | bytes 921602 | tf_op jit(solution)/shard_map/jit(_where)/select_n | solution.py:921
  1.8 0.0 copy-done
  1.8 0.0 copy-start.3
  1.8 0.0 copy-start.4
  1.8 0.0 copy-start.5
  1.9 0.3 %shard_map.104 = (f32[1152,128]{1,0:T(8,128)S(1)}, f32[600,128]{1,0:T(8,128)S(1)}) custom-call(f32[2,8,24,384]{3,2,1,0:T(8,128)S(1)} %broadcast_select_fusion.in_ref, s32[8,24,384]{2,1,0:T(8,128)S(1)} %copy-done), custom_call_target="tpu_custom_call" | custom-call | tf_op jit(solution)/shard_map/pallas_call | solution.py:40
  2.2 0.5 %collective-permute-start.1 = (f32[600,128]{1,0:T(8,128)S(1)}, f32[600,128]{1,0:T(8,128)S(1)}, u32[]{:S(2)}, u32[]{:S(2)}) collective-permute-start(f32[600,128]{1,0:T(8,128)S(1)} %get-tuple-element.42), channel_id=1, source_target_pairs={{0,1},{1,0},{2,3},{3,2},{4,5},{5,4},{6,7},{7,6},{8,9},{9,8},{10,11... | collective-permute-start | bytes 921608 | tf_op jit(solution)/shard_map/ppermute | solution.py:910
  2.7 0.2 shard_map.105
  2.9 0.1 collective-permute-start
  3.0 0.0 copy-done.5
  3.0 0.1 select_maximum_fusion.tab
  3.1 0.1 shard_map.103.tab
  3.2 0.2 %shard_map.106 = (f32[88,384]{1,0:T(8,128)S(1)}, f32[88,384]{1,0:T(8,128)S(1)}, f32[88,384]{1,0:T(8,128)S(1)}, f32[24,128]{1,0:T(8,128)S(1)}) custom-call(f32[280,128]{1,0:T(8,128)S(1)} %shard_map.103.tab, f32[2,8,24,384]{3,2,1,0:T(8,128)S(1)} %broadcast_select_fusion.in_ref, f32[1152,128]{1,0:T(8,128)S(1)} %get-tuple-element.39.a_ref), custom_call_target="tpu_custom_call" | custom-call | tf_op jit(solution)/shard_map/pallas_call | solution.py:40
  3.5 0.5 %collective-permute-done.1.got_ref.one_ref = f32[600,128]{1,0:T(8,128)S(1)} collective-permute-done((f32[600,128]{1,0:T(8,128)S(1)}, f32[600,128]{1,0:T(8,128)S(1)}, u32[]{:S(2)}, u32[]{:S(2)}) %collective-permute-start.1) | collective-permute-done | bytes 307232 | tf_op jit(solution)/shard_map/ppermute | solution.py:910
  3.9 0.7 %shard_map.107 = (f32[120,768]{1,0:T(8,128)S(1)}, f32[192,768]{1,0:T(8,128)S(1)}, f32[32,128]{1,0:T(8,128)S(1)}) custom-call(f32[280,128]{1,0:T(8,128)S(1)} %shard_map.103.tab, f32[2,8,24,384]{3,2,1,0:T(8,128)S(1)} %broadcast_select_fusion.in_ref, f32[1152,128]{1,0:T(8,128)S(1)} %get-tuple-element.39.a_ref, ...), custom_call_target="tpu_custom_call" | custom-call | flops 10000000000 | tf_op jit(solution)/shard_map/pallas_call | solution.py:40
  4.6 0.1 collective-permute-done.got_ref
  4.7 0.1 shard_map.109
  4.8 0.7 %collective-permute-start.3 = (f32[120,768]{1,0:T(8,128)S(1)}, f32[120,768]{1,0:T(8,128)S(1)}, u32[]{:S(2)}, u32[]{:S(2)}) collective-permute-start(f32[120,768]{1,0:T(8,128)S(1)} %get-tuple-element.54), channel_id=1, source_target_pairs={{1,4},{3,6},{4,1},{5,8},{6,3},{7,10},{8,5},{9,12},{10,7},{11,14},{... | collective-permute-start | bytes 1105928 | tf_op jit(solution)/shard_map/ppermute | solution.py:910
  5.5 2.9 %collective-permute-start.2 = (f32[72,128]{1,0:T(8,128)S(1)}, f32[72,128]{1,0:T(8,128)S(1)}, u32[]{:S(2)}, u32[]{:S(2)}) collective-permute-start(f32[72,128]{1,0:T(8,128)S(1)} %get-tuple-element.52), channel_id=1, source_target_pairs={{0,2},{1,3},{2,0},{3,1},{4,6},{5,7},{6,4},{7,5},{8,10},{9,11},{10,... | collective-permute-start | bytes 110600 | tf_op jit(solution)/shard_map/ppermute | solution.py:910
  8.3 0.7 %collective-permute-start.4 = (f32[32,128]{1,0:T(8,128)S(1)}, f32[32,128]{1,0:T(8,128)S(1)}, u32[]{:S(2)}, u32[]{:S(2)}) collective-permute-start(f32[32,128]{1,0:T(8,128)S(1)} %get-tuple-element.55), channel_id=1, source_target_pairs={{1,6},{3,4},{4,3},{5,10},{6,1},{7,8},{8,7},{9,14},{10,5},{11,12},{... | collective-permute-start | bytes 49160 | tf_op jit(solution)/shard_map/ppermute | solution.py:910
  9.0 0.1 shard_map.108
  9.1 1.2 %collective-permute-done.2.refs_0_ = f32[72,128]{1,0:T(8,128)S(1)} collective-permute-done((f32[72,128]{1,0:T(8,128)S(1)}, f32[72,128]{1,0:T(8,128)S(1)}, u32[]{:S(2)}, u32[]{:S(2)}) %collective-permute-start.2) | collective-permute-done | bytes 36896 | tf_op jit(solution)/shard_map/ppermute | solution.py:910
  10.3 0.3 %shard_map.111 = (f32[56,384]{1,0:T(8,128)S(1)}, f32[56,384]{1,0:T(8,128)S(1)}, f32[56,384]{1,0:T(8,128)S(1)}, f32[56,384]{1,0:T(8,128)S(1)}, f32[56,384]{1,0:T(...) custom-call(f32[280,128]{1,0:T(8,128)S(1)} %shard_map.103.tab, ...), custom_call_target="tpu_custom_call" | custom-call | tf_op jit(solution)/shard_map/pallas_call | solution.py:40
  10.6 2.3 %shard_map.110 = (f32[296,896]{1,0:T(8,128)S(1)}, f32[296,896]{1,0:T(8,128)S(1)}, f32[296,896]{1,0:T(8,128)S(1)}, f32[296,896]{1,0:T(8,128)S(1)}, f32[296,896]{1...) custom-call(f32[280,128]{1,0:T(8,128)S(1)} %shard_map.103.tab, ...), custom_call_target="tpu_custom_call" | custom-call | tf_op jit(solution)/shard_map/pallas_call | solution.py:40
  12.9 0.0 collective-permute-done.4.refs_1_
  12.9 0.0 collective-permute-done.3.zr_ref
  12.9 1.1 %shard_map.112 = (f32[32,384]{1,0:T(8,128)S(1)}, f32[24,384]{1,0:T(8,128)S(1)}, f32[96,256]{1,0:T(8,128)S(1)}) custom-call(f32[280,128]{1,0:T(8,128)S(1)} %shard_map.103.tab, f32[120,768]{1,0:T(8,128)S(1)} %collective-permute-done.3.zr_ref, f32[72,128]{1,0:T(8,128)S(1)} %collective-permute-done.2.refs_0_, f32[32,128]{1,0:T(8,128)S(1)} %collective-permute-done.4.refs_1_, ...), custom_call_target="tpu_custom_call" | custom-call | tf_op jit(solution)/shard_map/pallas_call | solution.py:40
  14.0 4.1 %collective-permute-start.5 = (f32[32,384]{1,0:T(8,128)S(1)}, f32[32,384]{1,0:T(8,128)S(1)}, u32[]{:S(2)}, u32[]{:S(2)}) collective-permute-start(f32[32,384]{1,0:T(8,128)S(1)} %get-tuple-element.73), channel_id=1, source_target_pairs={{0,1},{1,0},{2,3},{3,2},{4,5},{5,4},{6,7},{7,6},{8,9},{9,8},{10,11... | collective-permute-start | bytes 147464 | tf_op jit(solution)/shard_map/ppermute | solution.py:910
  18.1 0.9 %collective-permute-done.5.xr_ref = f32[32,384]{1,0:T(8,128)S(1)} collective-permute-done((f32[32,384]{1,0:T(8,128)S(1)}, f32[32,384]{1,0:T(8,128)S(1)}, u32[]{:S(2)}, u32[]{:S(2)}) %collective-permute-start.5) | collective-permute-done | bytes 49184 | tf_op jit(solution)/shard_map/ppermute | solution.py:910
  19.0 0.8 %shard_map.113 = (f32[8,24,384]{2,1,0:T(8,128)}, f32[3,6,4,256]{3,2,1,0:T(4,128)}, f32[24,384]{1,0:T(8,128)}) custom-call(f32[296,896]{1,0:T(8,128)S(1)} %get-tuple-element.53.refs_7_.t_in, f32[24,384]{1,0:T(8,128)S(1)} %get-tuple-element.72.keep_ref, f32[32,384]{1,0:T(8,128)S(1)} %collective-permute-done.5.xr_ref, f32[96,256]{1,0:T(8,128)S(1)} %get-tuple-element.74.u_in), custom_call_target="tpu_custom_call" | custom-call | tf_op jit(solution)/shard_map/pallas_call | solution.py:40
  (6 shorter events, 0.0 us)
Async XLA Ops:
  0.6 1.2 %copy-start = (s32[8,24,384]{2,1,0:T(8,128)S(1)}, s32[8,24,384]{2,1,0:T(8,128)}, u32[]{:S(2)}) copy-start(s32[8,24,384]{2,1,0:T(8,128)} %id_ref.1) | copy-start | bytes 884740
  0.6 2.1 %copy-start.2 = (s32[6,4,256]{2,1,0:T(4,128)S(1)}, s32[6,4,256]{2,1,0:T(4,128)}, u32[]{:S(2)}) copy-start(s32[6,4,256]{2,1,0:T(4,128)} %mat_ref.1) | copy-start | bytes 73732
  0.7 2.1 %copy-start.1 = (f32[3,6,4,256]{3,2,1,0:T(4,128)S(1)}, f32[3,6,4,256]{3,2,1,0:T(4,128)}, u32[]{:S(2)}) copy-start(f32[3,6,4,256]{3,2,1,0:T(4,128)} %u_ref.1) | copy-start | bytes 221188
  1.8 1.2 %copy-start.3 = (f32[16]{0:T(128)S(1)}, f32[16]{0:T(128)}, u32[]{:S(2)}) copy-start(f32[16]{0:T(128)} %param.15) | copy-start | bytes 196
  1.8 1.2 %copy-start.4 = (f32[16]{0:T(128)S(1)}, f32[16]{0:T(128)}, u32[]{:S(2)}) copy-start(f32[16]{0:T(128)} %param.14) | copy-start | bytes 196
  1.8 1.2 %copy-start.5 = (f32[16]{0:T(128)S(1)}, f32[16]{0:T(128)}, u32[]{:S(2)}) copy-start(f32[16]{0:T(128)} %param.13) | copy-start | bytes 196
  2.2 1.7 %collective-permute-start.1 = (f32[600,128]{1,0:T(8,128)S(1)}, f32[600,128]{1,0:T(8,128)S(1)}, u32[]{:S(2)}, u32[]{:S(2)}) collective-permute-start(f32[600,128]{1,0:T(8,128)S(1)} %get-tuple-element.42), channel_id=1, source_target_pairs={{0,1},{1,0},{2,3},{3,2},{4,5},{5,4},{6,7},{7,6},{8,9},{9,8},{10,11... | collective-permute-start | bytes 921608 | tf_op jit(solution)/shard_map/ppermute | solution.py:910
  2.9 1.8 %collective-permute-start = (f32[800,128]{1,0:T(8,128)S(1)}, f32[800,128]{1,0:T(8,128)S(1)}, u32[]{:S(2)}, u32[]{:S(2)}) collective-permute-start(f32[800,128]{1,0:T(8,128)S(1)} %get-tuple-element.40), channel_id=1, source_target_pairs={{0,1},{1,0},{2,3},{3,2},{4,5},{5,4},{6,7},{7,6},{8,9},{9,8},{10,11... | collective-permute-start | bytes 1228808 | tf_op jit(solution)/shard_map/ppermute | solution.py:910
  4.8 8.1 %collective-permute-start.3 = (f32[120,768]{1,0:T(8,128)S(1)}, f32[120,768]{1,0:T(8,128)S(1)}, u32[]{:S(2)}, u32[]{:S(2)}) collective-permute-start(f32[120,768]{1,0:T(8,128)S(1)} %get-tuple-element.54), channel_id=1, source_target_pairs={{1,4},{3,6},{4,1},{5,8},{6,3},{7,10},{8,5},{9,12},{10,7},{11,14},{... | collective-permute-start | bytes 1105928 | tf_op jit(solution)/shard_map/ppermute | solution.py:910
  5.5 4.8 %collective-permute-start.2 = (f32[72,128]{1,0:T(8,128)S(1)}, f32[72,128]{1,0:T(8,128)S(1)}, u32[]{:S(2)}, u32[]{:S(2)}) collective-permute-start(f32[72,128]{1,0:T(8,128)S(1)} %get-tuple-element.52), channel_id=1, source_target_pairs={{0,2},{1,3},{2,0},{3,1},{4,6},{5,7},{6,4},{7,5},{8,10},{9,11},{10,... | collective-permute-start | bytes 110600 | tf_op jit(solution)/shard_map/ppermute | solution.py:910
  8.3 4.6 %collective-permute-start.4 = (f32[32,128]{1,0:T(8,128)S(1)}, f32[32,128]{1,0:T(8,128)S(1)}, u32[]{:S(2)}, u32[]{:S(2)}) collective-permute-start(f32[32,128]{1,0:T(8,128)S(1)} %get-tuple-element.55), channel_id=1, source_target_pairs={{1,6},{3,4},{4,3},{5,10},{6,1},{7,8},{8,7},{9,14},{10,5},{11,12},{... | collective-permute-start | bytes 49160 | tf_op jit(solution)/shard_map/ppermute | solution.py:910
  14.0 5.0 %collective-permute-start.5 = (f32[32,384]{1,0:T(8,128)S(1)}, f32[32,384]{1,0:T(8,128)S(1)}, u32[]{:S(2)}, u32[]{:S(2)}) collective-permute-start(f32[32,384]{1,0:T(8,128)S(1)} %get-tuple-element.73), channel_id=1, source_target_pairs={{0,1},{1,0},{2,3},{3,2},{4,5},{5,4},{6,7},{7,6},{8,9},{9,8},{10,11... | collective-permute-start | bytes 147464 | tf_op jit(solution)/shard_map/ppermute | solution.py:910

commit v7 on v6

--- a/solution.py
+++ b/solution.py
@@ -135,8 +135,7 @@
 
 
 def k_rows(in_ref, id_ref, a_ref, one_ref):
-    core = lax.axis_index(CORE)
-    other = 1 - core
+    other = 1 - lax.axis_index(CORE)
     rows = in_ref.shape[2]
     n_t = in_ref.shape[3] // LANES
     n = 16 * HALO
@@ -152,9 +151,6 @@
             one_ref[to + 16 * g : to + 16 * g + 16, :] = a_ref[pl.ds(pl.multiple_of(i, 16), 16), :]
         for b in range(2):
             one_ref[to + n + 8 * b : to + n + 8 * b + 8, :] = power_rows(in_ref, other, b, t)
-    for k, x in enumerate(far_strip(in_ref, a_ref, other, core * (n_t - 1), core)):
-        to = (n + 16) * n_t + 8 * k
-        one_ref[to : to + 8, :] = x
 
 
 def k_rest(n_edges, in_ref, a_ref, u_ref, mat_ref, two_ref, mg_ref, m_ref):
@@ -183,6 +179,9 @@
             fields += [m_ref[pl.ds(pl.multiple_of(i + 8 * f, 8), 8), :] for f in range(4)]
         at = two_ref.shape[0] - 8 * (n_edges - e)
         (two_ref[at : at + 8, :],) = packed(side, fields, MSPAN, MHALO)
+    for k, x in enumerate(far_strip(in_ref, a_ref, other, core * (n_t - 1), core)):
+        at = two_ref.shape[0] - 8 * (n_edges + far_rows(rows) - k)
+        two_ref[at : at + 8, :] = x
     rest = 16 * (rows - 1 - HALO)
     for t in range(n_t):
         to = (rest + rows - 16) * t
@@ -357,20 +356,19 @@
     return slice(at, at + 8), tile_lanes(q % (wide // LANES))
 
 
-def k_beside(n_edges, rows, n_t, far_ref, one_ref, got_ref, mg_ref, z_ref, *refs):
+def k_beside(n_edges, rows, far_ref, got_ref, mg_ref, z_ref, *refs):
     near_refs, c_refs = refs[:n_edges], refs[n_edges : 2 * n_edges]
     core = lax.axis_index(CORE)
     mrows = mg_ref.shape[0] // 32
-    n = 16 * HALO
     for e in range(n_edges):
         side = edge_side(n_edges, e)
         mlanes = edge_tile(side, mg_ref.shape[1])
         fields = [mg_ref[8 * i : 8 * i + 8, mlanes] for i in range(4 * MHALO, 4 * mrows)]
         far = [near_refs[e][8 * k : 8 * k + 8, :] for k in range(4)]
         for k in range(far_rows(rows)):
-            at = (n + 16) * n_t + 8 * k
+            at = got_ref.shape[0] - 8 * (n_edges + far_rows(rows) - k)
             x = row8(far_ref, far_rows(rows) * e + k)
-            far.append(jnp.where(core == side, x, one_ref[at : at + 8, :]))
+            far.append(jnp.where(core == side, x, got_ref[at : at + 8, :]))
         far += packed(side, fields, MSPAN, MHALO)
         at = got_ref.shape[0] - 8 * (n_edges - e)
         far.append(got_ref[at : at + 8, :])
@@ -924,12 +922,12 @@
     (tab,) = call(k_tables, [(16 * (NMAT + 1) + 8, LANES)], [tab])
     n = 16 * HALO
     n_far = 8 * far_rows(rows)
-    cells, one = call(k_rows, [(16 * rows * n_t, LANES), ((n + 16) * n_t + n_far, LANES)], [both, ids])
+    cells, one = call(k_rows, [(16 * rows * n_t, LANES), ((n + 16) * n_t, LANES)], [both, ids])
     got1 = send(one, swap)
     two, mg = call(
         functools.partial(k_rest, n_edges),
         [
-            ((16 * (rows - 1 - HALO) + rows - 16) * n_t + 32 * MHALO * m_t + 8 * n_edges, LANES),
+            ((16 * (rows - 1 - HALO) + rows - 16) * n_t + 32 * MHALO * m_t + n_far + 8 * n_edges, LANES),
             (32 * mrows, mcols),
         ],
         [both, cells, offset, mat],
@@ -951,10 +949,10 @@
     )
     leaving = [z, *edges]
     leaving = call(
-        functools.partial(k_beside, n_edges, rows, n_t),
+        functools.partial(k_beside, n_edges, rows),
         [(n_c, LANES)] * n_edges + [x.shape for x in leaving],
-        [far, got1, got2, mg] + leaving,
-        aliases={4 + k: n_edges + k for k in range(len(leaving))},
+        [far, got2, mg] + leaving,
+        aliases={3 + k: n_edges + k for k in range(len(leaving))},
     )
     beside, z, near = leaving[:n_edges], leaving[n_edges], leaving[n_edges + 1 :]
     zr = send(z, along)

time: 20 us -> 19.9 us (level)
  no operation moved by 1% of the time
where the time goes in v7:
time: 19.9 us; the launch traced here: 19.7 us
  starting transfers between devices  8.82 us (44%)
  Pallas kernels  6.18 us (31%)
  waiting for transfers between devices  2.64 us (13%)
  other arithmetic  1.22 us (6%)
  between operations  0.79 us (4%)
    ppermute x6, starting transfers between devices, send(): return lax.ppermute(x, axes, pairs(dims, sends))  8.82 us
    pallas_call x11, Pallas kernels, call(): pl.pallas_call(kernel, out_shape=[jax.ShapeDtypeStruct(s, jnp.float32) fo...  6.18 us
    ppermute x6, waiting for transfers between devices, send(): return lax.ppermute(x, axes, pairs(dims, sends))  2.64 us
    select_n x1, other arithmetic, per_device(): both = jnp.where(kind == 0, temp[None], power[None, None])  1.14 us
  transfers between devices with their start and end apart: 6, of which 4 were waited for; matrix products, arithmetic and copies ran while one was open for 0% of the time, Pallas kernels for 20%

profile of v7, /device:TPU:0, one launch (start us, length us, event | category | flops | bytes accessed | tf_op | source)
XLA Modules:
  0.0 19.7 jit_solution(12954882287738611328)
XLA Ops:
  0.6 0.0 copy-start
  0.6 0.0 copy-start.2
  0.7 0.0 copy-start.1
  0.7 1.1 %broadcast_select_fusion.in_ref = f32[2,8,24,384]{3,2,1,0:T(8,128)S(1)} fusion(f32[24,384]{1,0:T(8,128)} %param.10, f32[8,24,384]{2,1,0:T(8,128)} %param.8, pred[2]{0:T(512)(128)(4,1)S(1)} %iota_compare_fusion.2), kind=kLoop, calls=%fused_computation | loop fusion | flops 147456 | bytes 921602 | tf_op jit(solution)/shard_map/jit(_where)/select_n | solution.py:919
  1.8 0.0 copy-start.3
  1.8 0.0 copy-start.4
  1.8 0.0 copy-start.5
  1.9 0.2 %shard_map.104 = (f32[1152,128]{1,0:T(8,128)S(1)}, f32[576,128]{1,0:T(8,128)S(1)}) custom-call(f32[2,8,24,384]{3,2,1,0:T(8,128)S(1)} %broadcast_select_fusion.in_ref, s32[8,24,384]{2,1,0:T(8,128)S(1)} %copy-done), custom_call_target="tpu_custom_call" | custom-call | tf_op jit(solution)/shard_map/pallas_call | solution.py:40
  2.1 0.5 %collective-permute-start.1 = (f32[576,128]{1,0:T(8,128)S(1)}, f32[576,128]{1,0:T(8,128)S(1)}, u32[]{:S(2)}, u32[]{:S(2)}) collective-permute-start(f32[576,128]{1,0:T(8,128)S(1)} %get-tuple-element.42), channel_id=1, source_target_pairs={{0,1},{1,0},{2,3},{3,2},{4,5},{5,4},{6,7},{7,6},{8,9},{9,8},{10,11... | collective-permute-start | bytes 884744 | tf_op jit(solution)/shard_map/ppermute | solution.py:908
  2.6 0.2 shard_map.105
  2.8 0.1 collective-permute-start
  3.0 0.0 copy-done.4
  3.0 0.1 select_maximum_fusion.tab
  3.0 0.1 shard_map.103.tab
  3.2 0.2 %shard_map.106 = (f32[88,384]{1,0:T(8,128)S(1)}, f32[88,384]{1,0:T(8,128)S(1)}, f32[88,384]{1,0:T(8,128)S(1)}, f32[24,128]{1,0:T(8,128)S(1)}) custom-call(f32[280,128]{1,0:T(8,128)S(1)} %shard_map.103.tab, f32[2,8,24,384]{3,2,1,0:T(8,128)S(1)} %broadcast_select_fusion.in_ref, f32[1152,128]{1,0:T(8,128)S(1)} %get-tuple-element.39.a_ref), custom_call_target="tpu_custom_call" | custom-call | tf_op jit(solution)/shard_map/pallas_call | solution.py:40
  3.4 0.4 %collective-permute-done.1.got_ref = f32[576,128]{1,0:T(8,128)S(1)} collective-permute-done((f32[576,128]{1,0:T(8,128)S(1)}, f32[576,128]{1,0:T(8,128)S(1)}, u32[]{:S(2)}, u32[]{:S(2)}) %collective-permute-start.1) | collective-permute-done | bytes 294944 | tf_op jit(solution)/shard_map/ppermute | solution.py:908
  3.8 0.7 %shard_map.107 = (f32[120,768]{1,0:T(8,128)S(1)}, f32[192,768]{1,0:T(8,128)S(1)}, f32[32,128]{1,0:T(8,128)S(1)}) custom-call(f32[280,128]{1,0:T(8,128)S(1)} %shard_map.103.tab, f32[2,8,24,384]{3,2,1,0:T(8,128)S(1)} %broadcast_select_fusion.in_ref, f32[1152,128]{1,0:T(8,128)S(1)} %get-tuple-element.39.a_ref, f32[576,128]{1,0:T(8,128)S(1)} %collective-permute-done.1.got_ref, ...), custom_call_target="tpu_custom_call" | custom-call | flops 10000000000 | tf_op jit(solution)/shard_map/pallas_call | solution.py:40
  4.5 0.2 collective-permute-done.got_ref
  4.7 0.1 shard_map.109
  4.7 0.7 %collective-permute-start.3 = (f32[120,768]{1,0:T(8,128)S(1)}, f32[120,768]{1,0:T(8,128)S(1)}, u32[]{:S(2)}, u32[]{:S(2)}) collective-permute-start(f32[120,768]{1,0:T(8,128)S(1)} %get-tuple-element.54), channel_id=1, source_target_pairs={{1,4},{3,6},{4,1},{5,8},{6,3},{7,10},{8,5},{9,12},{10,7},{11,14},{... | collective-permute-start | bytes 1105928 | tf_op jit(solution)/shard_map/ppermute | solution.py:908
  5.4 2.8 %collective-permute-start.2 = (f32[72,128]{1,0:T(8,128)S(1)}, f32[72,128]{1,0:T(8,128)S(1)}, u32[]{:S(2)}, u32[]{:S(2)}) collective-permute-start(f32[72,128]{1,0:T(8,128)S(1)} %get-tuple-element.52), channel_id=1, source_target_pairs={{0,2},{1,3},{2,0},{3,1},{4,6},{5,7},{6,4},{7,5},{8,10},{9,11},{10,... | collective-permute-start | bytes 110600 | tf_op jit(solution)/shard_map/ppermute | solution.py:908
  8.2 0.7 %collective-permute-start.4 = (f32[32,128]{1,0:T(8,128)S(1)}, f32[32,128]{1,0:T(8,128)S(1)}, u32[]{:S(2)}, u32[]{:S(2)}) collective-permute-start(f32[32,128]{1,0:T(8,128)S(1)} %get-tuple-element.55), channel_id=1, source_target_pairs={{1,6},{3,4},{4,3},{5,10},{6,1},{7,8},{8,7},{9,14},{10,5},{11,12},{... | collective-permute-start | bytes 49160 | tf_op jit(solution)/shard_map/ppermute | solution.py:908
  8.9 0.1 shard_map.108
  9.0 1.2 %collective-permute-done.2.refs_0_ = f32[72,128]{1,0:T(8,128)S(1)} collective-permute-done((f32[72,128]{1,0:T(8,128)S(1)}, f32[72,128]{1,0:T(8,128)S(1)}, u32[]{:S(2)}, u32[]{:S(2)}) %collective-permute-start.2) | collective-permute-done | bytes 36896 | tf_op jit(solution)/shard_map/ppermute | solution.py:908
  10.2 0.3 %shard_map.111 = (f32[56,384]{1,0:T(8,128)S(1)}, f32[56,384]{1,0:T(8,128)S(1)}, f32[56,384]{1,0:T(8,128)S(1)}, f32[56,384]{1,0:T(8,128)S(1)}, f32[56,384]{1,0:T(...) custom-call(f32[280,128]{1,0:T(8,128)S(1)} %shard_map.103.tab, ...), custom_call_target="tpu_custom_call" | custom-call | tf_op jit(solution)/shard_map/pallas_call | solution.py:40
  10.4 2.3 %shard_map.110 = (f32[296,896]{1,0:T(8,128)S(1)}, f32[296,896]{1,0:T(8,128)S(1)}, f32[296,896]{1,0:T(8,128)S(1)}, f32[296,896]{1,0:T(8,128)S(1)}, f32[296,896]{1...) custom-call(f32[280,128]{1,0:T(8,128)S(1)} %shard_map.103.tab, ...), custom_call_target="tpu_custom_call" | custom-call | tf_op jit(solution)/shard_map/pallas_call | solution.py:40
  12.8 0.0 collective-permute-done.4.refs_1_
  12.8 0.0 collective-permute-done.3.zr_ref
  12.8 1.1 %shard_map.112 = (f32[32,384]{1,0:T(8,128)S(1)}, f32[24,384]{1,0:T(8,128)S(1)}, f32[96,256]{1,0:T(8,128)S(1)}) custom-call(f32[280,128]{1,0:T(8,128)S(1)} %shard_map.103.tab, f32[120,768]{1,0:T(8,128)S(1)} %collective-permute-done.3.zr_ref, f32[72,128]{1,0:T(8,128)S(1)} %collective-permute-done.2.refs_0_, f32[32,128]{1,0:T(8,128)S(1)} %collective-permute-done.4.refs_1_, ...), custom_call_target="tpu_custom_call" | custom-call | tf_op jit(solution)/shard_map/pallas_call | solution.py:40
  13.9 4.1 %collective-permute-start.5 = (f32[32,384]{1,0:T(8,128)S(1)}, f32[32,384]{1,0:T(8,128)S(1)}, u32[]{:S(2)}, u32[]{:S(2)}) collective-permute-start(f32[32,384]{1,0:T(8,128)S(1)} %get-tuple-element.73), channel_id=1, source_target_pairs={{0,1},{1,0},{2,3},{3,2},{4,5},{5,4},{6,7},{7,6},{8,9},{9,8},{10,11... | collective-permute-start | bytes 147464 | tf_op jit(solution)/shard_map/ppermute | solution.py:908
  18.0 0.9 %collective-permute-done.5.xr_ref = f32[32,384]{1,0:T(8,128)S(1)} collective-permute-done((f32[32,384]{1,0:T(8,128)S(1)}, f32[32,384]{1,0:T(8,128)S(1)}, u32[]{:S(2)}, u32[]{:S(2)}) %collective-permute-start.5) | collective-permute-done | bytes 49184 | tf_op jit(solution)/shard_map/ppermute | solution.py:908
  18.9 0.8 %shard_map.113 = (f32[8,24,384]{2,1,0:T(8,128)}, f32[3,6,4,256]{3,2,1,0:T(4,128)}, f32[24,384]{1,0:T(8,128)}) custom-call(f32[296,896]{1,0:T(8,128)S(1)} %get-tuple-element.53.refs_7_.t_in, f32[24,384]{1,0:T(8,128)S(1)} %get-tuple-element.72.keep_ref, f32[32,384]{1,0:T(8,128)S(1)} %collective-permute-done.5.xr_ref, f32[96,256]{1,0:T(8,128)S(1)} %get-tuple-element.74.u_in), custom_call_target="tpu_custom_call" | custom-call | tf_op jit(solution)/shard_map/pallas_call | solution.py:40
  (6 shorter events, 0.0 us)
Async XLA Ops:
  0.6 1.2 %copy-start = (s32[8,24,384]{2,1,0:T(8,128)S(1)}, s32[8,24,384]{2,1,0:T(8,128)}, u32[]{:S(2)}) copy-start(s32[8,24,384]{2,1,0:T(8,128)} %id_ref.1) | copy-start | bytes 884740
  0.6 2.0 %copy-start.2 = (s32[6,4,256]{2,1,0:T(4,128)S(1)}, s32[6,4,256]{2,1,0:T(4,128)}, u32[]{:S(2)}) copy-start(s32[6,4,256]{2,1,0:T(4,128)} %mat_ref.1) | copy-start | bytes 73732
  0.7 2.0 %copy-start.1 = (f32[3,6,4,256]{3,2,1,0:T(4,128)S(1)}, f32[3,6,4,256]{3,2,1,0:T(4,128)}, u32[]{:S(2)}) copy-start(f32[3,6,4,256]{3,2,1,0:T(4,128)} %u_ref.1) | copy-start | bytes 221188
  1.8 1.1 %copy-start.3 = (f32[16]{0:T(128)S(1)}, f32[16]{0:T(128)}, u32[]{:S(2)}) copy-start(f32[16]{0:T(128)} %param.15) | copy-start | bytes 196
  1.8 1.1 %copy-start.4 = (f32[16]{0:T(128)S(1)}, f32[16]{0:T(128)}, u32[]{:S(2)}) copy-start(f32[16]{0:T(128)} %param.14) | copy-start | bytes 196
  1.8 1.1 %copy-start.5 = (f32[16]{0:T(128)S(1)}, f32[16]{0:T(128)}, u32[]{:S(2)}) copy-start(f32[16]{0:T(128)} %param.13) | copy-start | bytes 196
  2.1 1.7 %collective-permute-start.1 = (f32[576,128]{1,0:T(8,128)S(1)}, f32[576,128]{1,0:T(8,128)S(1)}, u32[]{:S(2)}, u32[]{:S(2)}) collective-permute-start(f32[576,128]{1,0:T(8,128)S(1)} %get-tuple-element.42), channel_id=1, source_target_pairs={{0,1},{1,0},{2,3},{3,2},{4,5},{5,4},{6,7},{7,6},{8,9},{9,8},{10,11... | collective-permute-start | bytes 884744 | tf_op jit(solution)/shard_map/ppermute | solution.py:908
  2.8 1.8 %collective-permute-start = (f32[824,128]{1,0:T(8,128)S(1)}, f32[824,128]{1,0:T(8,128)S(1)}, u32[]{:S(2)}, u32[]{:S(2)}) collective-permute-start(f32[824,128]{1,0:T(8,128)S(1)} %get-tuple-element.40), channel_id=1, source_target_pairs={{0,1},{1,0},{2,3},{3,2},{4,5},{5,4},{6,7},{7,6},{8,9},{9,8},{10,11... | collective-permute-start | bytes 1265672 | tf_op jit(solution)/shard_map/ppermute | solution.py:908
  4.7 8.0 %collective-permute-start.3 = (f32[120,768]{1,0:T(8,128)S(1)}, f32[120,768]{1,0:T(8,128)S(1)}, u32[]{:S(2)}, u32[]{:S(2)}) collective-permute-start(f32[120,768]{1,0:T(8,128)S(1)} %get-tuple-element.54), channel_id=1, source_target_pairs={{1,4},{3,6},{4,1},{5,8},{6,3},{7,10},{8,5},{9,12},{10,7},{11,14},{... | collective-permute-start | bytes 1105928 | tf_op jit(solution)/shard_map/ppermute | solution.py:908
  5.4 4.7 %collective-permute-start.2 = (f32[72,128]{1,0:T(8,128)S(1)}, f32[72,128]{1,0:T(8,128)S(1)}, u32[]{:S(2)}, u32[]{:S(2)}) collective-permute-start(f32[72,128]{1,0:T(8,128)S(1)} %get-tuple-element.52), channel_id=1, source_target_pairs={{0,2},{1,3},{2,0},{3,1},{4,6},{5,7},{6,4},{7,5},{8,10},{9,11},{10,... | collective-permute-start | bytes 110600 | tf_op jit(solution)/shard_map/ppermute | solution.py:908
  8.2 4.6 %collective-permute-start.4 = (f32[32,128]{1,0:T(8,128)S(1)}, f32[32,128]{1,0:T(8,128)S(1)}, u32[]{:S(2)}, u32[]{:S(2)}) collective-permute-start(f32[32,128]{1,0:T(8,128)S(1)} %get-tuple-element.55), channel_id=1, source_target_pairs={{1,6},{3,4},{4,3},{5,10},{6,1},{7,8},{8,7},{9,14},{10,5},{11,12},{... | collective-permute-start | bytes 49160 | tf_op jit(solution)/shard_map/ppermute | solution.py:908
  13.9 5.0 %collective-permute-start.5 = (f32[32,384]{1,0:T(8,128)S(1)}, f32[32,384]{1,0:T(8,128)S(1)}, u32[]{:S(2)}, u32[]{:S(2)}) collective-permute-start(f32[32,384]{1,0:T(8,128)S(1)} %get-tuple-element.73), channel_id=1, source_target_pairs={{0,1},{1,0},{2,3},{3,2},{4,5},{5,4},{6,7},{7,6},{8,9},{9,8},{10,11... | collective-permute-start | bytes 147464 | tf_op jit(solution)/shard_map/ppermute | solution.py:908

commit v8 on v7

--- a/solution.py
+++ b/solution.py
@@ -24,6 +24,7 @@
 FRONT = 9
 AHEAD = 5
 STEP = 3
+HBM = pl.BlockSpec(memory_space=pltpu.HBM)
 SPAN = 11
 MSPAN = 8
 NMAT = 16
@@ -36,12 +37,12 @@
 UNROLL_STRAIN = 3
 
 
-def call(kernel, outs, args, scratch=(), specs=None, aliases=None, cost=0):
+def call(kernel, outs, args, scratch=(), specs=None, out_specs=None, aliases=None, cost=0):
     return pl.pallas_call(
         kernel,
         out_shape=[jax.ShapeDtypeStruct(s, jnp.float32) for s in outs],
         in_specs=specs or [VMEM] * len(args),
-        out_specs=[VMEM] * len(outs),
+        out_specs=out_specs or [VMEM] * len(outs),
         input_output_aliases=aliases or {},
         cost_estimate=pl.CostEstimate(flops=cost, bytes_accessed=0, transcendentals=0) if cost else None,
         scratch_shapes=[pltpu.VMEM(s, jnp.float32) if isinstance(s, tuple) else s for s in scratch],
@@ -194,8 +195,10 @@
     for t in range(m_t):
         for g in range(MHALO):
             i = 32 * (mrows * t + turned(core, mrows - 1, mrows - 1 - g))
-            k = (rest + rows - 16) * n_t + 32 * (MHALO * t + g)
-            two_ref[k : k + 32, :] = m_ref[pl.ds(pl.multiple_of(i, 32), 32), :]
+            k = (rest + rows - 16) * n_t + 4 * ML * (MHALO * t + g)
+            x = m_ref[pl.ds(pl.multiple_of(i, 32), 32), :]
+            for f in range(4):
+                two_ref[k + ML * f : k + ML * (f + 1), :] = x[8 * f : 8 * f + ML, :]
 
 
 def power_rows(in_ref, turn, b, t):
@@ -408,8 +411,11 @@
 
     mw_ref[0 : 32 * mrows, :] = mg_ref[...]
     for t in range(mw_ref.shape[1] // LANES):
-        at = (rest + rows - 16) * n_t + 32 * MHALO * t
-        mw_ref[32 * mrows : 32 * (mrows + MHALO), tile_lanes(t)] = got_ref[at : at + 32 * MHALO, :]
+        for k in range(4 * MHALO):
+            at = (rest + rows - 16) * n_t + ML * (4 * MHALO * t + k)
+            to = 32 * mrows + 8 * k
+            x = jnp.where(sub_iota(LANES) < ML, got_ref[at : at + 8, :], 0.0)
+            mw_ref[to : to + 8, tile_lanes(t)] = x
 
 
 class Sides:
@@ -824,36 +830,75 @@
             u_ref[8 * (mrows * d + g) : 8 * (mrows * d + g) + 8, :] = row8(d_refs[d], i)[:, 0:mcols]
 
 
-def k_out(rows, mrows, t_in, keep_ref, xr_ref, u_in, t_out, u_out, slow_ref, buf, die, wide_die, ubuf):
-    half = slow_ref.shape[1]
+def put(ref, at, x):
+    count = ref.shape[0] * LANES // x.shape[1]
+    for t, piece in enumerate(tiles(x)):
+        ref[count * t + at : count * t + at + piece.shape[0], :] = piece
+
+
+def k_most(rows, mrows, t_in, keep_ref, u_in, t_out, u_out, warm_ref, buf, ubuf, t_vm, u_vm, sem):
+    half = keep_ref.shape[1]
     mcols = u_in.shape[1]
     core = lax.axis_index(CORE)
 
-    def put(ref, at, x):
-        count = ref.shape[0] * LANES // x.shape[1]
-        for t, piece in enumerate(tiles(x)):
-            ref[count * t + at : count * t + at + piece.shape[0], :] = piece
-
     def build(rev):
         lo = half if rev else 0
-        for g in range(rows):
+        for g in range(rows - 8):
             i = rows - 1 - g if rev else g
             if g < 2:
                 x = keep_ref[8 * g : 8 * g + 8, :]
-            elif g < rows - 3:
+            else:
+                x = t_in[8 * (FRONT + g) : 8 * (FRONT + g) + 8, lo : lo + half]
+            put(buf, 8 * (i - 8 if rev else i), x)
+        for g in range(mrows):
+            i = mrows - 1 - g if rev else g
+            for d in range(3):
+                put(ubuf, 8 * (mrows * d + i), row8(u_in, mrows * d + g))
+
+    @pl.when(core == 0)
+    def _():
+        build(False)
+
+    @pl.when(core != 0)
+    def _():
+        build(True)
+
+    most = rows - 8
+    for t in range(half // LANES):
+        for l in range(DEPTH):
+            t_vm[l, :, tile_lanes(t)] = buf[pl.ds(8 * most * t + l, most, stride=8), :]
+    first = pl.ds(pl.multiple_of(8 * core, 8), most)
+    out = pltpu.make_async_copy(t_vm, t_out.at[:, first, :], sem.at[0])
+    out.start()
+    for t in range(mcols // LANES):
+        for d in range(3):
+            for l in range(ML):
+                u_vm[d, l, :, tile_lanes(t)] = ubuf[pl.ds(8 * mrows * (3 * t + d) + l, mrows, stride=8), :]
+    u_copy = pltpu.make_async_copy(u_vm, u_out, sem.at[1])
+    u_copy.start()
+    warm_ref[first, :] = 1.0 + 0.2 * t_vm[0]
+    out.wait()
+    u_copy.wait()
+
+
+def k_last(rows, mrows, t_in, keep_ref, xr_ref, warm_ref, t_old, t_out, slow_ref, buf, die, wide_die, t_vm, s_vm, sem):
+    half = keep_ref.shape[1]
+    core = lax.axis_index(CORE)
+
+    def build(rev):
+        lo = half if rev else 0
+        for g in range(rows - 8, rows):
+            if g < rows - 3:
                 x = t_in[8 * (FRONT + g) : 8 * (FRONT + g) + 8, lo : lo + half]
             else:
                 k = rows - 1 - g
                 x = xr_ref[8 * k : 8 * k + 8, :]
-            put(buf, 8 * i, x)
+            put(buf, 8 * (rows - 1 - g if rev else g - rows + 8), x)
         for g in range(mrows):
             mine = 2 * mrows - 1 - g if rev else g
             theirs = g if rev else 2 * mrows - 1 - g
             die[mine : mine + 1, :] = keep_ref[16 + g : 17 + g, 0:LANES]
             die[theirs : theirs + 1, :] = xr_ref[24 + g : 25 + g, 0:LANES]
-            for d in range(3):
-                i = mrows - 1 - g if rev else g
-                put(ubuf, 8 * (mrows * d + i), row8(u_in, mrows * d + g))
 
     @pl.when(core == 0)
     def _():
@@ -864,20 +909,23 @@
         build(True)
 
     for t in range(half // LANES):
-        at = 8 * rows * t
         for l in range(DEPTH):
-            t_out[l, :, tile_lanes(t)] = buf[pl.ds(at + l, rows, stride=8), :]
-    for t in range(mcols // LANES):
-        for d in range(3):
-            for l in range(ML):
-                u_out[d, l, :, tile_lanes(t)] = ubuf[pl.ds(8 * mrows * (3 * t + d) + l, mrows, stride=8), :]
+            t_vm[l, :, tile_lanes(t)] = buf[pl.ds(64 * t + l, 8, stride=8), :]
+    at = pl.ds(pl.multiple_of((rows - 8) * (1 - core), 8), 8)
+    out = pltpu.make_async_copy(t_vm, t_out.at[:, at, :], sem.at[0])
+    out.start()
+    s_vm[...] = warm_ref[...]
+    s_vm[at, :] = 1.0 + 0.2 * t_vm[0]
     lane = lane_iota(2 * mrows)
     for t in range(half // LANES):
         x = gather_lanes(die[...], (lane + LANES * t) // 3)
         for b in range(3):
             wide_die[pl.ds(b, 2 * mrows, stride=3), :] = x
-        slow = 1.0 + 0.2 * buf[pl.ds(8 * rows * t, rows, stride=8), :] + 0.5 * wide_die[...]
-        slow_ref[:, tile_lanes(t)] = slow
+        s_vm[:, tile_lanes(t)] = s_vm[:, tile_lanes(t)] + 0.5 * wide_die[...]
+    slow = pltpu.make_async_copy(s_vm, slow_ref, sem.at[1])
+    slow.start()
+    out.wait()
+    slow.wait()
 
 
 def pairs(dims, sends):
@@ -927,7 +975,7 @@
     two, mg = call(
         functools.partial(k_rest, n_edges),
         [
-            ((16 * (rows - 1 - HALO) + rows - 16) * n_t + 32 * MHALO * m_t + n_far + 8 * n_edges, LANES),
+            ((16 * (rows - 1 - HALO) + rows - 16) * n_t + 4 * ML * MHALO * m_t + n_far + 8 * n_edges, LANES),
             (32 * mrows, mcols),
         ],
         [both, cells, offset, mat],
@@ -995,16 +1043,34 @@
         + [(8 * HALO, LANES)] * 4,
     )
     xr = send(x, swap)
-    t_out, u_out, slow = call(
-        functools.partial(k_out, rows, mrows),
+    t_most, u_out, warm = call(
+        functools.partial(k_most, rows, mrows),
         [temp.shape, offset.shape, power.shape],
-        [t2, keep, xr, u],
+        [t2, keep, u],
         scratch=[
-            (8 * rows * n_t, LANES),
+            (8 * (rows - 8) * n_t, LANES),
+            (24 * mrows * m_t, LANES),
+            (temp.shape[0], rows - 8, half),
+            offset.shape,
+            pltpu.SemaphoreType.DMA((2,)),
+        ],
+        out_specs=[HBM, HBM, VMEM],
+    )
+    t_out, slow = call(
+        functools.partial(k_last, rows, mrows),
+        [temp.shape, power.shape],
+        [t2, keep, xr, warm, t_most],
+        scratch=[
+            (64 * n_t, LANES),
             (2 * mrows, LANES),
             (rows, LANES),
-            (24 * mrows * m_t, LANES),
+            (temp.shape[0], 8, half),
+            power.shape,
+            pltpu.SemaphoreType.DMA((2,)),
         ],
+        specs=[VMEM] * 4 + [HBM],
+        out_specs=[HBM, HBM],
+        aliases={4: 0},
     )
     return t_out, u_out, slow
 

time: 19.9 us -> 19.8 us (level)
  waiting for transfers between devices: 2.64 us -> 1.82 us
  Pallas kernels: 6.18 us -> 6.87 us
    ppermute x6, waiting for transfers between devices: 2.64 us -> 1.82 us  [send(): return lax.ppermute(x, axes, pairs(dims, sends))]
    pallas_call x11 -> x12, Pallas kernels: 6.18 us -> 6.87 us  [call(): pl.pallas_call(kernel, out_shape=[jax.ShapeDtypeStruct(s, jnp.float32) fo...]
  transfers between devices with their start and end apart: 6 -> 6, of which waited for: 4 -> 4; matrix products, arithmetic and copies ran while one was open for 0% -> 0% of each run, Pallas kernels for 20% -> 24%
where the time goes in v8:
time: 19.8 us; the launch traced here: 19.6 us
  starting transfers between devices  8.86 us (45%)
  Pallas kernels  6.87 us (35%)
  waiting for transfers between devices  1.82 us (9%)
  other arithmetic  1.22 us (6%)
  between operations  0.8 us (4%)
    ppermute x6, starting transfers between devices, send(): return lax.ppermute(x, axes, pairs(dims, sends))  8.86 us
    pallas_call x12, Pallas kernels, call(): pl.pallas_call(kernel, out_shape=[jax.ShapeDtypeStruct(s, jnp.float32) fo...  6.87 us
    ppermute x6, waiting for transfers between devices, send(): return lax.ppermute(x, axes, pairs(dims, sends))  1.82 us
    select_n x1, other arithmetic, per_device(): both = jnp.where(kind == 0, temp[None], power[None, None])  1.14 us
  transfers between devices with their start and end apart: 6, of which 4 were waited for; matrix products, arithmetic and copies ran while one was open for 0% of the time, Pallas kernels for 24%

profile of v8, /device:TPU:0, one launch (start us, length us, event | category | flops | bytes accessed | tf_op | source)
XLA Modules:
  0.0 19.6 jit_solution(1060322716481088736)
XLA Ops:
  0.6 0.0 copy-start
  0.6 0.0 copy-start.2
  0.7 0.0 copy-start.1
  0.7 1.1 %broadcast_select_fusion.in_ref = f32[2,8,24,384]{3,2,1,0:T(8,128)S(1)} fusion(f32[24,384]{1,0:T(8,128)} %param.10, f32[8,24,384]{2,1,0:T(8,128)} %param.8, pred[2]{0:T(512)(128)(4,1)S(1)} %iota_compare_fusion.2), kind=kLoop, calls=%fused_computation | loop fusion | flops 147456 | bytes 921602 | tf_op jit(solution)/shard_map/jit(_where)/select_n | solution.py:967
  1.8 0.0 copy-start.3
  1.8 0.0 copy-start.4
  1.8 0.0 copy-start.5
  1.9 0.2 %shard_map.104 = (f32[1152,128]{1,0:T(8,128)S(1)}, f32[576,128]{1,0:T(8,128)S(1)}) custom-call(f32[2,8,24,384]{3,2,1,0:T(8,128)S(1)} %broadcast_select_fusion.in_ref, s32[8,24,384]{2,1,0:T(8,128)S(1)} %copy-done), custom_call_target="tpu_custom_call" | custom-call | tf_op jit(solution)/shard_map/pallas_call | solution.py:41
  2.1 0.5 %collective-permute-start.1 = (f32[576,128]{1,0:T(8,128)S(1)}, f32[576,128]{1,0:T(8,128)S(1)}, u32[]{:S(2)}, u32[]{:S(2)}) collective-permute-start(f32[576,128]{1,0:T(8,128)S(1)} %get-tuple-element.47), channel_id=1, source_target_pairs={{0,1},{1,0},{2,3},{3,2},{4,5},{5,4},{6,7},{7,6},{8,9},{9,8},{10,11... | collective-permute-start | bytes 884744 | tf_op jit(solution)/shard_map/ppermute | solution.py:956
  2.6 0.2 shard_map.105
  2.8 0.1 collective-permute-start
  3.0 0.1 select_maximum_fusion.tab
  3.0 0.1 shard_map.103.tab
  3.2 0.2 %shard_map.106 = (f32[88,384]{1,0:T(8,128)S(1)}, f32[88,384]{1,0:T(8,128)S(1)}, f32[88,384]{1,0:T(8,128)S(1)}, f32[24,128]{1,0:T(8,128)S(1)}) custom-call(f32[280,128]{1,0:T(8,128)S(1)} %shard_map.103.tab, f32[2,8,24,384]{3,2,1,0:T(8,128)S(1)} %broadcast_select_fusion.in_ref, f32[1152,128]{1,0:T(8,128)S(1)} %get-tuple-element.44.a_ref), custom_call_target="tpu_custom_call" | custom-call | tf_op jit(solution)/shard_map/pallas_call | solution.py:41
  3.4 0.4 %collective-permute-done.1.got_ref = f32[576,128]{1,0:T(8,128)S(1)} collective-permute-done((f32[576,128]{1,0:T(8,128)S(1)}, f32[576,128]{1,0:T(8,128)S(1)}, u32[]{:S(2)}, u32[]{:S(2)}) %collective-permute-start.1) | collective-permute-done | bytes 294944 | tf_op jit(solution)/shard_map/ppermute | solution.py:956
  3.8 0.7 %shard_map.107 = (f32[120,768]{1,0:T(8,128)S(1)}, f32[192,768]{1,0:T(8,128)S(1)}, f32[32,128]{1,0:T(8,128)S(1)}) custom-call(f32[280,128]{1,0:T(8,128)S(1)} %shard_map.103.tab, f32[2,8,24,384]{3,2,1,0:T(8,128)S(1)} %broadcast_select_fusion.in_ref, f32[1152,128]{1,0:T(8,128)S(1)} %get-tuple-element.44.a_ref, f32[576,128]{1,0:T(8,128)S(1)} %collective-permute-done.1.got_ref, ...), custom_call_target="tpu_custom_call" | custom-call | flops 10000000000 | tf_op jit(solution)/shard_map/pallas_call | solution.py:41
  4.5 0.1 collective-permute-done.got_ref
  4.6 0.1 shard_map.109
  4.7 0.7 %collective-permute-start.3 = (f32[120,768]{1,0:T(8,128)S(1)}, f32[120,768]{1,0:T(8,128)S(1)}, u32[]{:S(2)}, u32[]{:S(2)}) collective-permute-start(f32[120,768]{1,0:T(8,128)S(1)} %get-tuple-element.59), channel_id=1, source_target_pairs={{1,4},{3,6},{4,1},{5,8},{6,3},{7,10},{8,5},{9,12},{10,7},{11,14},{... | collective-permute-start | bytes 1105928 | tf_op jit(solution)/shard_map/ppermute | solution.py:956
  5.4 2.8 %collective-permute-start.2 = (f32[72,128]{1,0:T(8,128)S(1)}, f32[72,128]{1,0:T(8,128)S(1)}, u32[]{:S(2)}, u32[]{:S(2)}) collective-permute-start(f32[72,128]{1,0:T(8,128)S(1)} %get-tuple-element.57), channel_id=1, source_target_pairs={{0,2},{1,3},{2,0},{3,1},{4,6},{5,7},{6,4},{7,5},{8,10},{9,11},{10,... | collective-permute-start | bytes 110600 | tf_op jit(solution)/shard_map/ppermute | solution.py:956
  8.2 0.7 %collective-permute-start.4 = (f32[32,128]{1,0:T(8,128)S(1)}, f32[32,128]{1,0:T(8,128)S(1)}, u32[]{:S(2)}, u32[]{:S(2)}) collective-permute-start(f32[32,128]{1,0:T(8,128)S(1)} %get-tuple-element.60), channel_id=1, source_target_pairs={{1,6},{3,4},{4,3},{5,10},{6,1},{7,8},{8,7},{9,14},{10,5},{11,12},{... | collective-permute-start | bytes 49160 | tf_op jit(solution)/shard_map/ppermute | solution.py:956
  8.9 0.1 shard_map.108
  9.0 1.2 %collective-permute-done.2.refs_0_ = f32[72,128]{1,0:T(8,128)S(1)} collective-permute-done((f32[72,128]{1,0:T(8,128)S(1)}, f32[72,128]{1,0:T(8,128)S(1)}, u32[]{:S(2)}, u32[]{:S(2)}) %collective-permute-start.2) | collective-permute-done | bytes 36896 | tf_op jit(solution)/shard_map/ppermute | solution.py:956
  10.1 0.3 %shard_map.111 = (f32[56,384]{1,0:T(8,128)S(1)}, f32[56,384]{1,0:T(8,128)S(1)}, f32[56,384]{1,0:T(8,128)S(1)}, f32[56,384]{1,0:T(8,128)S(1)}, f32[56,384]{1,0:T(...) custom-call(f32[280,128]{1,0:T(8,128)S(1)} %shard_map.103.tab, ...), custom_call_target="tpu_custom_call" | custom-call | tf_op jit(solution)/shard_map/pallas_call | solution.py:41
  10.4 2.3 %shard_map.110 = (f32[296,896]{1,0:T(8,128)S(1)}, f32[296,896]{1,0:T(8,128)S(1)}, f32[296,896]{1,0:T(8,128)S(1)}, f32[296,896]{1,0:T(8,128)S(1)}, f32[296,896]{1...) custom-call(f32[280,128]{1,0:T(8,128)S(1)} %shard_map.103.tab, ...), custom_call_target="tpu_custom_call" | custom-call | tf_op jit(solution)/shard_map/pallas_call | solution.py:41
  12.8 0.0 collective-permute-done.4.refs_1_
  12.8 0.0 collective-permute-done.3.zr_ref
  12.8 1.1 %shard_map.112 = (f32[32,384]{1,0:T(8,128)S(1)}, f32[24,384]{1,0:T(8,128)S(1)}, f32[96,256]{1,0:T(8,128)S(1)}) custom-call(f32[280,128]{1,0:T(8,128)S(1)} %shard_map.103.tab, f32[120,768]{1,0:T(8,128)S(1)} %collective-permute-done.3.zr_ref, f32[72,128]{1,0:T(8,128)S(1)} %collective-permute-done.2.refs_0_, f32[32,128]{1,0:T(8,128)S(1)} %collective-permute-done.4.refs_1_, ...), custom_call_target="tpu_custom_call" | custom-call | tf_op jit(solution)/shard_map/pallas_call | solution.py:41
  13.9 4.1 %collective-permute-start.5 = (f32[32,384]{1,0:T(8,128)S(1)}, f32[32,384]{1,0:T(8,128)S(1)}, u32[]{:S(2)}, u32[]{:S(2)}) collective-permute-start(f32[32,384]{1,0:T(8,128)S(1)} %get-tuple-element.78), channel_id=1, source_target_pairs={{0,1},{1,0},{2,3},{3,2},{4,5},{5,4},{6,7},{7,6},{8,9},{9,8},{10,11... | collective-permute-start | bytes 147464 | tf_op jit(solution)/shard_map/ppermute | solution.py:956
  18.0 0.8 %shard_map.113 = (f32[8,24,384]{2,1,0:T(8,128)}, f32[3,6,4,256]{3,2,1,0:T(4,128)}, f32[24,384]{1,0:T(8,128)S(1)}) custom-call(f32[296,896]{1,0:T(8,128)S(1)} %get-tuple-element.58.refs_7_.t_in, f32[24,384]{1,0:T(8,128)S(1)} %get-tuple-element.77.keep_ref, f32[96,256]{1,0:T(8,128)S(1)} %get-tuple-element.79.u_in), custom_call_target="tpu_custom_call" | custom-call | tf_op jit(solution)/shard_map/pallas_call | solution.py:41
  18.8 0.1 collective-permute-done.5.xr_ref
  18.9 0.7 %shard_map.114 = (f32[8,24,384]{2,1,0:T(8,128)}, f32[24,384]{1,0:T(8,128)}) custom-call(f32[296,896]{1,0:T(8,128)S(1)} %get-tuple-element.58.refs_7_.t_in, f32[24,384]{1,0:T(8,128)S(1)} %get-tuple-element.77.keep_ref, f32[32,384]{1,0:T(8,128)S(1)} %collective-permute-done.5.xr_ref, ...), custom_call_target="tpu_custom_call", output_to_operand_aliasing={{0}: (4, {})} | custom-call | tf_op jit(solution)/shard_map/pallas_call | solution.py:41
  (7 shorter events, 0.0 us)
Async XLA Ops:
  0.6 1.2 %copy-start = (s32[8,24,384]{2,1,0:T(8,128)S(1)}, s32[8,24,384]{2,1,0:T(8,128)}, u32[]{:S(2)}) copy-start(s32[8,24,384]{2,1,0:T(8,128)} %id_ref.1) | copy-start | bytes 884740
  0.6 2.0 %copy-start.2 = (s32[6,4,256]{2,1,0:T(4,128)S(1)}, s32[6,4,256]{2,1,0:T(4,128)}, u32[]{:S(2)}) copy-start(s32[6,4,256]{2,1,0:T(4,128)} %mat_ref.1) | copy-start | bytes 73732
  0.7 2.0 %copy-start.1 = (f32[3,6,4,256]{3,2,1,0:T(4,128)S(1)}, f32[3,6,4,256]{3,2,1,0:T(4,128)}, u32[]{:S(2)}) copy-start(f32[3,6,4,256]{3,2,1,0:T(4,128)} %u_ref.1) | copy-start | bytes 221188
  1.8 1.1 %copy-start.3 = (f32[16]{0:T(128)S(1)}, f32[16]{0:T(128)}, u32[]{:S(2)}) copy-start(f32[16]{0:T(128)} %param.15) | copy-start | bytes 196
  1.8 1.1 %copy-start.4 = (f32[16]{0:T(128)S(1)}, f32[16]{0:T(128)}, u32[]{:S(2)}) copy-start(f32[16]{0:T(128)} %param.14) | copy-start | bytes 196
  1.8 1.1 %copy-start.5 = (f32[16]{0:T(128)S(1)}, f32[16]{0:T(128)}, u32[]{:S(2)}) copy-start(f32[16]{0:T(128)} %param.13) | copy-start | bytes 196
  2.1 1.7 %collective-permute-start.1 = (f32[576,128]{1,0:T(8,128)S(1)}, f32[576,128]{1,0:T(8,128)S(1)}, u32[]{:S(2)}, u32[]{:S(2)}) collective-permute-start(f32[576,128]{1,0:T(8,128)S(1)} %get-tuple-element.47), channel_id=1, source_target_pairs={{0,1},{1,0},{2,3},{3,2},{4,5},{5,4},{6,7},{7,6},{8,9},{9,8},{10,11... | collective-permute-start | bytes 884744 | tf_op jit(solution)/shard_map/ppermute | solution.py:956
  2.8 1.8 %collective-permute-start = (f32[776,128]{1,0:T(8,128)S(1)}, f32[776,128]{1,0:T(8,128)S(1)}, u32[]{:S(2)}, u32[]{:S(2)}) collective-permute-start(f32[776,128]{1,0:T(8,128)S(1)} %get-tuple-element.45), channel_id=1, source_target_pairs={{0,1},{1,0},{2,3},{3,2},{4,5},{5,4},{6,7},{7,6},{8,9},{9,8},{10,11... | collective-permute-start | bytes 1191944 | tf_op jit(solution)/shard_map/ppermute | solution.py:956
  4.7 8.1 %collective-permute-start.3 = (f32[120,768]{1,0:T(8,128)S(1)}, f32[120,768]{1,0:T(8,128)S(1)}, u32[]{:S(2)}, u32[]{:S(2)}) collective-permute-start(f32[120,768]{1,0:T(8,128)S(1)} %get-tuple-element.59), channel_id=1, source_target_pairs={{1,4},{3,6},{4,1},{5,8},{6,3},{7,10},{8,5},{9,12},{10,7},{11,14},{... | collective-permute-start | bytes 1105928 | tf_op jit(solution)/shard_map/ppermute | solution.py:956
  5.4 4.8 %collective-permute-start.2 = (f32[72,128]{1,0:T(8,128)S(1)}, f32[72,128]{1,0:T(8,128)S(1)}, u32[]{:S(2)}, u32[]{:S(2)}) collective-permute-start(f32[72,128]{1,0:T(8,128)S(1)} %get-tuple-element.57), channel_id=1, source_target_pairs={{0,2},{1,3},{2,0},{3,1},{4,6},{5,7},{6,4},{7,5},{8,10},{9,11},{10,... | collective-permute-start | bytes 110600 | tf_op jit(solution)/shard_map/ppermute | solution.py:956
  8.2 4.6 %collective-permute-start.4 = (f32[32,128]{1,0:T(8,128)S(1)}, f32[32,128]{1,0:T(8,128)S(1)}, u32[]{:S(2)}, u32[]{:S(2)}) collective-permute-start(f32[32,128]{1,0:T(8,128)S(1)} %get-tuple-element.60), channel_id=1, source_target_pairs={{1,6},{3,4},{4,3},{5,10},{6,1},{7,8},{8,7},{9,14},{10,5},{11,12},{... | collective-permute-start | bytes 49160 | tf_op jit(solution)/shard_map/ppermute | solution.py:956
  13.9 5.0 %collective-permute-start.5 = (f32[32,384]{1,0:T(8,128)S(1)}, f32[32,384]{1,0:T(8,128)S(1)}, u32[]{:S(2)}, u32[]{:S(2)}) collective-permute-start(f32[32,384]{1,0:T(8,128)S(1)} %get-tuple-element.78), channel_id=1, source_target_pairs={{0,1},{1,0},{2,3},{3,2},{4,5},{5,4},{6,7},{7,6},{8,9},{9,8},{10,11... | collective-permute-start | bytes 147464 | tf_op jit(solution)/shard_map/ppermute | solution.py:956

commit v9 on v7

--- a/solution.py
+++ b/solution.py
@@ -356,7 +356,7 @@
     return slice(at, at + 8), tile_lanes(q % (wide // LANES))
 
 
-def k_beside(n_edges, rows, far_ref, got_ref, mg_ref, z_ref, *refs):
+def k_beside(n_edges, rows, far_ref, got_ref, mg_ref, *refs):
     near_refs, c_refs = refs[:n_edges], refs[n_edges : 2 * n_edges]
     core = lax.axis_index(CORE)
     mrows = mg_ref.shape[0] // 32
@@ -947,15 +947,15 @@
         cost=EDGE_COST,
         scratch=[(8 * HALO, wide)] * 5,
     )
-    leaving = [z, *edges]
+    zr = send(z, along)
+    leaving = edges
     leaving = call(
         functools.partial(k_beside, n_edges, rows),
         [(n_c, LANES)] * n_edges + [x.shape for x in leaving],
         [far, got2, mg] + leaving,
         aliases={3 + k: n_edges + k for k in range(len(leaving))},
     )
-    beside, z, near = leaving[:n_edges], leaving[n_edges], leaving[n_edges + 1 :]
-    zr = send(z, along)
+    beside, near = leaving[:n_edges], leaving[n_edges:]
     if n_edges == 1:
         sides = [send(beside[0], lambda r, c, a: (r, 1 - c, a))]
         corners = [send(near[0], lambda r, c, a: along(r, 1 - c, a))]

time: 19.9 us -> 19.8 us (level)
  transfers between devices with their start and end apart: 6 -> 6, of which waited for: 4 -> 3; matrix products, arithmetic and copies ran while one was open for 0% -> 0% of each run, Pallas kernels for 20% -> 20%
where the time goes in v9:
time: 19.8 us; the launch traced here: 19.6 us
  starting transfers between devices  8.91 us (45%)
  Pallas kernels  6.19 us (31%)
  waiting for transfers between devices  2.49 us (13%)
  other arithmetic  1.22 us (6%)
  between operations  0.8 us (4%)
    ppermute x6, starting transfers between devices, send(): return lax.ppermute(x, axes, pairs(dims, sends))  8.91 us
    pallas_call x11, Pallas kernels, call(): pl.pallas_call(kernel, out_shape=[jax.ShapeDtypeStruct(s, jnp.float32) fo...  6.19 us
    ppermute x6, waiting for transfers between devices, send(): return lax.ppermute(x, axes, pairs(dims, sends))  2.49 us
    select_n x1, other arithmetic, per_device(): both = jnp.where(kind == 0, temp[None], power[None, None])  1.14 us
  transfers between devices with their start and end apart: 6, of which 3 were waited for; matrix products, arithmetic and copies ran while one was open for 0% of the time, Pallas kernels for 20%

profile of v9, /device:TPU:0, one launch (start us, length us, event | category | flops | bytes accessed | tf_op | source)
XLA Modules:
  0.0 19.6 jit_solution(3247941294966445748)
XLA Ops:
  0.6 0.0 copy-start
  0.6 0.0 copy-start.2
  0.7 1.1 %broadcast_select_fusion.in_ref = f32[2,8,24,384]{3,2,1,0:T(8,128)S(1)} fusion(f32[24,384]{1,0:T(8,128)} %param.10, f32[8,24,384]{2,1,0:T(8,128)} %param.8, pred[2]{0:T(512)(128)(4,1)S(1)} %iota_compare_fusion.2), kind=kLoop, calls=%fused_computation | loop fusion | flops 147456 | bytes 921602 | tf_op jit(solution)/shard_map/jit(_where)/select_n | solution.py:919
  1.8 0.0 copy-start.3
  1.8 0.0 copy-start.4
  1.8 0.0 copy-start.5
  1.9 0.2 %shard_map.104 = (f32[1152,128]{1,0:T(8,128)S(1)}, f32[576,128]{1,0:T(8,128)S(1)}) custom-call(f32[2,8,24,384]{3,2,1,0:T(8,128)S(1)} %broadcast_select_fusion.in_ref, s32[8,24,384]{2,1,0:T(8,128)S(1)} %copy-done), custom_call_target="tpu_custom_call" | custom-call | tf_op jit(solution)/shard_map/pallas_call | solution.py:40
  2.1 0.5 %collective-permute-start.1 = (f32[576,128]{1,0:T(8,128)S(1)}, f32[576,128]{1,0:T(8,128)S(1)}, u32[]{:S(2)}, u32[]{:S(2)}) collective-permute-start(f32[576,128]{1,0:T(8,128)S(1)} %get-tuple-element.41), channel_id=1, source_target_pairs={{0,1},{1,0},{2,3},{3,2},{4,5},{5,4},{6,7},{7,6},{8,9},{9,8},{10,11... | collective-permute-start | bytes 884744 | tf_op jit(solution)/shard_map/ppermute | solution.py:908
  2.6 0.0 copy-done.1
  2.6 0.2 shard_map.105
  2.8 0.1 collective-permute-start
  3.0 0.0 copy-done.4
  3.0 0.1 select_maximum_fusion.tab
  3.0 0.1 shard_map.103.tab
  3.2 0.2 %shard_map.106 = (f32[88,384]{1,0:T(8,128)S(1)}, f32[88,384]{1,0:T(8,128)S(1)}, f32[88,384]{1,0:T(8,128)S(1)}, f32[24,128]{1,0:T(8,128)S(1)}) custom-call(f32[280,128]{1,0:T(8,128)S(1)} %shard_map.103.tab, f32[2,8,24,384]{3,2,1,0:T(8,128)S(1)} %broadcast_select_fusion.in_ref, f32[1152,128]{1,0:T(8,128)S(1)} %get-tuple-element.38.a_ref), custom_call_target="tpu_custom_call" | custom-call | tf_op jit(solution)/shard_map/pallas_call | solution.py:40
  3.4 0.4 %collective-permute-done.1.got_ref = f32[576,128]{1,0:T(8,128)S(1)} collective-permute-done((f32[576,128]{1,0:T(8,128)S(1)}, f32[576,128]{1,0:T(8,128)S(1)}, u32[]{:S(2)}, u32[]{:S(2)}) %collective-permute-start.1) | collective-permute-done | bytes 294944 | tf_op jit(solution)/shard_map/ppermute | solution.py:908
  3.8 0.7 %shard_map.107 = (f32[120,768]{1,0:T(8,128)S(1)}, f32[192,768]{1,0:T(8,128)S(1)}, f32[32,128]{1,0:T(8,128)S(1)}) custom-call(f32[280,128]{1,0:T(8,128)S(1)} %shard_map.103.tab, f32[2,8,24,384]{3,2,1,0:T(8,128)S(1)} %broadcast_select_fusion.in_ref, f32[1152,128]{1,0:T(8,128)S(1)} %get-tuple-element.38.a_ref, f32[576,128]{1,0:T(8,128)S(1)} %collective-permute-done.1.got_ref, ...), custom_call_target="tpu_custom_call" | custom-call | flops 10000000000 | tf_op jit(solution)/shard_map/pallas_call | solution.py:40
  4.5 0.7 %collective-permute-start.3 = (f32[120,768]{1,0:T(8,128)S(1)}, f32[120,768]{1,0:T(8,128)S(1)}, u32[]{:S(2)}, u32[]{:S(2)}) collective-permute-start(f32[120,768]{1,0:T(8,128)S(1)} %get-tuple-element.52), channel_id=1, source_target_pairs={{1,4},{3,6},{4,1},{5,8},{6,3},{7,10},{8,5},{9,12},{10,7},{11,14},{... | collective-permute-start | bytes 1105928 | tf_op jit(solution)/shard_map/ppermute | solution.py:908
  5.2 0.0 collective-permute-done.got_ref
  5.2 0.1 shard_map.109
  5.3 2.9 %collective-permute-start.2 = (f32[72,128]{1,0:T(8,128)S(1)}, f32[72,128]{1,0:T(8,128)S(1)}, u32[]{:S(2)}, u32[]{:S(2)}) collective-permute-start(f32[72,128]{1,0:T(8,128)S(1)} %get-tuple-element.50), channel_id=1, source_target_pairs={{0,2},{1,3},{2,0},{3,1},{4,6},{5,7},{6,4},{7,5},{8,10},{9,11},{10,... | collective-permute-start | bytes 110600 | tf_op jit(solution)/shard_map/ppermute | solution.py:908
  8.2 0.7 %collective-permute-start.4 = (f32[32,128]{1,0:T(8,128)S(1)}, f32[32,128]{1,0:T(8,128)S(1)}, u32[]{:S(2)}, u32[]{:S(2)}) collective-permute-start(f32[32,128]{1,0:T(8,128)S(1)} %get-tuple-element.53), channel_id=1, source_target_pairs={{1,6},{3,4},{4,3},{5,10},{6,1},{7,8},{8,7},{9,14},{10,5},{11,12},{... | collective-permute-start | bytes 49160 | tf_op jit(solution)/shard_map/ppermute | solution.py:908
  8.8 0.1 shard_map.108
  8.9 1.2 %collective-permute-done.2.refs_0_ = f32[72,128]{1,0:T(8,128)S(1)} collective-permute-done((f32[72,128]{1,0:T(8,128)S(1)}, f32[72,128]{1,0:T(8,128)S(1)}, u32[]{:S(2)}, u32[]{:S(2)}) %collective-permute-start.2) | collective-permute-done | bytes 36896 | tf_op jit(solution)/shard_map/ppermute | solution.py:908
  10.1 0.3 %shard_map.111 = (f32[56,384]{1,0:T(8,128)S(1)}, f32[56,384]{1,0:T(8,128)S(1)}, f32[56,384]{1,0:T(8,128)S(1)}, f32[56,384]{1,0:T(8,128)S(1)}, f32[56,384]{1,0:T(...) custom-call(f32[280,128]{1,0:T(8,128)S(1)} %shard_map.103.tab, ...), custom_call_target="tpu_custom_call" | custom-call | tf_op jit(solution)/shard_map/pallas_call | solution.py:40
  10.4 2.3 %shard_map.110 = (f32[296,896]{1,0:T(8,128)S(1)}, f32[296,896]{1,0:T(8,128)S(1)}, f32[296,896]{1,0:T(8,128)S(1)}, f32[296,896]{1,0:T(8,128)S(1)}, f32[296,896]{1...) custom-call(f32[280,128]{1,0:T(8,128)S(1)} %shard_map.103.tab, ...), custom_call_target="tpu_custom_call" | custom-call | tf_op jit(solution)/shard_map/pallas_call | solution.py:40
  12.7 0.0 collective-permute-done.4.refs_1_
  12.7 0.0 collective-permute-done.3.zr_ref
  12.7 1.1 %shard_map.112 = (f32[32,384]{1,0:T(8,128)S(1)}, f32[24,384]{1,0:T(8,128)S(1)}, f32[96,256]{1,0:T(8,128)S(1)}) custom-call(f32[280,128]{1,0:T(8,128)S(1)} %shard_map.103.tab, f32[120,768]{1,0:T(8,128)S(1)} %collective-permute-done.3.zr_ref, f32[72,128]{1,0:T(8,128)S(1)} %collective-permute-done.2.refs_0_, f32[32,128]{1,0:T(8,128)S(1)} %collective-permute-done.4.refs_1_, ...), custom_call_target="tpu_custom_call" | custom-call | tf_op jit(solution)/shard_map/pallas_call | solution.py:40
  13.9 4.1 %collective-permute-start.5 = (f32[32,384]{1,0:T(8,128)S(1)}, f32[32,384]{1,0:T(8,128)S(1)}, u32[]{:S(2)}, u32[]{:S(2)}) collective-permute-start(f32[32,384]{1,0:T(8,128)S(1)} %get-tuple-element.71), channel_id=1, source_target_pairs={{0,1},{1,0},{2,3},{3,2},{4,5},{5,4},{6,7},{7,6},{8,9},{9,8},{10,11... | collective-permute-start | bytes 147464 | tf_op jit(solution)/shard_map/ppermute | solution.py:908
  17.9 0.9 %collective-permute-done.5.xr_ref = f32[32,384]{1,0:T(8,128)S(1)} collective-permute-done((f32[32,384]{1,0:T(8,128)S(1)}, f32[32,384]{1,0:T(8,128)S(1)}, u32[]{:S(2)}, u32[]{:S(2)}) %collective-permute-start.5) | collective-permute-done | bytes 49184 | tf_op jit(solution)/shard_map/ppermute | solution.py:908
  18.8 0.8 %shard_map.113 = (f32[8,24,384]{2,1,0:T(8,128)}, f32[3,6,4,256]{3,2,1,0:T(4,128)}, f32[24,384]{1,0:T(8,128)}) custom-call(f32[296,896]{1,0:T(8,128)S(1)} %get-tuple-element.51.refs_7_.t_in, f32[24,384]{1,0:T(8,128)S(1)} %get-tuple-element.70.keep_ref, f32[32,384]{1,0:T(8,128)S(1)} %collective-permute-done.5.xr_ref, f32[96,256]{1,0:T(8,128)S(1)} %get-tuple-element.72.u_in), custom_call_target="tpu_custom_call" | custom-call | tf_op jit(solution)/shard_map/pallas_call | solution.py:40
  (6 shorter events, 0.0 us)
Async XLA Ops:
  0.6 1.2 %copy-start = (s32[8,24,384]{2,1,0:T(8,128)S(1)}, s32[8,24,384]{2,1,0:T(8,128)}, u32[]{:S(2)}) copy-start(s32[8,24,384]{2,1,0:T(8,128)} %id_ref.1) | copy-start | bytes 884740
  0.6 2.0 %copy-start.2 = (s32[6,4,256]{2,1,0:T(4,128)S(1)}, s32[6,4,256]{2,1,0:T(4,128)}, u32[]{:S(2)}) copy-start(s32[6,4,256]{2,1,0:T(4,128)} %mat_ref.1) | copy-start | bytes 73732
  0.7 2.0 %copy-start.1 = (f32[3,6,4,256]{3,2,1,0:T(4,128)S(1)}, f32[3,6,4,256]{3,2,1,0:T(4,128)}, u32[]{:S(2)}) copy-start(f32[3,6,4,256]{3,2,1,0:T(4,128)} %u_ref.1) | copy-start | bytes 221188
  1.8 1.1 %copy-start.3 = (f32[16]{0:T(128)S(1)}, f32[16]{0:T(128)}, u32[]{:S(2)}) copy-start(f32[16]{0:T(128)} %param.15) | copy-start | bytes 196
  1.8 1.1 %copy-start.4 = (f32[16]{0:T(128)S(1)}, f32[16]{0:T(128)}, u32[]{:S(2)}) copy-start(f32[16]{0:T(128)} %param.14) | copy-start | bytes 196
  1.8 1.1 %copy-start.5 = (f32[16]{0:T(128)S(1)}, f32[16]{0:T(128)}, u32[]{:S(2)}) copy-start(f32[16]{0:T(128)} %param.13) | copy-start | bytes 196
  2.1 1.7 %collective-permute-start.1 = (f32[576,128]{1,0:T(8,128)S(1)}, f32[576,128]{1,0:T(8,128)S(1)}, u32[]{:S(2)}, u32[]{:S(2)}) collective-permute-start(f32[576,128]{1,0:T(8,128)S(1)} %get-tuple-element.41), channel_id=1, source_target_pairs={{0,1},{1,0},{2,3},{3,2},{4,5},{5,4},{6,7},{7,6},{8,9},{9,8},{10,11... | collective-permute-start | bytes 884744 | tf_op jit(solution)/shard_map/ppermute | solution.py:908
  2.8 2.4 %collective-permute-start = (f32[824,128]{1,0:T(8,128)S(1)}, f32[824,128]{1,0:T(8,128)S(1)}, u32[]{:S(2)}, u32[]{:S(2)}) collective-permute-start(f32[824,128]{1,0:T(8,128)S(1)} %get-tuple-element.39), channel_id=1, source_target_pairs={{0,1},{1,0},{2,3},{3,2},{4,5},{5,4},{6,7},{7,6},{8,9},{9,8},{10,11... | collective-permute-start | bytes 1265672 | tf_op jit(solution)/shard_map/ppermute | solution.py:908
  4.5 8.2 %collective-permute-start.3 = (f32[120,768]{1,0:T(8,128)S(1)}, f32[120,768]{1,0:T(8,128)S(1)}, u32[]{:S(2)}, u32[]{:S(2)}) collective-permute-start(f32[120,768]{1,0:T(8,128)S(1)} %get-tuple-element.52), channel_id=1, source_target_pairs={{1,4},{3,6},{4,1},{5,8},{6,3},{7,10},{8,5},{9,12},{10,7},{11,14},{... | collective-permute-start | bytes 1105928 | tf_op jit(solution)/shard_map/ppermute | solution.py:908
  5.3 4.8 %collective-permute-start.2 = (f32[72,128]{1,0:T(8,128)S(1)}, f32[72,128]{1,0:T(8,128)S(1)}, u32[]{:S(2)}, u32[]{:S(2)}) collective-permute-start(f32[72,128]{1,0:T(8,128)S(1)} %get-tuple-element.50), channel_id=1, source_target_pairs={{0,2},{1,3},{2,0},{3,1},{4,6},{5,7},{6,4},{7,5},{8,10},{9,11},{10,... | collective-permute-start | bytes 110600 | tf_op jit(solution)/shard_map/ppermute | solution.py:908
  8.2 4.6 %collective-permute-start.4 = (f32[32,128]{1,0:T(8,128)S(1)}, f32[32,128]{1,0:T(8,128)S(1)}, u32[]{:S(2)}, u32[]{:S(2)}) collective-permute-start(f32[32,128]{1,0:T(8,128)S(1)} %get-tuple-element.53), channel_id=1, source_target_pairs={{1,6},{3,4},{4,3},{5,10},{6,1},{7,8},{8,7},{9,14},{10,5},{11,12},{... | collective-permute-start | bytes 49160 | tf_op jit(solution)/shard_map/ppermute | solution.py:908
  13.9 5.0 %collective-permute-start.5 = (f32[32,384]{1,0:T(8,128)S(1)}, f32[32,384]{1,0:T(8,128)S(1)}, u32[]{:S(2)}, u32[]{:S(2)}) collective-permute-start(f32[32,384]{1,0:T(8,128)S(1)} %get-tuple-element.71), channel_id=1, source_target_pairs={{0,1},{1,0},{2,3},{3,2},{4,5},{5,4},{6,7},{7,6},{8,9},{9,8},{10,11... | collective-permute-start | bytes 147464 | tf_op jit(solution)/shard_map/ppermute | solution.py:908
